TPU v7x, 512 devices: a whole 4x8x8 slice. The times are simulated.
512 devices in a mesh: row: 32 (over x_hi, y, core), col: 16 (over z, x_lo).
Axes of the slice: x: 4 (x_hi: 2, x_lo: 2; x = x_hi * 2 + x_lo), y: 8, z: 8, core: 2. Of those that a mesh axis runs over, the one named last changes fastest.
Arguments:
- front_rows: bfloat16 [512, 128, 512], P('row', 'col'), may hold values from -0.0546875 to 0.0546875
- slot_blocks: int32 [512], P('row'), may hold values from -1 to 95, as said below
- inv_factor: float32 [512, 512], replicated
- ancestor_inv: float32 [12288, 12288], P('row', 'col'), may hold values from -6 to 6
Outputs:
- offdiag_inv: float32 [12288, 512], P(('row', 'col'))
- diag_inv: float32 [512, 512], P('col')
Inputs may be any that keep to these rules, and one draw needn't show every extreme that they name: `slot_blocks`: each of the 96 blocks stands in exactly one slot and -1 marks an empty slot. Block b belongs to column panel b // 6; the 16 slots of one row index hold at most 1 block of one panel, and some row index holds exactly 1 block of every panel.
All inputs are finite; a program needn't handle non-finite values.
Results may differ from a plain program's by a relative error of at most 0.0041.
Values may be sent and summed in bfloat16 or wider, within the bound.
No kernel may reach another device: no remote copies, remote signals or barrier semaphores. Data moves between devices by JAX's collectives and lax.ppermute only.
A program may use at most 64 MiB of HBM per device.

v0:
```python
import jax
import jax.numpy as jnp
from jax import lax
from jax.sharding import PartitionSpec as P


def spread(block, axis, owner):
    block = jnp.where(lax.axis_index(axis) == owner, block, jnp.zeros_like(block))
    return lax.psum(block, axis)


def select_matrix(block_ids, panels, panel_blocks, cand_count):
    panel_of = jnp.where(block_ids >= 0, block_ids // panel_blocks, -1)
    member = panel_of[None, :] == panels[:, None]
    ranking = jnp.cumsum(member.astype(jnp.int32), axis=1) - 1
    levels = jnp.arange(cand_count, dtype=jnp.int32)
    return member[:, None, :] & (ranking[:, None, :] == levels[None, :, None])


def body(front_rows, slot_blocks, inv_factor, ancestor_inv):
    col_count = lax.axis_size("col")
    row_count = lax.axis_size("row")
    col_index = lax.axis_index("col")
    row_index = lax.axis_index("row")
    slot_count = front_rows.shape[0]
    block_height = front_rows.shape[1] * col_count
    panel_width = front_rows.shape[2]
    tile_rows, panel_rows = ancestor_inv.shape
    panel_blocks = panel_rows // block_height
    cand_count = slot_count // col_count
    own_panel = jnp.reshape(col_index, (1,))
    own_choice = select_matrix(slot_blocks, own_panel, panel_blocks, cand_count)[0]
    cand_ids = jnp.sum(jnp.where(own_choice, slot_blocks[None, :] + 1, 0), axis=1) - 1
    gathered = lax.all_gather(front_rows, "col", axis=1, tiled=True)
    picked = jnp.einsum(
        "ks,sbw->kbw", own_choice.astype(jnp.bfloat16), gathered, preferred_element_type=jnp.float32
    ).astype(jnp.bfloat16)
    scaled = jnp.einsum(
        "kbw,wv->kbv",
        picked.astype(jnp.float32),
        inv_factor,
        precision=lax.Precision.HIGHEST,
        preferred_element_type=jnp.float32,
    ).astype(jnp.bfloat16)

    def absorb(totals, one_block, offset, is_valid):
        partial_sum, assembled = totals
        clipped = jnp.clip(offset, 0, panel_blocks - 1) * block_height
        columns = lax.dynamic_slice_in_dim(ancestor_inv, clipped, block_height, 1)
        update = jnp.dot(
            columns,
            one_block.astype(jnp.float32),
            precision=lax.Precision.HIGHEST,
            preferred_element_type=jnp.float32,
        )
        partial_sum = partial_sum + jnp.where(is_valid, update, 0.0)
        current = lax.dynamic_slice_in_dim(assembled, clipped, block_height, 0)
        assembled = lax.dynamic_update_slice_in_dim(
            assembled, jnp.where(is_valid, one_block, current), clipped, 0
        )
        return (partial_sum, assembled)

    initial = (
        jnp.zeros((tile_rows, panel_width), jnp.float32),
        jnp.zeros((panel_rows, panel_width), jnp.bfloat16),
    )
    blocks = lax.all_gather(scaled, "row", axis=0, tiled=True)
    block_ids = lax.all_gather(cand_ids, "row", axis=0, tiled=True)

    def take_member(member_index, running):
        number = block_ids[member_index]
        offset = number - col_index * panel_blocks
        is_valid = (number >= 0) & (offset >= 0) & (offset < panel_blocks)
        one_block = lax.dynamic_index_in_dim(blocks, member_index, 0, keepdims=False)
        return absorb(running, one_block, offset, is_valid)

    partial_sum, assembled = lax.fori_loop(0, blocks.shape[0], take_member, initial)
    root_col = row_index * col_count // row_count
    panel_start = row_index * tile_rows - root_col * panel_rows
    own_rows = lax.dynamic_slice_in_dim(assembled, panel_start, tile_rows, 0)
    row_factor = spread(own_rows, "col", root_col)
    column_total = lax.psum_scatter(partial_sum, "col", scatter_dimension=0, tiled=True)
    share_rows = tile_rows // col_count
    own_factor = lax.dynamic_slice_in_dim(row_factor, col_index * share_rows, share_rows, 0)
    gram_part = jnp.einsum(
        "pi,pj->ij",
        own_factor.astype(jnp.float32),
        column_total,
        precision=lax.Precision.HIGHEST,
        preferred_element_type=jnp.float32,
    )
    diag_width = panel_width // col_count
    gram_piece = lax.psum_scatter(gram_part, "col", scatter_dimension=0, tiled=True)
    gram_block = lax.psum(gram_piece, "row")
    factor_cols = lax.dynamic_slice_in_dim(inv_factor, col_index * diag_width, diag_width, 1)
    factor_gram = jnp.einsum(
        "pi,pj->ij",
        factor_cols,
        inv_factor,
        precision=lax.Precision.HIGHEST,
        preferred_element_type=jnp.float32,
    )
    diag_rows = factor_gram + gram_block
    return (-column_total, diag_rows)


def solution(mesh):
    in_specs = (P("row", "col", None), P("row"), P(), P("row", "col"))
    out_specs = (P(("row", "col"), None), P("col", None))
    return jax.shard_map(body, mesh=mesh, in_specs=in_specs, out_specs=out_specs, check_vma=False)
```

profile of v0, /device:TPU:1, one launch (start us, length us, event | category | flops | bytes accessed | tf_op | source)
XLA Modules:
  0.0 867.8 jit_solution(10194297184229428001)
XLA Ops:
  8.9 73.3 %all-gather.4.cloned.1.call-done = bf16[16,128,512]{2,1,0:T(8,128)(2,1)} async-done(((bf16[16,8,512]{2,1,0:T(8,128)(2,1)}), bf16[16,128,512]{2,1,0:T(8,128)(2,1)}) %all-gather.4.cloned.1.call-update) | async-done | bytes 2097168 | tf_op jit(solution)/shard_map/all_gather | solution.py:34
  82.2 2.9 fusion.6
  89.6 24.2 %all-reduce = s32[32]{0:T(128)S(1)} all-reduce(s32[32]{0:T(128)S(1)} %dynamic-update-slice), channel_id=1, replica_groups=mesh['row'=32,'col'=16] {'row'}, use_global_device_ids=true, to_apply=%add | all-reduce | flops 32 | bytes 256
  113.9 72.6 %all-gather.6.cloned.1.call-done = bf16[4096,512]{1,0:T(8,128)(2,1)} async-done(((bf16[128,512]{1,0:T(8,128)(2,1)}), bf16[4096,512]{1,0:T(8,128)(2,1)}) %all-gather.6.cloned.1.call-update) | async-done | bytes 4194320 | tf_op jit(solution)/shard_map/all_gather | solution.py:67
  186.5 141.6 %while.18 = (s32[]{:T(128)}, f32[384,512]{1,0:T(8,128)S(1)}, bf16[768,512]{1,0:T(8,128)(2,1)S(1)}, s32[32]{0:T(128)S(1)}, s32[]{:T(128)}, /*index=5*/f32[384,768...) while((s32[]{:T(128)}, f32[384,512]{1,0:T(8,128)S(1)}, ...), condition=%wide.region_3.4_spmd.clone, body=%wide.region_2.3_spmd.clone.sunk | while | flops 302645248 | bytes 2294048 | solution.py:77
  188.4 1.6 fusion.25
  192.9 1.6 fusion.25
  201.7 1.6 fusion.25
  210.6 1.6 fusion.25
  223.8 1.6 fusion.25
  232.7 1.6 fusion.25
  246.0 1.6 fusion.25
  254.8 1.6 fusion.25
  268.1 1.6 fusion.25
  276.9 1.6 fusion.25
  290.2 1.6 fusion.25
  299.1 1.6 fusion.25
  321.2 1.6 fusion.25
  329.7 129.2 %all-reduce.4.cloned.1.call-done = bf16[384,512]{1,0:T(8,128)(2,1)} async-done(((bf16[384,512]{1,0:T(8,128)(2,1)}), bf16[384,512]{1,0:T(8,128)(2,1)}) %all-reduce.4.cloned.1.call-update) | async-done | bytes 393232 | tf_op jit(solution)/shard_map/psum | solution.py:9
  458.9 74.9 %reduce-scatter.3.cloned.1.call-done = f32[24,512]{1,0:T(8,128)} async-done(((f32[384,512]{1,0:T(8,128)}), f32[24,512]{1,0:T(8,128)}) %reduce-scatter.3.cloned.1.call-update) | async-done | bytes 49168 | tf_op jit(solution)/shard_map/reduce_scatter | solution.py:82
  533.9 2.5 fusion.9
  536.4 73.1 %reduce-scatter.5.cloned.1.call-done = f32[32,512]{1,0:T(8,128)} async-done(((f32[512,512]{1,0:T(8,128)}), f32[32,512]{1,0:T(8,128)}) %reduce-scatter.5.cloned.1.call-update) | async-done | bytes 65552 | tf_op jit(solution)/shard_map/reduce_scatter | solution.py:93
  610.1 248.6 %all-reduce.6.cloned.1.call-done = f32[32,512]{1,0:T(8,128)} async-done(((f32[32,512]{1,0:T(8,128)}), f32[32,512]{1,0:T(8,128)}) %all-reduce.6.cloned.1.call-update) | async-done | bytes 65552 | tf_op jit(solution)/shard_map/psum | solution.py:94
  858.7 2.2 convolution_add_fusion
  (116 shorter events, 86.3 us)
Async XLA Ops:
  7.2 78.0 %copy-start = (f32[512,512]{1,0:T(8,128)S(1)}, f32[512,512]{1,0:T(8,128)}, u32[]{:S(2)}) copy-start(f32[512,512]{1,0:T(8,128)} %param.8) | copy-start | bytes 3145732
  7.2 79.2 %copy-start.3 = (s32[16]{0:T(128)S(1)}, s32[16]{0:T(128)}, u32[]{:S(2)}) copy-start(s32[16]{0:T(128)} %param.7) | copy-start | bytes 196
  7.2 75.0 %all-gather.4.cloned.1.call-start = ((), (), s32[]{:S(2)}) async-start(), calls=%async_computation.2 | async-start | bytes 2228224 | tf_op jit(solution)/shard_map/all_gather | solution.py:34
  7.9 178.5 %all-gather.6.cloned.1.call-start = ((), (), s32[]{:S(2)}) async-start(), calls=%async_computation.7 | async-start | bytes 4325376 | tf_op jit(solution)/shard_map/all_gather | solution.py:67
  86.3 372.6 %all-reduce.4.cloned.1.call-start = ((), (), s32[]{:S(2)}) async-start(), calls=%async_computation.4 | async-start | bytes 786432 | tf_op jit(solution)/shard_map/psum | solution.py:9
  328.2 1.0 copy-start.1
  329.1 204.8 %reduce-scatter.3.cloned.1.call-start = ((), (), s32[]{:S(2)}) async-start(), calls=%async_computation.3 | async-start | bytes 835584 | tf_op jit(solution)/shard_map/reduce_scatter | solution.py:82
  329.7 279.8 %reduce-scatter.5.cloned.1.call-start = ((), (), s32[]{:S(2)}) async-start(), calls=%async_computation.5 | async-start | bytes 1114112 | tf_op jit(solution)/shard_map/reduce_scatter | solution.py:93
  533.9 75.6 %copy-start.2 = (f32[24,512]{1,0:T(8,128)S(1)}, f32[24,512]{1,0:T(8,128)}, u32[]{:S(2)}) copy-start(f32[24,512]{1,0:T(8,128)} %reduce-scatter.3.cloned.1.call-done) | copy-start | bytes 147460
  536.4 322.4 %all-reduce.6.cloned.1.call-start = ((), (), s32[]{:S(2)}) async-start(), calls=%async_computation.6 | async-start | bytes 131072 | tf_op jit(solution)/shard_map/psum | solution.py:94
Sparse Core Ops, SparseCore 0:
  10.1 72.0 all-gather.3
  86.4 99.9 all-gather.5
  329.2 129.6 all-reduce.3
  461.8 71.9 reduce-scatter.2
  536.5 72.9 reduce-scatter.4
  612.5 246.1 all-reduce.5
where the time goes:
time: 871 us; the launch traced here: 868 us
  waiting for transfers between devices  673 us (77%)
  matrix products  58.3 us (7%)
  loops' own time  42.9 us (5%)
  other arithmetic  33.2 us (4%)
  blocking collectives  24.2 us (3%)
  local copies, waits for them, and re-layouts  21 us (2%)
  between operations  14.9 us (2%)
    psum x1, waiting for transfers between devices, body(): gram_block = lax.psum(gram_piece, 'row')  249 us
    psum x1, waiting for transfers between devices, spread(): return lax.psum(block, axis)  129 us
    reduce_scatter x1, waiting for transfers between devices, body(): lax.psum_scatter(partial_sum, 'col', scatter_dimension=0, tiled=True)  74.9 us
    all_gather x1, waiting for transfers between devices, body(): gathered = lax.all_gather(front_rows, 'col', axis=1, tiled=True)  73.3 us
    reduce_scatter x1, waiting for transfers between devices, body(): lax.psum_scatter(gram_part, 'col', scatter_dimension=0, tiled=True)  73.1 us
    all_gather x1, waiting for transfers between devices, body(): blocks = lax.all_gather(scaled, 'row', axis=0, tiled=True)  72.6 us
    dot_general x32, matrix products, absorb(): jnp.dot(columns, one_block.astype(jnp.float32), precision=lax.Precision.H...  49.6 us
    another operation x1, loops' own time, body(): lax.fori_loop(0, blocks.shape[0], take_member, initial)  42.9 us
  transfers between devices with their start and end apart: 6, of which 6 were waited for; matrix products, arithmetic and copies ran while one was open for 0% of the time, Pallas kernels for 0%

commit v1 on v0

v1 whole, which is shorter than its diff:
```python
import jax
import jax.numpy as jnp
from jax import lax
from jax.sharding import PartitionSpec as P

BF16 = jnp.bfloat16
F32 = jnp.float32


def body(front_rows, slot_blocks, inv_factor, ancestor_inv):
    col_count = lax.axis_size("col")
    row_count = lax.axis_size("row")
    chip_count = row_count // 2
    col_index = lax.axis_index("col")
    row_index = lax.axis_index("row")
    core = row_index % 2
    slot_count, chunk_rows, width = front_rows.shape
    half = width // 2
    tile_rows, panel_rows = ancestor_inv.shape
    block_rows = chunk_rows * col_count
    panel_blocks = panel_rows // block_rows
    same_core = [[2 * j + k for j in range(chip_count)] for k in range(2)]
    core_pairs = [[2 * j, 2 * j + 1] for j in range(chip_count)]
    core_swap = [(i, i ^ 1) for i in range(row_count)]

    scaled = jnp.dot(
        front_rows.reshape(slot_count * chunk_rows, width).astype(F32),
        inv_factor,
        precision=lax.Precision.HIGHEST,
        preferred_element_type=F32,
    ).astype(BF16)
    slot_panel = jnp.where(slot_blocks >= 0, slot_blocks // panel_blocks, -1)
    panels = jnp.arange(col_count, dtype=jnp.int32)
    chosen = slot_panel[None, :] == panels[:, None]
    by_panel = jnp.einsum(
        "ps,sbw->pbw",
        chosen.astype(BF16),
        scaled.reshape(slot_count, chunk_rows, width),
        preferred_element_type=F32,
    ).astype(BF16)
    mine = slot_panel == col_index
    offset = jnp.sum(jnp.where(mine, slot_blocks % panel_blocks + 1, 0)) - 1

    block = lax.all_to_all(by_panel, "col", 0, 0, tiled=True)
    dealt = block.reshape(chip_count, chunk_rows, 2, half).transpose(0, 2, 1, 3)
    dealt = dealt.reshape(row_count, chunk_rows, half)
    tag = jnp.full((row_count, chunk_rows, 128), offset.astype(BF16), BF16)
    taken = lax.all_to_all(jnp.concatenate([dealt, tag], 2), "row", 0, 0, tiled=True)
    numbers = taken[:, 0, half].astype(F32)
    place = numbers[None, :] == jnp.arange(panel_blocks, dtype=F32)[:, None]
    piece = jnp.einsum(
        "os,sbw->obw", place.astype(BF16), taken[:, :, :half], preferred_element_type=F32
    ).astype(BF16)

    copies = jnp.broadcast_to(piece[None], (chip_count, *piece.shape))
    parts = lax.all_to_all(copies, "row", 0, 0, tiled=True, axis_index_groups=same_core)
    own_half = parts.transpose(1, 0, 2, 3).reshape(panel_rows, half)
    other_half = lax.ppermute(own_half, "row", core_swap)

    tile = ancestor_inv.astype(BF16)
    own_sum = jnp.dot(tile, own_half, preferred_element_type=F32)
    other_sum = jnp.dot(tile, other_half, preferred_element_type=F32)

    def both(own, other):
        return jnp.where(
            core == 0, jnp.concatenate([own, other], 1), jnp.concatenate([other, own], 1)
        )

    share = tile_rows // col_count
    start = row_index * share
    share_rows = both(
        lax.dynamic_slice_in_dim(own_half, start, share, 0),
        lax.dynamic_slice_in_dim(other_half, start, share, 0),
    )
    route = [
        (r * col_count + p, (2 * p + r // col_count) * col_count + r % col_count)
        for r in range(row_count)
        for p in range(col_count)
    ]
    own_factor = lax.ppermute(share_rows, ("row", "col"), route)

    partial_sums = both(own_sum, other_sum).astype(BF16).reshape(col_count, share, width)
    arrived = lax.all_to_all(partial_sums, "col", 0, 0, tiled=True)
    column_total = jnp.sum(arrived.astype(F32), axis=0)

    pair_total = lax.all_gather(column_total, "row", axis=0, tiled=True, axis_index_groups=core_pairs)
    pair_factor = lax.all_gather(own_factor, "row", axis=0, tiled=True, axis_index_groups=core_pairs)
    gram_part = lax.dot_general(
        pair_factor,
        pair_total.astype(BF16),
        (((0,), (0,)), ((), ())),
        preferred_element_type=F32,
    )
    diag_width = width // col_count
    gram_half = lax.dynamic_index_in_dim(
        gram_part.reshape(col_count, 2, diag_width // 2, width), core, 1, keepdims=False
    ).astype(BF16)
    gram_piece = jnp.sum(lax.all_to_all(gram_half, "col", 0, 0, tiled=True).astype(F32), axis=0)
    copies = jnp.broadcast_to(gram_piece.astype(BF16)[None], (chip_count, *gram_piece.shape))
    pieces = lax.all_to_all(copies, "row", 0, 0, tiled=True, axis_index_groups=same_core)
    gram_rows = jnp.sum(pieces.astype(F32), axis=0)
    gram_block = lax.all_gather(gram_rows, "row", axis=0, tiled=True, axis_index_groups=core_pairs)
    factor_cols = lax.dynamic_slice_in_dim(inv_factor, col_index * diag_width, diag_width, 1)
    factor_gram = lax.dot_general(
        factor_cols,
        inv_factor,
        (((0,), (0,)), ((), ())),
        precision=lax.Precision.HIGHEST,
        preferred_element_type=F32,
    )
    return (-column_total, factor_gram + gram_block)


def solution(mesh):
    in_specs = (P("row", "col", None), P("row"), P(), P("row", "col"))
    out_specs = (P(("row", "col"), None), P("col", None))
    return jax.shard_map(body, mesh=mesh, in_specs=in_specs, out_specs=out_specs, check_vma=False)
```

time: 871 us -> 134 us (0.15)
  waiting for transfers between devices: 673 us -> 25.9 us
  matrix products: 58.3 us -> 4.21 us
  blocking collectives: 24.2 us -> 69.4 us
  loops' own time: 42.9 us -> 0 us
  other arithmetic: 33.2 us -> 3.34 us
  starting transfers between devices: 0.24 us -> 27.4 us
  local copies, waits for them, and re-layouts: 21 us -> 1.89 us
  between operations: 14.9 us -> 1.51 us
    psum x2 -> x0, waiting for transfers between devices: 378 us -> none  [the longest x1 249 us: body(): gram_block = lax.psum(gram_piece, 'row')]
    reduce_scatter x2 -> x0, waiting for transfers between devices: 148 us -> none  [the longest x1 74.9 us: body(): lax.psum_scatter(partial_sum, 'col', scatter_dimension=0, tiled=True)]
    all_gather x2 -> x0, waiting for transfers between devices: 146 us -> none  [the longest x1 73.3 us: body(): gathered = lax.all_gather(front_rows, 'col', axis=1, tiled=True)]
    all_to_all x0 -> x3, blocking collectives: none -> 58.6 us  [the longest x1 23 us: body(): lax.all_to_all(jnp.concatenate([dealt, tag], 2), 'row', 0, 0, tiled=True)]
    dot_general x36 -> x7, matrix products: 58.3 us -> 4.21 us  [the longest x1 1.4 us: body(): jnp.dot(front_rows.reshape(slot_count * chunk_rows, width).astype(F32), i...]
    another operation x1 -> x0, loops' own time: 42.9 us -> none  [body(): lax.fori_loop(0, blocks.shape[0], take_member, initial)]
    dynamic_update_slice x32 -> x0, other arithmetic: 30.2 us -> none  [absorb(): lax.dynamic_update_slice_in_dim(assembled, jnp.where(is_valid, one_block,...]
    unnamed x1 -> x0, blocking collectives: 24.2 us -> none
  transfers between devices with their start and end apart: 6 -> 5, of which waited for: 6 -> 5; matrix products, arithmetic and copies ran while one was open for 0% -> 0% of each run, Pallas kernels for 0% -> 0%
where the time goes in v1:
time: 134 us
  blocking collectives  69.4 us (52%)
  starting transfers between devices  27.4 us (20%)
  waiting for transfers between devices  25.9 us (19%)
  matrix products  4.21 us (3%)
  other arithmetic  3.34 us (2%)
  local copies, waits for them, and re-layouts  1.89 us (1%)
  between operations  1.51 us (1%)
    all_to_all x1, blocking collectives, body(): lax.all_to_all(jnp.concatenate([dealt, tag], 2), 'row', 0, 0, tiled=True)  23 us
    all_to_all x1, blocking collectives, body(): lax.all_to_all(gram_half, 'col', 0, 0, tiled=True).astype(F32)  20.1 us
    all_to_all x1, blocking collectives, body(): lax.all_to_all(copies, 'row', 0, 0, tiled=True, axis_index_groups=same_core)  15.4 us
    all_to_all x1, starting transfers between devices, body(): block = lax.all_to_all(by_panel, 'col', 0, 0, tiled=True)  11.9 us
    all_to_all x1, waiting for transfers between devices, body(): lax.all_to_all(copies, 'row', 0, 0, tiled=True, axis_index_groups=same_core)  9.23 us
    all_to_all x1, waiting for transfers between devices, body(): block = lax.all_to_all(by_panel, 'col', 0, 0, tiled=True)  7.82 us
    all_gather x1, blocking collectives, body(): lax.all_gather(gram_rows, 'row', axis=0, tiled=True, axis_index_groups=co...  5.08 us
    all_to_all x1, waiting for transfers between devices, body(): arrived = lax.all_to_all(partial_sums, 'col', 0, 0, tiled=True)  4.78 us
  transfers between devices with their start and end apart: 5, of which 5 were waited for; matrix products, arithmetic and copies ran while one was open for 0% of the time, Pallas kernels for 0%

profile of v1, /device:TPU:1, one launch (start us, length us, event | category | flops | bytes accessed | tf_op | source)
XLA Modules:
  0.0 133.6 jit_solution(8898353291982399446)
XLA Ops:
  0.6 1.4 %fusion.19 = (s32[]{:T(128)}, s32[16]{0:T(128)S(1)}) fusion(s32[16]{0:T(128)} %param.5, s32[]{:T(128)S(6)} %axis_index.25), kind=kLoop, calls=%fused_computation.38 | loop fusion | flops 287 | bytes 136 | tf_op jit(solution)/shard_map/reduce_sum | solution.py:42
  2.0 1.4 %fusion = bf16[16,8,512]{2,1,0:T(8,128)(2,1)S(1)} fusion(f32[512,512]{1,0:T(8,128)S(1)} %copy-done, bf16[16,8,512]{2,1,0:T(8,128)(2,1)} %param.4), kind=kOutput, calls=%fused_computation.4 | convolution fusion | flops 402718720 | bytes 1310720 | tf_op jit(solution)/shard_map/dot_general | solution.py:26
  3.6 0.7 copy.22
  4.3 11.9 %all-to-all-start = ((bf16[16,8,512]{2,1,0:T(8,128)(2,1)}), bf16[16,8,512]{2,1,0:T(8,128)(2,1)S(1)}, u32[]{:S(2)}, u32[]{:S(2)}) async-start(bf16[16,8,512]{2,1,0:T(8,128)(2,1)} %copy.22), calls=%async_computation | async-start | bytes 262144 | tf_op jit(solution)/shard_map/all_to_all | solution.py:44
  16.9 7.8 %all-to-all-done = bf16[16,8,512]{2,1,0:T(8,128)(2,1)S(1)} async-done(((bf16[16,8,512]{2,1,0:T(8,128)(2,1)}), bf16[16,8,512]{2,1,0:T(8,128)(2,1)S(1)}, u32[]{:S(2)}, u32[]{:S(2)}) %all-to-all-start) | async-done | bytes 131104 | tf_op jit(solution)/shard_map/all_to_all | solution.py:44
  24.8 23.0 %all_to_all.30 = bf16[32,8,384]{2,1,0:T(8,128)(2,1)S(1)} all-to-all(bf16[32,8,384]{2,1,0:T(8,128)(2,1)S(1)} %concatenate.25), channel_id=1, replica_groups=mesh['row'=32,'col'=16] {'row'}, dimensions={0} | all-to-all | bytes 393216 | tf_op jit(solution)/shard_map/all_to_all | solution.py:48
  48.3 15.4 %all_to_all.31 = bf16[16,6,8,256]{3,2,1,0:T(8,128)(2,1)S(1)} all-to-all(bf16[16,6,8,256]{3,2,1,0:T(8,128)(2,1)S(1)} %broadcast_in_dim.7), channel_id=1, replica_groups={{0,32,64,96,128,160,192,224,256,288,320,352,384,416,448,480},{16,48,80,..., dimensions={0} | all-to-all | bytes 786432 | tf_op jit(solution)/shard_map/all_to_all | solution.py:56
  63.8 4.7 %collective-permute-start = (bf16[768,256]{1,0:T(8,128)(2,1)S(1)}, bf16[768,256]{1,0:T(8,128)(2,1)S(1)}, u32[]{:S(2)}, u32[]{:S(2)}) collective-permute-start(bf16[768,256]{1,0:T(8,128)(2,1)S(1)} %bitcast.30), channel_id=1, source_target_pairs={{0,16},{16,0},{32,48},{48,32},{64,80},{80,64},{96,112},{112,96},{1... | collective-permute-start | bytes 1179656 | tf_op jit(solution)/shard_map/ppermute | solution.py:58
  68.5 0.4 convolution_bitcast_fusion.1
  69.1 0.7 collective-permute-done
  70.4 0.8 fusion.1
  71.3 3.6 %all-to-all-start.3 = ((bf16[16,24,512]{2,1,0:T(8,128)(2,1)}), bf16[16,24,512]{2,1,0:T(8,128)(2,1)S(1)}, u32[]{:S(2)}, u32[]{:S(2)}) async-start(bf16[16,24,512]{2,1,0:T(8,128)(2,1)} %fusion.1), calls=%async_computation.3 | async-start | bytes 786432 | tf_op jit(solution)/shard_map/all_to_all | solution.py:83
  74.9 3.7 %collective-permute-start.1 = (bf16[24,512]{1,0:T(8,128)(2,1)S(1)}, bf16[24,512]{1,0:T(8,128)(2,1)S(1)}, u32[]{:S(2)}, u32[]{:S(2)}) collective-permute-start(bf16[24,512]{1,0:T(8,128)(2,1)S(1)} %maximum_select_fusion.1), channel_id=1, source_target_pairs={{0,0},{1,32},{2,64},{3,96},{4,128},{5,160},{6,192},{7,224},{8,256}... | collective-permute-start | bytes 73736 | tf_op jit(solution)/shard_map/ppermute | solution.py:80
  78.6 3.3 %collective-permute-done.1 = bf16[24,512]{1,0:T(8,128)(2,1)S(1)} collective-permute-done((bf16[24,512]{1,0:T(8,128)(2,1)S(1)}, bf16[24,512]{1,0:T(8,128)(2,1)S(1)}, u32[]{:S(2)}, u32[]{:S(2)}) %collective-permute-start.1) | collective-permute-done | bytes 24608 | tf_op jit(solution)/shard_map/ppermute | solution.py:80
  81.9 1.8 %all_gather.9 = bf16[48,512]{1,0:T(8,128)(2,1)S(1)} all-gather(bf16[24,512]{1,0:T(8,128)(2,1)S(1)} %collective-permute-done.1), channel_id=1, replica_groups={{0,16},{32,48},{64,80},{96,112},{128,144},{160,176},{192,208},{224,240}..., dimensions={0}, use_global_device_ids=true | all-gather | bytes 73728 | tf_op jit(solution)/shard_map/all_gather | solution.py:87
  83.7 4.8 %all-to-all-done.3 = bf16[16,24,512]{2,1,0:T(8,128)(2,1)S(1)} async-done(((bf16[16,24,512]{2,1,0:T(8,128)(2,1)}), bf16[16,24,512]{2,1,0:T(8,128)(2,1)S(1)}, u32[]{:S(2)}, u32[]{:S(2)}) %all-to-all-start.3) | async-done | bytes 393248 | tf_op jit(solution)/shard_map/all_to_all | solution.py:83
  88.6 0.6 fusion.22
  89.2 3.9 %all_gather.10 = bf16[48,512]{1,0:T(8,128)(2,1)S(1)} all-gather(bf16[24,512]{1,0:T(8,128)(2,1)S(1)} %get-tuple-element.6), channel_id=1, replica_groups={{0,16},{32,48},{64,80},{96,112},{128,144},{160,176},{192,208},{224,240}..., dimensions={0}, use_global_device_ids=true | all-gather | bytes 73728 | tf_op jit(solution)/shard_map/all_gather | solution.py:86
  93.5 20.1 %all_to_all.32 = bf16[16,16,512]{2,1,0:T(8,128)(2,1)S(1)} all-to-all(bf16[16,16,512]{2,1,0:T(8,128)(2,1)S(1)} %fusion.4), channel_id=1, replica_groups=mesh['row'=32,'col'=16] {'col'}, dimensions={0} | all-to-all | bytes 524288 | tf_op jit(solution)/shard_map/all_to_all | solution.py:98
  113.6 0.7 broadcast_in_dim.8
  114.3 3.5 %all-to-all-start.5 = ((bf16[16,16,512]{2,1,0:T(8,128)(2,1)}), bf16[16,16,512]{2,1,0:T(8,128)(2,1)S(1)}, u32[]{:S(2)}, u32[]{:S(2)}) async-start(bf16[16,16,512]{2,1,0:T(8,128)(2,1)} %broadcast_in_dim.8), calls=%async_computation.5 | async-start | bytes 524288 | tf_op jit(solution)/shard_map/all_to_all | solution.py:100
  117.9 9.2 %all-to-all-done.5 = bf16[16,16,512]{2,1,0:T(8,128)(2,1)S(1)} async-done(((bf16[16,16,512]{2,1,0:T(8,128)(2,1)}), bf16[16,16,512]{2,1,0:T(8,128)(2,1)S(1)}, u32[]{:S(2)}, u32[]{:S(2)}) %all-to-all-start.5) | async-done | bytes 262176 | tf_op jit(solution)/shard_map/all_to_all | solution.py:100
  127.1 5.1 %all_gather.11 = f32[32,512]{1,0:T(8,128)S(1)} all-gather(f32[16,512]{1,0:T(8,128)S(1)} %convert_reduce_fusion.1), channel_id=1, replica_groups={{0,16},{32,48},{64,80},{96,112},{128,144},{160,176},{192,208},{224,240}..., dimensions={0}, use_global_device_ids=true | all-gather | bytes 98304 | tf_op jit(solution)/shard_map/all_gather | solution.py:102
  132.2 1.4 %convolution_add_fusion = f32[32,512]{1,0:T(8,128)} fusion(f32[32,512]{1,0:T(8,128)S(1)} %all_gather.11, f32[512,512]{1,0:T(8,128)S(1)} %copy-done, s32[]{:T(128)S(6)} %select_n.60), kind=kOutput, calls=%fused_computation.5 | convolution fusion | flops 100679680 | bytes 1441796 | tf_op jit(solution)/shard_map/dot_general | solution.py:104
  (25 shorter events, 2.0 us)
Async XLA Ops:
  0.6 1.4 %copy-start = (f32[512,512]{1,0:T(8,128)S(1)}, f32[512,512]{1,0:T(8,128)}, u32[]{:S(2)}) copy-start(f32[512,512]{1,0:T(8,128)} %param.6) | copy-start | bytes 3145732
  4.3 20.4 %all-to-all-start = ((bf16[16,8,512]{2,1,0:T(8,128)(2,1)}), bf16[16,8,512]{2,1,0:T(8,128)(2,1)S(1)}, u32[]{:S(2)}, u32[]{:S(2)}) async-start(bf16[16,8,512]{2,1,0:T(8,128)(2,1)} %copy.22), calls=%async_computation | async-start | bytes 262144 | tf_op jit(solution)/shard_map/all_to_all | solution.py:44
  48.1 20.4 %copy-start.1 = (f32[384,768]{1,0:T(8,128)S(1)}, f32[384,768]{1,0:T(8,128)}, u32[]{:S(2)}) copy-start(f32[384,768]{1,0:T(8,128)} %param.7) | copy-start | bytes 3538948
  63.8 6.0 %collective-permute-start = (bf16[768,256]{1,0:T(8,128)(2,1)S(1)}, bf16[768,256]{1,0:T(8,128)(2,1)S(1)}, u32[]{:S(2)}, u32[]{:S(2)}) collective-permute-start(bf16[768,256]{1,0:T(8,128)(2,1)S(1)} %bitcast.30), channel_id=1, source_target_pairs={{0,16},{16,0},{32,48},{48,32},{64,80},{80,64},{96,112},{112,96},{1... | collective-permute-start | bytes 1179656 | tf_op jit(solution)/shard_map/ppermute | solution.py:58
  71.3 17.3 %all-to-all-start.3 = ((bf16[16,24,512]{2,1,0:T(8,128)(2,1)}), bf16[16,24,512]{2,1,0:T(8,128)(2,1)S(1)}, u32[]{:S(2)}, u32[]{:S(2)}) async-start(bf16[16,24,512]{2,1,0:T(8,128)(2,1)} %fusion.1), calls=%async_computation.3 | async-start | bytes 786432 | tf_op jit(solution)/shard_map/all_to_all | solution.py:83
  74.9 7.0 %collective-permute-start.1 = (bf16[24,512]{1,0:T(8,128)(2,1)S(1)}, bf16[24,512]{1,0:T(8,128)(2,1)S(1)}, u32[]{:S(2)}, u32[]{:S(2)}) collective-permute-start(bf16[24,512]{1,0:T(8,128)(2,1)S(1)} %maximum_select_fusion.1), channel_id=1, source_target_pairs={{0,0},{1,32},{2,64},{3,96},{4,128},{5,160},{6,192},{7,224},{8,256}... | collective-permute-start | bytes 73736 | tf_op jit(solution)/shard_map/ppermute | solution.py:80
  114.3 12.8 %all-to-all-start.5 = ((bf16[16,16,512]{2,1,0:T(8,128)(2,1)}), bf16[16,16,512]{2,1,0:T(8,128)(2,1)S(1)}, u32[]{:S(2)}, u32[]{:S(2)}) async-start(bf16[16,16,512]{2,1,0:T(8,128)(2,1)} %broadcast_in_dim.8), calls=%async_computation.5 | async-start | bytes 524288 | tf_op jit(solution)/shard_map/all_to_all | solution.py:100

commit v2 on v1

v2 whole, which is shorter than its diff:
```python
import jax
import jax.numpy as jnp
from jax import lax
from jax.experimental import pallas as pl
from jax.experimental.pallas import tpu as pltpu
from jax.sharding import PartitionSpec as P

BF16 = jnp.bfloat16
F32 = jnp.float32
TAG = 128
SMEM = pl.BlockSpec(memory_space=pltpu.SMEM)
VMEM = pl.BlockSpec(memory_space=pltpu.VMEM)
PARAMS = pltpu.CompilerParams(vmem_limit_bytes=16 * 2**20)


def dot(a, b, dims=((1,), (0,))):
    return lax.dot_general(a, b, (dims, ((), ())), preferred_element_type=F32)


def split(x):
    high = x.astype(BF16)
    return high, (x - high.astype(F32)).astype(BF16)


def by_core(shape, natural, group):
    column = lax.broadcasted_iota(jnp.int32, shape, natural)
    place = lax.broadcasted_iota(jnp.int32, shape, 1 - natural)
    part = group // 2
    core = (column % group) // part
    target = core * (shape[natural] // 2) + (column // group) * part + column % part
    return jnp.where(target == place, 1.0, 0.0).astype(BF16)


def scale_kernel(panel_blocks, group, slots_ref, rows_ref, factor_ref, out_ref, scaled_ref):
    width = factor_ref.shape[1]
    high, low = split(factor_ref[...])
    rows = rows_ref[...]
    scaled = (dot(rows, high) + dot(rows, low)).astype(BF16)
    scaled_ref[...] = dot(scaled, by_core((width, width), 0, group))
    out_ref[...] = jnp.zeros_like(out_ref)
    slot_count = slots_ref.shape[0]
    height = rows_ref.shape[0] // slot_count
    for s in range(slot_count):
        block = slots_ref[s]

        @pl.when(block >= 0)
        def _():
            panel = block // panel_blocks
            number = (block - panel * panel_blocks + 1).astype(F32)
            out_ref[panel, :, :width] = scaled_ref[s * height : (s + 1) * height, :].astype(BF16)
            out_ref[panel, :, width:] = jnp.full((height, TAG), number, F32).astype(BF16)


def place_kernel(taken_ref, out_ref):
    width = taken_ref.shape[2] - TAG
    tags = [taken_ref[s, :, width:].astype(F32) for s in range(taken_ref.shape[0])]
    for lanes in range(0, width, TAG):
        values = [
            taken_ref[s, :, lanes : lanes + TAG].astype(F32) for s in range(taken_ref.shape[0])
        ]
        for number in range(out_ref.shape[0]):
            total = jnp.zeros_like(values[0])
            for tag, value in zip(tags, values):
                total = total + jnp.where(tag == number + 1, value, 0.0)
            out_ref[number, :, lanes : lanes + TAG] = total.astype(BF16)


def merge_kernel(core_ref, pair_ref, out_ref, copies_ref):
    half = out_ref.shape[2]

    def merge(first):
        for b in range(out_ref.shape[0]):
            rows = [pair_ref[k, b, :, first : first + half].astype(F32) for k in range(2)]
            rows = (rows[0] + rows[1]).astype(BF16)
            out_ref[b] = rows
            for copy in range(copies_ref.shape[0]):
                copies_ref[copy, b] = rows

    @pl.when(core_ref[0] == 0)
    def _():
        merge(0)

    @pl.when(core_ref[0] == 1)
    def _():
        merge(half)


def product_kernel(group, tile_ref, halves_ref, out_ref):
    half = halves_ref.shape[2]
    back = by_core((2 * half, 2 * half), 1, group)
    panel = dot(halves_ref[0], back[:half]) + dot(halves_ref[1], back[half:])
    panel = panel.astype(BF16)
    high, low = split(tile_ref[...])
    out_ref[...] = (dot(high, panel) + dot(low, panel)).astype(BF16)


def body(front_rows, slot_blocks, inv_factor, ancestor_inv):
    col_count = lax.axis_size("col")
    row_count = lax.axis_size("row")
    chip_count = row_count // 2
    col_index = lax.axis_index("col")
    core = lax.axis_index("row") % 2
    core_arg = jnp.reshape(core, (1,)).astype(jnp.int32)
    slot_count, chunk_rows, width = front_rows.shape
    half = width // 2
    tile_rows, panel_rows = ancestor_inv.shape
    block_rows = chunk_rows * col_count
    panel_blocks = panel_rows // block_rows
    share = tile_rows // col_count
    diag_width = width // col_count
    same_core = [[2 * j + k for j in range(chip_count)] for k in range(2)]
    core_pairs = [[2 * j, 2 * j + 1] for j in range(chip_count)]

    def pair_gather(x):
        return lax.all_gather(x, "row", axis=0, axis_index_groups=core_pairs)

    def over_row(x):
        return lax.all_to_all(x, "row", 0, 0, tiled=True, axis_index_groups=same_core)

    def over_col(x):
        return lax.all_to_all(x, "col", 0, 0, tiled=True)

    factor_cols = lax.dynamic_slice_in_dim(inv_factor, col_index * diag_width, diag_width, 1)
    factor_gram = lax.optimization_barrier(
        lax.dot_general(
            factor_cols,
            inv_factor,
            (((0,), (0,)), ((), ())),
            precision=lax.Precision.HIGHEST,
            preferred_element_type=F32,
        )
    )

    by_panel = pl.pallas_call(
        lambda *refs: scale_kernel(panel_blocks, diag_width, *refs),
        out_shape=jax.ShapeDtypeStruct((col_count, chunk_rows, width + TAG), BF16),
        in_specs=[SMEM, VMEM, VMEM],
        out_specs=VMEM,
        scratch_shapes=[pltpu.VMEM((slot_count * chunk_rows, width), F32)],
        compiler_params=PARAMS,
    )(slot_blocks, front_rows.reshape(slot_count * chunk_rows, width), inv_factor)
    placed = pl.pallas_call(
        place_kernel,
        out_shape=jax.ShapeDtypeStruct((panel_blocks, chunk_rows, width), BF16),
        in_specs=[VMEM],
        out_specs=VMEM,
        compiler_params=PARAMS,
    )(over_row(by_panel))
    piece, copies = pl.pallas_call(
        merge_kernel,
        out_shape=(
            jax.ShapeDtypeStruct((panel_blocks, chunk_rows, half), BF16),
            jax.ShapeDtypeStruct((col_count, panel_blocks, chunk_rows, half), BF16),
        ),
        in_specs=[SMEM, VMEM],
        out_specs=(VMEM, VMEM),
        compiler_params=PARAMS,
    )(core_arg, pair_gather(placed))

    route = [
        ((2 * j + k) * col_count + p, (2 * p + k) * col_count + j)
        for j in range(chip_count)
        for k in range(2)
        for p in range(col_count)
    ]
    turned = lax.ppermute(piece, ("row", "col"), route)
    pair_factor = over_col(copies).transpose(1, 0, 2, 3).reshape(2 * tile_rows, half)
    copies = jnp.broadcast_to(turned[None], (chip_count, *turned.shape))
    own_half = over_row(copies).transpose(1, 0, 2, 3).reshape(panel_rows, half)

    partial_sums = pl.pallas_call(
        lambda *refs: product_kernel(diag_width, *refs),
        out_shape=jax.ShapeDtypeStruct((tile_rows, width), BF16),
        in_specs=[VMEM, VMEM],
        out_specs=VMEM,
        compiler_params=PARAMS,
    )(ancestor_inv, pair_gather(own_half))
    pair_sums = pair_gather(partial_sums).reshape(2 * tile_rows, width)
    gram_half = dot(pair_factor, pair_sums, ((0,), (0,))).astype(BF16)
    sent = jnp.concatenate(
        [
            gram_half.reshape(col_count, diag_width // 2, width),
            partial_sums.reshape(col_count, share, width),
        ],
        1,
    )
    sums = jnp.sum(over_col(sent).astype(F32), axis=0)
    gram_piece, column_total = sums[: diag_width // 2], sums[diag_width // 2 :]
    copies = jnp.broadcast_to(gram_piece.astype(BF16)[None], (chip_count, *gram_piece.shape))
    gram_rows = jnp.sum(over_row(copies).astype(F32), axis=0)
    gram_block = pair_gather(gram_rows).reshape(diag_width, width)
    return (-column_total, factor_gram + gram_block)


def solution(mesh):
    in_specs = (P("row", "col", None), P("row"), P(), P("row", "col"))
    out_specs = (P(("row", "col"), None), P("col", None))
    return jax.shard_map(body, mesh=mesh, in_specs=in_specs, out_specs=out_specs, check_vma=False)
```

time: 134 us -> 128 us (0.955)
  blocking collectives: 69.4 us -> 39.5 us
  waiting for transfers between devices: 25.9 us -> 41.9 us
  starting transfers between devices: 27.4 us -> 34.4 us
  Pallas kernels: 0 us -> 3.99 us
  matrix products: 4.21 us -> 1.12 us
  local copies, waits for them, and re-layouts: 1.89 us -> 4.33 us
  other arithmetic: 3.34 us -> 1.45 us
    all_to_all x3 -> x1, blocking collectives: 58.6 us -> 23.4 us  [over_col(): return lax.all_to_all(x, 'col', 0, 0, tiled=True)]
    all_to_all x3 -> x4, waiting for transfers between devices: 21.8 us -> 41.9 us  [the longest x3 29.1 us: over_row(): lax.all_to_all(x, 'row', 0, 0, tiled=True, axis_index_groups=same_core)]
    all_to_all x3 -> x4, starting transfers between devices: 19 us -> 33.7 us  [the longest x3 23.5 us: over_row(): lax.all_to_all(x, 'row', 0, 0, tiled=True, axis_index_groups=same_core)]
    ppermute x2 -> x1, starting transfers between devices: 8.38 us -> 0.66 us  [body(): turned = lax.ppermute(piece, ('row', 'col'), route)]
    all_gather x3 -> x4, blocking collectives: 10.8 us -> 16 us  [pair_gather(): return lax.all_gather(x, 'row', axis=0, axis_index_groups=core_pairs)]
    ppermute x2 -> x1, waiting for transfers between devices: 4.08 us -> 0.01 us  [body(): turned = lax.ppermute(piece, ('row', 'col'), route)]
    pallas_call x0 -> x4, Pallas kernels: none -> 3.99 us  [the longest x1 1.88 us: body(): pl.pallas_call(lambda *refs: scale_kernel(panel_blocks, diag_width, *refs...]
    unnamed x4 -> x10, local copies, waits for them, and re-layouts: 0.02 us -> 2.79 us
  transfers between devices with their start and end apart: 5 -> 5, of which waited for: 5 -> 4; matrix products, arithmetic and copies ran while one was open for 0% -> 1% of each run, Pallas kernels for 0% -> 0%
where the time goes in v2:
time: 128 us; the launch traced here: 127 us
  waiting for transfers between devices  41.9 us (33%)
  blocking collectives  39.5 us (31%)
  starting transfers between devices  34.4 us (27%)
  local copies, waits for them, and re-layouts  4.33 us (3%)
  Pallas kernels  3.99 us (3%)
  other arithmetic  1.45 us (1%)
    all_to_all x3, waiting for transfers between devices, over_row(): lax.all_to_all(x, 'row', 0, 0, tiled=True, axis_index_groups=same_core)  29.1 us
    all_to_all x3, starting transfers between devices, over_row(): lax.all_to_all(x, 'row', 0, 0, tiled=True, axis_index_groups=same_core)  23.5 us
    all_to_all x1, blocking collectives, over_col(): return lax.all_to_all(x, 'col', 0, 0, tiled=True)  23.4 us
    all_gather x4, blocking collectives, pair_gather(): return lax.all_gather(x, 'row', axis=0, axis_index_groups=core_pairs)  16 us
    all_to_all x1, waiting for transfers between devices, over_col(): return lax.all_to_all(x, 'col', 0, 0, tiled=True)  12.8 us
    all_to_all x1, starting transfers between devices, over_col(): return lax.all_to_all(x, 'col', 0, 0, tiled=True)  10.2 us
    unnamed x10, local copies, waits for them, and re-layouts  2.79 us
  transfers between devices with their start and end apart: 5, of which 4 were waited for; matrix products, arithmetic and copies ran while one was open for 1% of the time, Pallas kernels for 0%

profile of v2, /device:TPU:1, one launch (start us, length us, event | category | flops | bytes accessed | tf_op | source)
XLA Modules:
  0.0 127.4 jit_solution(685540425745440203)
XLA Ops:
  0.6 1.2 copy-done
  1.9 0.9 copy-done.3
  2.8 0.7 copy-done.4
  3.4 1.9 %shard_map.59 = bf16[16,8,640]{2,1,0:T(8,128)(2,1)} custom-call(s32[16]{0:T(128)S(1)} %copy-done.4, bf16[128,512]{1,0:T(8,128)(2,1)S(1)} %bitcast.15, f32[512,512]{1,0:T(8,128)S(1)} %copy-done), custom_call_target="tpu_custom_call" | custom-call | tf_op jit(solution)/shard_map/pallas_call | solution.py:134
  5.3 10.2 %all-to-all-start = ((bf16[16,8,640]{2,1,0:T(8,128)(2,1)}), bf16[16,8,640]{2,1,0:T(8,128)(2,1)S(1)}, u32[]{:S(2)}, u32[]{:S(2)}) async-start(bf16[16,8,640]{2,1,0:T(8,128)(2,1)} %shard_map.59), calls=%async_computation | async-start | bytes 327680 | tf_op jit(solution)/shard_map/all_to_all | solution.py:118
  15.6 8.9 %all-to-all-done.taken_ref = bf16[16,8,640]{2,1,0:T(8,128)(2,1)S(1)} async-done(((bf16[16,8,640]{2,1,0:T(8,128)(2,1)}), bf16[16,8,640]{2,1,0:T(8,128)(2,1)S(1)}, u32[]{:S(2)}, u32[]{:S(2)}) %all-to-all-start) | async-done | bytes 163872 | tf_op jit(solution)/shard_map/all_to_all | solution.py:118
  24.7 3.8 %all-gather = bf16[12,8,512]{2,1,0:T(8,128)(2,1)S(1)} all-gather(bf16[6,8,512]{2,1,0:T(8,128)(2,1)S(1)} %shard_map.60), channel_id=2, replica_groups={{0,16},{32,48},{64,80},{96,112},{128,144},{160,176},{192,208},{224,240}..., dimensions={0}, use_global_device_ids=true | all-gather | bytes 147456 | tf_op jit(solution)/shard_map/all_gather | solution.py:115
  28.5 0.8 shard_map.61
  29.3 10.2 %all-to-all-start.1 = ((bf16[16,6,8,256]{3,2,1,0:T(8,128)(2,1)}), bf16[16,6,8,256]{3,2,1,0:T(8,128)(2,1)S(1)}, u32[]{:S(2)}, u32[]{:S(2)}) async-start(bf16[16,6,8,256]{3,2,1,0:T(8,128)(2,1)} %get-tuple-element.4), calls=%async_computation.1 | async-start | bytes 786432 | tf_op jit(solution)/shard_map/all_to_all | solution.py:121
  39.5 0.7 collective-permute-start
  40.1 12.8 %all-to-all-done.1 = bf16[16,6,8,256]{3,2,1,0:T(8,128)(2,1)S(1)} async-done(((bf16[16,6,8,256]{3,2,1,0:T(8,128)(2,1)}), bf16[16,6,8,256]{3,2,1,0:T(8,128)(2,1)S(1)}, u32[]{:S(2)}, u32[]{:S(2)}) %all-to-all-start.1) | async-done | bytes 393248 | tf_op jit(solution)/shard_map/all_to_all | solution.py:121
  53.0 0.8 broadcast_in_dim.4
  53.7 8.2 %all-to-all-start.2 = ((bf16[16,6,8,256]{3,2,1,0:T(8,128)(2,1)}), bf16[16,6,8,256]{3,2,1,0:T(8,128)(2,1)S(1)}, u32[]{:S(2)}, u32[]{:S(2)}) async-start(bf16[16,6,8,256]{3,2,1,0:T(8,128)(2,1)} %broadcast_in_dim.4), calls=%async_computation.2 | async-start | bytes 786432 | tf_op jit(solution)/shard_map/all_to_all | solution.py:118
  61.9 12.2 %all-to-all-done.2 = bf16[16,6,8,256]{3,2,1,0:T(8,128)(2,1)S(1)} async-done(((bf16[16,6,8,256]{3,2,1,0:T(8,128)(2,1)}), bf16[16,6,8,256]{3,2,1,0:T(8,128)(2,1)S(1)}, u32[]{:S(2)}, u32[]{:S(2)}) %all-to-all-start.2) | async-done | bytes 393248 | tf_op jit(solution)/shard_map/all_to_all | solution.py:118
  74.2 4.8 %all_gather.23.refs_1_ = bf16[2,768,256]{2,1,0:T(8,128)(2,1)S(1)} all-gather(bf16[1,768,256]{2,1,0:T(8,128)(2,1)S(1)} %bitcast.17), channel_id=1, replica_groups={{0,16},{32,48},{64,80},{96,112},{128,144},{160,176},{192,208},{224,240}..., dimensions={0}, use_global_device_ids=true | all-gather | bytes 1179648 | tf_op jit(solution)/shard_map/all_gather | solution.py:115
  79.0 1.2 shard_map.62
  80.2 2.4 %all-gather.1 = bf16[768,512]{1,0:T(8,128)(2,1)S(1)} all-gather(bf16[384,512]{1,0:T(8,128)(2,1)S(1)} %shard_map.62), channel_id=3, replica_groups={{0,16},{32,48},{64,80},{96,112},{128,144},{160,176},{192,208},{224,240}..., dimensions={0}, use_global_device_ids=true | all-gather | bytes 1179648 | tf_op jit(solution)/shard_map/all_gather | solution.py:115
  83.0 23.4 %all_to_all.25 = bf16[16,40,512]{2,1,0:T(8,128)(2,1)S(1)} all-to-all(bf16[16,40,512]{2,1,0:T(8,128)(2,1)S(1)} %pad_maximum_fusion), channel_id=1, replica_groups=mesh['row'=32,'col'=16] {'col'}, dimensions={0} | all-to-all | bytes 1310720 | tf_op jit(solution)/shard_map/all_to_all | solution.py:121
  106.6 0.7 broadcast_in_dim.5
  107.3 5.1 %all-to-all-start.4 = ((bf16[16,16,512]{2,1,0:T(8,128)(2,1)}), bf16[16,16,512]{2,1,0:T(8,128)(2,1)S(1)}, u32[]{:S(2)}, u32[]{:S(2)}) async-start(bf16[16,16,512]{2,1,0:T(8,128)(2,1)} %broadcast_in_dim.5), calls=%async_computation.4 | async-start | bytes 524288 | tf_op jit(solution)/shard_map/all_to_all | solution.py:118
  112.5 0.7 fusion
  113.8 7.9 %all-to-all-done.4 = bf16[16,16,512]{2,1,0:T(8,128)(2,1)S(1)} async-done(((bf16[16,16,512]{2,1,0:T(8,128)(2,1)}), bf16[16,16,512]{2,1,0:T(8,128)(2,1)S(1)}, u32[]{:S(2)}, u32[]{:S(2)}) %all-to-all-start.4) | async-done | bytes 262176 | tf_op jit(solution)/shard_map/all_to_all | solution.py:118
  121.8 5.0 %all-gather.2 = f32[32,512]{1,0:T(8,128)S(1)} all-gather(f32[16,512]{1,0:T(8,128)S(1)} %convert_reduce_fusion.1), channel_id=4, replica_groups={{0,16},{32,48},{64,80},{96,112},{128,144},{160,176},{192,208},{224,240}..., dimensions={0}, use_global_device_ids=true | all-gather | bytes 98304 | tf_op jit(solution)/shard_map/all_gather | solution.py:115
  126.8 0.6 add.12
  (17 shorter events, 1.4 us)
Async XLA Ops:
  0.6 1.2 copy-start
  1.9 0.9 copy-start.3
  2.8 0.7 copy-start.4
  5.3 19.2 %all-to-all-start = ((bf16[16,8,640]{2,1,0:T(8,128)(2,1)}), bf16[16,8,640]{2,1,0:T(8,128)(2,1)S(1)}, u32[]{:S(2)}, u32[]{:S(2)}) async-start(bf16[16,8,640]{2,1,0:T(8,128)(2,1)} %shard_map.59), calls=%async_computation | async-start | bytes 327680 | tf_op jit(solution)/shard_map/all_to_all | solution.py:118
  29.3 23.7 %all-to-all-start.1 = ((bf16[16,6,8,256]{3,2,1,0:T(8,128)(2,1)}), bf16[16,6,8,256]{3,2,1,0:T(8,128)(2,1)S(1)}, u32[]{:S(2)}, u32[]{:S(2)}) async-start(bf16[16,6,8,256]{3,2,1,0:T(8,128)(2,1)} %get-tuple-element.4), calls=%async_computation.1 | async-start | bytes 786432 | tf_op jit(solution)/shard_map/all_to_all | solution.py:121
  39.5 0.7 collective-permute-start
  53.7 20.5 %all-to-all-start.2 = ((bf16[16,6,8,256]{3,2,1,0:T(8,128)(2,1)}), bf16[16,6,8,256]{3,2,1,0:T(8,128)(2,1)S(1)}, u32[]{:S(2)}, u32[]{:S(2)}) async-start(bf16[16,6,8,256]{3,2,1,0:T(8,128)(2,1)} %broadcast_in_dim.4), calls=%async_computation.2 | async-start | bytes 786432 | tf_op jit(solution)/shard_map/all_to_all | solution.py:118
  61.9 17.1 %copy-start.2 = (f32[384,768]{1,0:T(8,128)S(1)}, f32[384,768]{1,0:T(8,128)}, u32[]{:S(2)}) copy-start(f32[384,768]{1,0:T(8,128)} %refs_0_.3) | copy-start | bytes 3538948
  83.0 29.4 %copy-start.1 = (f32[512,512]{1,0:T(8,128)S(1)}, f32[512,512]{1,0:T(8,128)}, u32[]{:S(2)}) copy-start(f32[512,512]{1,0:T(8,128)} %refs_2_.1) | copy-start | bytes 3145732
  107.3 14.4 %all-to-all-start.4 = ((bf16[16,16,512]{2,1,0:T(8,128)(2,1)}), bf16[16,16,512]{2,1,0:T(8,128)(2,1)S(1)}, u32[]{:S(2)}, u32[]{:S(2)}) async-start(bf16[16,16,512]{2,1,0:T(8,128)(2,1)} %broadcast_in_dim.5), calls=%async_computation.4 | async-start | bytes 524288 | tf_op jit(solution)/shard_map/all_to_all | solution.py:118

commit v3 on v2

--- a/solution.py
+++ b/solution.py
@@ -65,16 +65,13 @@
             out_ref[number, :, lanes : lanes + TAG] = total.astype(BF16)
 
 
-def merge_kernel(core_ref, pair_ref, out_ref, copies_ref):
+def merge_kernel(core_ref, pair_ref, out_ref):
     half = out_ref.shape[2]
 
     def merge(first):
         for b in range(out_ref.shape[0]):
             rows = [pair_ref[k, b, :, first : first + half].astype(F32) for k in range(2)]
-            rows = (rows[0] + rows[1]).astype(BF16)
-            out_ref[b] = rows
-            for copy in range(copies_ref.shape[0]):
-                copies_ref[copy, b] = rows
+            out_ref[b] = (rows[0] + rows[1]).astype(BF16)
 
     @pl.when(core_ref[0] == 0)
     def _():
@@ -137,7 +134,7 @@
         in_specs=[SMEM, VMEM, VMEM],
         out_specs=VMEM,
         scratch_shapes=[pltpu.VMEM((slot_count * chunk_rows, width), F32)],
-        compiler_params=PARAMS,
+        compiler_params=pltpu.CompilerParams(vmem_limit_bytes=60 * 2**20),
     )(slot_blocks, front_rows.reshape(slot_count * chunk_rows, width), inv_factor)
     placed = pl.pallas_call(
         place_kernel,
@@ -146,14 +143,11 @@
         out_specs=VMEM,
         compiler_params=PARAMS,
     )(over_row(by_panel))
-    piece, copies = pl.pallas_call(
+    piece = pl.pallas_call(
         merge_kernel,
-        out_shape=(
-            jax.ShapeDtypeStruct((panel_blocks, chunk_rows, half), BF16),
-            jax.ShapeDtypeStruct((col_count, panel_blocks, chunk_rows, half), BF16),
-        ),
+        out_shape=jax.ShapeDtypeStruct((panel_blocks, chunk_rows, half), BF16),
         in_specs=[SMEM, VMEM],
-        out_specs=(VMEM, VMEM),
+        out_specs=VMEM,
         compiler_params=PARAMS,
     )(core_arg, pair_gather(placed))
 
@@ -164,9 +158,20 @@
         for p in range(col_count)
     ]
     turned = lax.ppermute(piece, ("row", "col"), route)
-    pair_factor = over_col(copies).transpose(1, 0, 2, 3).reshape(2 * tile_rows, half)
     copies = jnp.broadcast_to(turned[None], (chip_count, *turned.shape))
     own_half = over_row(copies).transpose(1, 0, 2, 3).reshape(panel_rows, half)
+
+    turns = share // chunk_rows
+    by_tile = piece.reshape(2, turns, chunk_rows, half)
+    chunks = [
+        lax.ppermute(
+            lax.dynamic_index_in_dim(by_tile, (t - col_index) % turns, 1, keepdims=False),
+            "col",
+            [((turns * d + t) % col_count, d) for d in range(col_count)],
+        )
+        for t in range(turns)
+    ]
+    pair_factor = jnp.stack(chunks, 1).reshape(2 * share, half)
 
     partial_sums = pl.pallas_call(
         lambda *refs: product_kernel(diag_width, *refs),
@@ -175,17 +180,19 @@
         out_specs=VMEM,
         compiler_params=PARAMS,
     )(ancestor_inv, pair_gather(own_half))
-    pair_sums = pair_gather(partial_sums).reshape(2 * tile_rows, width)
-    gram_half = dot(pair_factor, pair_sums, ((0,), (0,))).astype(BF16)
-    sent = jnp.concatenate(
-        [
-            gram_half.reshape(col_count, diag_width // 2, width),
-            partial_sums.reshape(col_count, share, width),
-        ],
-        1,
-    )
-    sums = jnp.sum(over_col(sent).astype(F32), axis=0)
-    gram_piece, column_total = sums[: diag_width // 2], sums[diag_width // 2 :]
+    arrived = over_col(partial_sums.reshape(col_count, share, width))
+    column_total = jnp.sum(arrived.astype(F32), axis=0)
+
+    pair_total = pair_gather(column_total).reshape(2 * share, width)
+    gram_half = lax.dot_general(
+        pair_factor.astype(F32),
+        pair_total,
+        (((0,), (0,)), ((), ())),
+        precision=lax.Precision.HIGH,
+        preferred_element_type=F32,
+    ).astype(BF16)
+    arrived = over_col(gram_half.reshape(col_count, diag_width // 2, width))
+    gram_piece = jnp.sum(arrived.astype(F32), axis=0)
     copies = jnp.broadcast_to(gram_piece.astype(BF16)[None], (chip_count, *gram_piece.shape))
     gram_rows = jnp.sum(over_row(copies).astype(F32), axis=0)
     gram_block = pair_gather(gram_rows).reshape(diag_width, width)

time: 128 us -> 132 us (1.031)
  blocking collectives: 39.5 us -> 68.7 us
  waiting for transfers between devices: 41.9 us -> 19.3 us
  local copies, waits for them, and re-layouts: 4.33 us -> 0.79 us
    all_to_all x0 -> x1, blocking collectives: none -> 32.2 us  [over_row(): lax.all_to_all(x, 'row', 0, 0, tiled=True, axis_index_groups=same_core)]
    all_to_all x3 -> x2, waiting for transfers between devices: 29.1 us -> 16.8 us  [over_row(): lax.all_to_all(x, 'row', 0, 0, tiled=True, axis_index_groups=same_core)]
    all_to_all x1, waiting for transfers between devices: 12.8 us -> 1.8 us  [over_col(): return lax.all_to_all(x, 'col', 0, 0, tiled=True)]
    ppermute x0 -> x3, starting transfers between devices: none -> 10.9 us  [body(): lax.ppermute(lax.dynamic_index_in_dim(by_tile, (t - col_index) % turns, 1...]
    all_to_all x3 -> x2, starting transfers between devices: 23.5 us -> 15.4 us  [over_row(): lax.all_to_all(x, 'row', 0, 0, tiled=True, axis_index_groups=same_core)]
    all_to_all x1, blocking collectives: 23.4 us -> 18.6 us  [over_col(): return lax.all_to_all(x, 'col', 0, 0, tiled=True)]
    all_to_all x1, starting transfers between devices: 10.2 us -> 7.13 us  [over_col(): return lax.all_to_all(x, 'col', 0, 0, tiled=True)]
    unnamed x10 -> x4, local copies, waits for them, and re-layouts: 2.79 us -> 0.01 us
  transfers between devices with their start and end apart: 5 -> 7, of which waited for: 4 -> 4; matrix products, arithmetic and copies ran while one was open for 1% -> 1% of each run, Pallas kernels for 0% -> 0%
where the time goes in v3:
time: 132 us; the launch traced here: 131 us
  blocking collectives  68.7 us (52%)
  starting transfers between devices  34 us (26%)
  waiting for transfers between devices  19.3 us (15%)
  Pallas kernels  4.78 us (4%)
  other arithmetic  1.41 us (1%)
    all_to_all x1, blocking collectives, over_row(): lax.all_to_all(x, 'row', 0, 0, tiled=True, axis_index_groups=same_core)  32.2 us
    all_to_all x1, blocking collectives, over_col(): return lax.all_to_all(x, 'col', 0, 0, tiled=True)  18.6 us
    all_gather x4, blocking collectives, pair_gather(): return lax.all_gather(x, 'row', axis=0, axis_index_groups=core_pairs)  17.9 us
    all_to_all x2, waiting for transfers between devices, over_row(): lax.all_to_all(x, 'row', 0, 0, tiled=True, axis_index_groups=same_core)  16.8 us
    all_to_all x2, starting transfers between devices, over_row(): lax.all_to_all(x, 'row', 0, 0, tiled=True, axis_index_groups=same_core)  15.4 us
    ppermute x3, starting transfers between devices, body(): lax.ppermute(lax.dynamic_index_in_dim(by_tile, (t - col_index) % turns, 1...  10.9 us
    all_to_all x1, starting transfers between devices, over_col(): return lax.all_to_all(x, 'col', 0, 0, tiled=True)  7.13 us
    pallas_call x1, Pallas kernels, body(): pl.pallas_call(lambda *refs: scale_kernel(panel_blocks, diag_width, *refs...  2.66 us
  transfers between devices with their start and end apart: 7, of which 4 were waited for; matrix products, arithmetic and copies ran while one was open for 1% of the time, Pallas kernels for 0%

profile of v3, /device:TPU:1, one launch (start us, length us, event | category | flops | bytes accessed | tf_op | source)
XLA Modules:
  0.0 130.9 jit_solution(5149355963242470308)
XLA Ops:
  0.6 2.7 %shard_map.59 = bf16[16,8,640]{2,1,0:T(8,128)(2,1)} custom-call(s32[16]{0:T(128)} %refs_0_.2, bf16[128,512]{1,0:T(8,128)(2,1)} %bitcast.26, f32[512,512]{1,0:T(8,128)} %refs_2_.1), custom_call_target="tpu_custom_call" | custom-call | tf_op jit(solution)/shard_map/pallas_call | solution.py:131
  3.3 10.2 %all-to-all-start = ((bf16[16,8,640]{2,1,0:T(8,128)(2,1)}), bf16[16,8,640]{2,1,0:T(8,128)(2,1)S(1)}, u32[]{:S(2)}, u32[]{:S(2)}) async-start(bf16[16,8,640]{2,1,0:T(8,128)(2,1)} %shard_map.59), calls=%async_computation | async-start | bytes 327680 | tf_op jit(solution)/shard_map/all_to_all | solution.py:115
  13.6 8.9 %all-to-all-done.taken_ref = bf16[16,8,640]{2,1,0:T(8,128)(2,1)S(1)} async-done(((bf16[16,8,640]{2,1,0:T(8,128)(2,1)}), bf16[16,8,640]{2,1,0:T(8,128)(2,1)S(1)}, u32[]{:S(2)}, u32[]{:S(2)}) %all-to-all-start) | async-done | bytes 163872 | tf_op jit(solution)/shard_map/all_to_all | solution.py:115
  22.7 3.8 %all-gather = bf16[12,8,512]{2,1,0:T(8,128)(2,1)S(1)} all-gather(bf16[6,8,512]{2,1,0:T(8,128)(2,1)S(1)} %shard_map.60), channel_id=2, replica_groups={{0,16},{32,48},{64,80},{96,112},{128,144},{160,176},{192,208},{224,240}..., dimensions={0}, use_global_device_ids=true | all-gather | bytes 147456 | tf_op jit(solution)/shard_map/all_gather | solution.py:112
  26.5 0.7 collective-permute-start
  27.2 32.2 %all_to_all.25 = bf16[16,6,8,256]{3,2,1,0:T(8,128)(2,1)S(1)} all-to-all(bf16[16,6,8,256]{3,2,1,0:T(8,128)(2,1)S(1)} %broadcast_in_dim.4), channel_id=1, replica_groups={{0,32,64,96,128,160,192,224,256,288,320,352,384,416,448,480},{16,48,80,..., dimensions={0} | all-to-all | bytes 786432 | tf_op jit(solution)/shard_map/all_to_all | solution.py:115
  59.5 4.9 %all_gather.23.refs_1_ = bf16[2,768,256]{2,1,0:T(8,128)(2,1)S(1)} all-gather(bf16[1,768,256]{2,1,0:T(8,128)(2,1)S(1)} %bitcast.24), channel_id=1, replica_groups={{0,16},{32,48},{64,80},{96,112},{128,144},{160,176},{192,208},{224,240}..., dimensions={0}, use_global_device_ids=true | all-gather | bytes 1179648 | tf_op jit(solution)/shard_map/all_gather | solution.py:112
  64.4 1.9 %shard_map.62 = bf16[384,512]{1,0:T(8,128)(2,1)} custom-call(f32[384,768]{1,0:T(8,128)S(1)} %copy-done, bf16[2,768,256]{2,1,0:T(8,128)(2,1)S(1)} %all_gather.23.refs_1_), custom_call_target="tpu_custom_call" | custom-call | tf_op jit(solution)/shard_map/pallas_call | solution.py:176
  66.3 7.1 %all-to-all-start.2 = ((bf16[16,24,512]{2,1,0:T(8,128)(2,1)}), bf16[16,24,512]{2,1,0:T(8,128)(2,1)S(1)}, u32[]{:S(2)}, u32[]{:S(2)}) async-start(bf16[16,24,512]{2,1,0:T(8,128)(2,1)} %bitcast.5), calls=%async_computation.2 | async-start | bytes 786432 | tf_op jit(solution)/shard_map/all_to_all | solution.py:118
  73.5 5.0 %collective-permute-start.2 = (bf16[2,8,256]{2,1,0:T(8,128)(2,1)S(1)}, bf16[2,8,256]{2,1,0:T(8,128)(2,1)S(1)}, u32[]{:S(2)}, u32[]{:S(2)}) collective-permute-start(bf16[2,8,256]{2,1,0:T(8,128)(2,1)S(1)} %get-tuple-element.4), channel_id=1, source_target_pairs={{1,0},{4,1},{7,2},{10,3},{13,4},{0,5},{3,6},{6,7},{9,8},{12,9},{15... | collective-permute-start | bytes 24584 | tf_op jit(solution)/shard_map/ppermute | solution.py:167
  78.5 5.2 %collective-permute-start.3 = (bf16[2,8,256]{2,1,0:T(8,128)(2,1)S(1)}, bf16[2,8,256]{2,1,0:T(8,128)(2,1)S(1)}, u32[]{:S(2)}, u32[]{:S(2)}) collective-permute-start(bf16[2,8,256]{2,1,0:T(8,128)(2,1)S(1)} %get-tuple-element.3), channel_id=1, source_target_pairs={{2,0},{5,1},{8,2},{11,3},{14,4},{1,5},{4,6},{7,7},{10,8},{13,9},{0... | collective-permute-start | bytes 24584 | tf_op jit(solution)/shard_map/ppermute | solution.py:167
  83.7 0.7 collective-permute-start.1
  84.4 0.7 collective-permute-done.3
  85.1 1.8 %all-to-all-done.2 = bf16[16,24,512]{2,1,0:T(8,128)(2,1)S(1)} async-done(((bf16[16,24,512]{2,1,0:T(8,128)(2,1)}), bf16[16,24,512]{2,1,0:T(8,128)(2,1)S(1)}, u32[]{:S(2)}, u32[]{:S(2)}) %all-to-all-start.2) | async-done | bytes 393248 | tf_op jit(solution)/shard_map/all_to_all | solution.py:118
  87.0 4.2 %all-gather.1 = f32[48,512]{1,0:T(8,128)S(1)} all-gather(f32[24,512]{1,0:T(8,128)S(1)} %convert_reduce_fusion), channel_id=3, replica_groups={{0,16},{32,48},{64,80},{96,112},{128,144},{160,176},{192,208},{224,240}..., dimensions={0}, use_global_device_ids=true | all-gather | bytes 147456 | tf_op jit(solution)/shard_map/all_gather | solution.py:112
  91.2 0.3 convolution_convert_fusion
  91.6 18.6 %all_to_all.26 = bf16[16,16,512]{2,1,0:T(8,128)(2,1)S(1)} all-to-all(bf16[16,16,512]{2,1,0:T(8,128)(2,1)S(1)} %bitcast.25), channel_id=1, replica_groups=mesh['row'=32,'col'=16] {'col'}, dimensions={0} | all-to-all | bytes 524288 | tf_op jit(solution)/shard_map/all_to_all | solution.py:118
  110.2 0.7 broadcast_in_dim.5
  110.9 5.1 %all-to-all-start.4 = ((bf16[16,16,512]{2,1,0:T(8,128)(2,1)}), bf16[16,16,512]{2,1,0:T(8,128)(2,1)S(1)}, u32[]{:S(2)}, u32[]{:S(2)}) async-start(bf16[16,16,512]{2,1,0:T(8,128)(2,1)} %broadcast_in_dim.5), calls=%async_computation.4 | async-start | bytes 524288 | tf_op jit(solution)/shard_map/all_to_all | solution.py:115
  116.1 0.7 fusion
  116.8 0.6 neg.3
  117.4 7.9 %all-to-all-done.4 = bf16[16,16,512]{2,1,0:T(8,128)(2,1)S(1)} async-done(((bf16[16,16,512]{2,1,0:T(8,128)(2,1)}), bf16[16,16,512]{2,1,0:T(8,128)(2,1)S(1)}, u32[]{:S(2)}, u32[]{:S(2)}) %all-to-all-start.4) | async-done | bytes 262176 | tf_op jit(solution)/shard_map/all_to_all | solution.py:115
  125.4 4.9 %all-gather.2 = f32[32,512]{1,0:T(8,128)S(1)} all-gather(f32[16,512]{1,0:T(8,128)S(1)} %convert_reduce_fusion.1), channel_id=4, replica_groups={{0,16},{32,48},{64,80},{96,112},{128,144},{160,176},{192,208},{224,240}..., dimensions={0}, use_global_device_ids=true | all-gather | bytes 98304 | tf_op jit(solution)/shard_map/all_gather | solution.py:112
  130.3 0.6 add.37
  (16 shorter events, 0.4 us)
Async XLA Ops:
  3.3 19.2 %all-to-all-start = ((bf16[16,8,640]{2,1,0:T(8,128)(2,1)}), bf16[16,8,640]{2,1,0:T(8,128)(2,1)S(1)}, u32[]{:S(2)}, u32[]{:S(2)}) async-start(bf16[16,8,640]{2,1,0:T(8,128)(2,1)} %shard_map.59), calls=%async_computation | async-start | bytes 327680 | tf_op jit(solution)/shard_map/all_to_all | solution.py:115
  26.5 0.7 collective-permute-start
  59.4 4.9 %copy-start = (f32[384,768]{1,0:T(8,128)S(1)}, f32[384,768]{1,0:T(8,128)}, u32[]{:S(2)}) copy-start(f32[384,768]{1,0:T(8,128)} %refs_0_.3) | copy-start | bytes 3538948
  66.3 20.6 %all-to-all-start.2 = ((bf16[16,24,512]{2,1,0:T(8,128)(2,1)}), bf16[16,24,512]{2,1,0:T(8,128)(2,1)S(1)}, u32[]{:S(2)}, u32[]{:S(2)}) async-start(bf16[16,24,512]{2,1,0:T(8,128)(2,1)} %bitcast.5), calls=%async_computation.2 | async-start | bytes 786432 | tf_op jit(solution)/shard_map/all_to_all | solution.py:118
  73.5 10.9 %collective-permute-start.2 = (bf16[2,8,256]{2,1,0:T(8,128)(2,1)S(1)}, bf16[2,8,256]{2,1,0:T(8,128)(2,1)S(1)}, u32[]{:S(2)}, u32[]{:S(2)}) collective-permute-start(bf16[2,8,256]{2,1,0:T(8,128)(2,1)S(1)} %get-tuple-element.4), channel_id=1, source_target_pairs={{1,0},{4,1},{7,2},{10,3},{13,4},{0,5},{3,6},{6,7},{9,8},{12,9},{15... | collective-permute-start | bytes 24584 | tf_op jit(solution)/shard_map/ppermute | solution.py:167
  78.5 6.6 %collective-permute-start.3 = (bf16[2,8,256]{2,1,0:T(8,128)(2,1)S(1)}, bf16[2,8,256]{2,1,0:T(8,128)(2,1)S(1)}, u32[]{:S(2)}, u32[]{:S(2)}) collective-permute-start(bf16[2,8,256]{2,1,0:T(8,128)(2,1)S(1)} %get-tuple-element.3), channel_id=1, source_target_pairs={{2,0},{5,1},{8,2},{11,3},{14,4},{1,5},{4,6},{7,7},{10,8},{13,9},{0... | collective-permute-start | bytes 24584 | tf_op jit(solution)/shard_map/ppermute | solution.py:167
  83.7 1.4 %collective-permute-start.1 = (bf16[2,8,256]{2,1,0:T(8,128)(2,1)S(1)}, bf16[2,8,256]{2,1,0:T(8,128)(2,1)S(1)}, u32[]{:S(2)}, u32[]{:S(2)}) collective-permute-start(bf16[2,8,256]{2,1,0:T(8,128)(2,1)S(1)} %get-tuple-element.2), channel_id=1, source_target_pairs={{0,0},{3,1},{6,2},{9,3},{12,4},{15,5},{2,6},{5,7},{8,8},{11,9},{14... | collective-permute-start | bytes 24584 | tf_op jit(solution)/shard_map/ppermute | solution.py:167
  87.0 29.1 %copy-start.1 = (f32[512,512]{1,0:T(8,128)S(1)}, f32[512,512]{1,0:T(8,128)}, u32[]{:S(2)}) copy-start(f32[512,512]{1,0:T(8,128)} %refs_2_.1) | copy-start | bytes 3145732
  110.9 14.4 %all-to-all-start.4 = ((bf16[16,16,512]{2,1,0:T(8,128)(2,1)}), bf16[16,16,512]{2,1,0:T(8,128)(2,1)S(1)}, u32[]{:S(2)}, u32[]{:S(2)}) async-start(bf16[16,16,512]{2,1,0:T(8,128)(2,1)} %broadcast_in_dim.5), calls=%async_computation.4 | async-start | bytes 524288 | tf_op jit(solution)/shard_map/all_to_all | solution.py:115

commit v4 on v2

v4 whole, which is shorter than its diff:
```python
import itertools

import jax
import jax.numpy as jnp
import numpy as np
from jax import lax
from jax.experimental import pallas as pl
from jax.experimental.pallas import tpu as pltpu
from jax.sharding import PartitionSpec as P

BF16 = jnp.bfloat16
F32 = jnp.float32
TAG = 128
SMEM = pl.BlockSpec(memory_space=pltpu.SMEM)
VMEM = pl.BlockSpec(memory_space=pltpu.VMEM)
PARAMS = pltpu.CompilerParams(vmem_limit_bytes=16 * 2**20)
FETCHING = pltpu.CompilerParams(vmem_limit_bytes=60 * 2**20)


def dot(a, b, dims=((1,), (0,))):
    return lax.dot_general(a, b, (dims, ((), ())), preferred_element_type=F32)


def split(x):
    high = x.astype(BF16)
    return high, (x - high.astype(F32)).astype(BF16)


def by_core(width, group):
    part = group // 2
    column = np.arange(width)
    target = (column % group) // part * (width // 2) + column // group * part + column % part
    matrix = np.zeros((width, width), np.float32)
    matrix[column, target] = 1.0
    return matrix


def chip_position(chip, col, chip_count):
    ys = chip_count // 2
    return chip // ys * 2 + col % 2, chip % ys, col // 2


def hops(a, b, sizes):
    return sum(min((p - q) % n, (q - p) % n) for p, q, n in zip(a, b, sizes))


def short_routes(chip_count, col_count):
    sizes = (4, chip_count // 2, col_count // 2)
    table = np.zeros((col_count, col_count), np.int32)
    for p in range(col_count):
        source = [chip_position(p, c, chip_count) for c in range(col_count)]
        target = [chip_position(j, p, chip_count) for j in range(chip_count)]
        cost = [[hops(s, t, sizes) for t in target] for s in source]
        for limit in itertools.count():
            owner = {}

            def assign(c, seen):
                for j in range(chip_count):
                    if cost[c][j] <= limit and j not in seen:
                        seen.add(j)
                        if j not in owner or assign(owner[j], seen):
                            owner[j] = c
                            return True
                return False

            if all(assign(c, set()) for c in range(col_count)):
                break
        for j, c in owner.items():
            table[p, c] = j
    return table


def scale_kernel(panel_blocks, slots_ref, rows_ref, factor_ref, order_ref, out_ref, scaled_ref):
    half = factor_ref.shape[1] // 2
    high, low = split(factor_ref[...])
    rows = rows_ref[...]
    scaled = (dot(rows, high) + dot(rows, low)).astype(BF16)
    scaled_ref[...] = dot(scaled, order_ref[...])
    out_ref[...] = jnp.zeros_like(out_ref)
    slot_count = slots_ref.shape[0]
    height = rows_ref.shape[0] // slot_count
    for s in range(slot_count):
        block = slots_ref[s]

        @pl.when(block >= 0)
        def _():
            panel = block // panel_blocks
            number = (block - panel * panel_blocks + 1).astype(F32)
            for k in range(2):
                part = scaled_ref[s * height : (s + 1) * height, k * half : (k + 1) * half]
                out_ref[2 * panel + k, :, :half] = part.astype(BF16)
                out_ref[2 * panel + k, :, half:] = jnp.full((height, TAG), number, F32).astype(BF16)


def place_kernel(taken_ref, out_ref):
    width = taken_ref.shape[2] - TAG
    sources = range(taken_ref.shape[0])
    for lanes in range(0, width, TAG):
        totals = [jnp.zeros((taken_ref.shape[1], TAG), F32) for _ in range(out_ref.shape[0])]
        for s in sources:
            tag = taken_ref[s, :, width:].astype(F32)
            value = taken_ref[s, :, lanes : lanes + TAG].astype(F32)
            totals = [t + jnp.where(tag == n + 1, value, 0.0) for n, t in enumerate(totals)]
        for n, total in enumerate(totals):
            out_ref[n, :, lanes : lanes + TAG] = total.astype(BF16)


def product_kernel(col_ref, chip_ref, tile_ref, parts_ref, piece_ref, back_ref, out_ref, panel_ref, sent_ref):
    chunks, blocks, height, half = parts_ref.shape[1:]
    share = sent_ref.shape[1] - height
    for c in range(chunks):
        for b in range(blocks):
            first = (b * chunks + c) * height
            for k in range(2):
                rows = parts_ref[k, chip_ref[c], b].astype(F32)
                panel_ref[first : first + height, k * half : (k + 1) * half] = rows
    panel = dot(panel_ref[...].astype(BF16), back_ref[...]).astype(BF16)
    high, low = split(tile_ref[...])
    sums = dot(high, panel) + dot(low, panel)
    sent_ref[:, :share, :] = sums.reshape(chunks, share, 2 * half)
    sent_ref[:, share:, :] = jnp.zeros((chunks, height, 2 * half), F32)
    for b in range(blocks // 2):
        target = (b * chunks + col_ref[0]) // (share // height)
        for h in range(2):
            rows = piece_ref[h * (blocks // 2) + b].astype(F32)
            sent_ref[target, share:, h * half : (h + 1) * half] = rows
    out_ref[...] = sent_ref[...].astype(BF16)


def total_kernel(col_ref, arrived_ref, total_ref, factor_ref):
    sources = arrived_ref.shape[0]
    share, width = total_ref.shape
    height = arrived_ref.shape[1] - share
    total = arrived_ref[0].astype(F32)
    for s in range(1, sources):
        total = total + arrived_ref[s].astype(F32)
    total_ref[...] = total[:share]
    turns = share // height
    for t in range(turns):
        rows = arrived_ref[(turns * col_ref[0] + t) % sources].astype(F32)[share:]
        for h in range(2):
            first = h * share + t * height
            factor_ref[first : first + height, :] = rows[:, h * width // 2 : (h + 1) * width // 2]


def copies_kernel(arrived_ref, out_ref):
    total = arrived_ref[0].astype(F32)
    for s in range(1, arrived_ref.shape[0]):
        total = total + arrived_ref[s].astype(F32)
    for copy in range(out_ref.shape[0]):
        out_ref[copy] = total.astype(BF16)


def body(front_rows, slot_blocks, inv_factor, ancestor_inv):
    col_count = lax.axis_size("col")
    row_count = lax.axis_size("row")
    chip_count = row_count // 2
    col_index = lax.axis_index("col")
    slot_count, chunk_rows, width = front_rows.shape
    half = width // 2
    tile_rows, panel_rows = ancestor_inv.shape
    block_rows = chunk_rows * col_count
    panel_blocks = panel_rows // block_rows
    share = tile_rows // col_count
    diag_width = width // col_count
    same_core = [[2 * j + k for j in range(chip_count)] for k in range(2)]
    core_pairs = [[2 * j, 2 * j + 1] for j in range(chip_count)]
    order = by_core(width, diag_width)
    table = short_routes(chip_count, col_count)
    col_arg = jnp.reshape(col_index, (1,)).astype(jnp.int32)
    chip_arg = lax.dynamic_index_in_dim(jnp.asarray(table), col_index, 0, keepdims=False)

    def pair_gather(x):
        return lax.all_gather(x, "row", axis=0, axis_index_groups=core_pairs)

    def over_row(x):
        return lax.all_to_all(x, "row", 0, 0, tiled=True, axis_index_groups=same_core)

    def over_col(x):
        return lax.all_to_all(x, "col", 0, 0, tiled=True)

    factor_cols = lax.dynamic_slice_in_dim(inv_factor, col_index * diag_width, diag_width, 1)
    factor_gram = lax.optimization_barrier(
        lax.dot_general(
            factor_cols,
            inv_factor,
            (((0,), (0,)), ((), ())),
            precision=lax.Precision.HIGHEST,
            preferred_element_type=F32,
        )
    )

    by_panel = pl.pallas_call(
        lambda *refs: scale_kernel(panel_blocks, *refs),
        out_shape=jax.ShapeDtypeStruct((row_count, chunk_rows, half + TAG), BF16),
        in_specs=[SMEM, VMEM, VMEM, VMEM],
        out_specs=VMEM,
        scratch_shapes=[pltpu.VMEM((slot_count * chunk_rows, width), F32)],
        compiler_params=FETCHING,
    )(
        slot_blocks,
        front_rows.reshape(slot_count * chunk_rows, width),
        inv_factor,
        jnp.asarray(order, BF16),
    )
    piece = pl.pallas_call(
        place_kernel,
        out_shape=jax.ShapeDtypeStruct((panel_blocks, chunk_rows, half), BF16),
        in_specs=[VMEM],
        out_specs=VMEM,
        compiler_params=PARAMS,
    )(lax.all_to_all(by_panel, "row", 0, 0, tiled=True))

    route = [
        ((2 * p + k) * col_count + c, (2 * int(table[p, c]) + k) * col_count + p)
        for p in range(col_count)
        for k in range(2)
        for c in range(col_count)
    ]
    turned = lax.ppermute(piece, ("row", "col"), route)
    parts = pair_gather(over_row(jnp.broadcast_to(turned[None], (chip_count, *turned.shape))))

    sent = pl.pallas_call(
        product_kernel,
        out_shape=jax.ShapeDtypeStruct((col_count, share + chunk_rows, width), BF16),
        in_specs=[SMEM, SMEM, VMEM, VMEM, VMEM, VMEM],
        out_specs=VMEM,
        scratch_shapes=[
            pltpu.VMEM((panel_rows, width), F32),
            pltpu.VMEM((col_count, share + chunk_rows, width), F32),
        ],
        compiler_params=PARAMS,
    )(col_arg, chip_arg, ancestor_inv, parts, piece, jnp.asarray(order.T, BF16))
    column_total, pair_factor = pl.pallas_call(
        total_kernel,
        out_shape=(
            jax.ShapeDtypeStruct((share, width), F32),
            jax.ShapeDtypeStruct((2 * share, half), F32),
        ),
        in_specs=[SMEM, VMEM],
        out_specs=(VMEM, VMEM),
        compiler_params=PARAMS,
    )(col_arg, over_col(sent))

    gram_half = lax.dot_general(
        pair_factor,
        pair_gather(column_total).reshape(2 * share, width),
        (((0,), (0,)), ((), ())),
        precision=lax.Precision.HIGH,
        preferred_element_type=F32,
    ).astype(BF16)
    copies = pl.pallas_call(
        copies_kernel,
        out_shape=jax.ShapeDtypeStruct((chip_count, diag_width // 2, width), BF16),
        in_specs=[VMEM],
        out_specs=VMEM,
        compiler_params=PARAMS,
    )(over_col(gram_half.reshape(col_count, diag_width // 2, width)))
    gram_rows = jnp.sum(over_row(copies).astype(F32), axis=0)
    gram_block = pair_gather(gram_rows).reshape(diag_width, width)
    return (-column_total, factor_gram + gram_block)


def solution(mesh):
    in_specs = (P("row", "col", None), P("row"), P(), P("row", "col"))
    out_specs = (P(("row", "col"), None), P("col", None))
    return jax.shard_map(body, mesh=mesh, in_specs=in_specs, out_specs=out_specs, check_vma=False)
```

time: 128 us -> 127 us (level)
  blocking collectives: 39.5 us -> 76 us
  starting transfers between devices: 34.4 us -> 13.3 us
  waiting for transfers between devices: 41.9 us -> 26.5 us
  local copies, waits for them, and re-layouts: 4.33 us -> 1.5 us
  Pallas kernels: 3.99 us -> 5.56 us
    all_to_all x0 -> x1, blocking collectives: none -> 22.9 us  [body(): lax.all_to_all(by_panel, 'row', 0, 0, tiled=True)]
    all_to_all x3 -> x2, starting transfers between devices: 23.5 us -> 9.44 us  [over_row(): lax.all_to_all(x, 'row', 0, 0, tiled=True, axis_index_groups=same_core)]
    all_to_all x1 -> x2, blocking collectives: 23.4 us -> 37 us  [over_col(): return lax.all_to_all(x, 'col', 0, 0, tiled=True)]
    all_to_all x1 -> x0, waiting for transfers between devices: 12.8 us -> none  [over_col(): return lax.all_to_all(x, 'col', 0, 0, tiled=True)]
    all_to_all x3 -> x2, waiting for transfers between devices: 29.1 us -> 17.8 us  [over_row(): lax.all_to_all(x, 'row', 0, 0, tiled=True, axis_index_groups=same_core)]
    all_to_all x1 -> x0, starting transfers between devices: 10.2 us -> none  [over_col(): return lax.all_to_all(x, 'col', 0, 0, tiled=True)]
    ppermute x1, waiting for transfers between devices: 0.01 us -> 8.65 us  [body(): turned = lax.ppermute(piece, ('row', 'col'), route)]
    ppermute x1, starting transfers between devices: 0.66 us -> 3.88 us  [body(): turned = lax.ppermute(piece, ('row', 'col'), route)]
  transfers between devices with their start and end apart: 5 -> 3, of which waited for: 4 -> 3; matrix products, arithmetic and copies ran while one was open for 1% -> 2% of each run, Pallas kernels for 0% -> 0%
where the time goes in v4:
time: 127 us; the launch traced here: 126 us
  blocking collectives  76 us (60%)
  waiting for transfers between devices  26.5 us (21%)
  starting transfers between devices  13.3 us (10%)
  Pallas kernels  5.56 us (4%)
  local copies, waits for them, and re-layouts  1.5 us (1%)
  other arithmetic  1.31 us (1%)
    all_to_all x2, blocking collectives, over_col(): return lax.all_to_all(x, 'col', 0, 0, tiled=True)  37 us
    all_to_all x1, blocking collectives, body(): lax.all_to_all(by_panel, 'row', 0, 0, tiled=True)  22.9 us
    all_to_all x2, waiting for transfers between devices, over_row(): lax.all_to_all(x, 'row', 0, 0, tiled=True, axis_index_groups=same_core)  17.8 us
    all_gather x3, blocking collectives, pair_gather(): return lax.all_gather(x, 'row', axis=0, axis_index_groups=core_pairs)  16.1 us
    all_to_all x2, starting transfers between devices, over_row(): lax.all_to_all(x, 'row', 0, 0, tiled=True, axis_index_groups=same_core)  9.44 us
    ppermute x1, waiting for transfers between devices, body(): turned = lax.ppermute(piece, ('row', 'col'), route)  8.65 us
    ppermute x1, starting transfers between devices, body(): turned = lax.ppermute(piece, ('row', 'col'), route)  3.88 us
    pallas_call x1, Pallas kernels, body(): pl.pallas_call(lambda *refs: scale_kernel(panel_blocks, *refs), out_shape...  2.79 us
  transfers between devices with their start and end apart: 3, of which 3 were waited for; matrix products, arithmetic and copies ran while one was open for 2% of the time, Pallas kernels for 0%

profile of v4, /device:TPU:1, one launch (start us, length us, event | category | flops | bytes accessed | tf_op | source)
XLA Modules:
  0.0 126.0 jit_solution(11519786200076255243)
XLA Ops:
  0.6 2.8 %shard_map.86 = bf16[32,8,384]{2,1,0:T(8,128)(2,1)} custom-call(s32[16]{0:T(128)} %refs_0_.1, bf16[128,512]{1,0:T(8,128)(2,1)} %bitcast.11, f32[512,512]{1,0:T(8,128)} %refs_2_.1, bf16[512,512]{1,0:T(8,128)(2,1)} %constant.24.clone.refs_3_), custom_call_target="tpu_custom_call" | custom-call | tf_op jit(solution)/shard_map/pallas_call | solution.py:193
  3.4 22.9 %all_to_all.25.taken_ref = bf16[32,8,384]{2,1,0:T(8,128)(2,1)S(1)} all-to-all(bf16[32,8,384]{2,1,0:T(8,128)(2,1)} %shard_map.86), channel_id=1, replica_groups=mesh['row'=32,'col'=16] {'row'}, dimensions={0} | all-to-all | bytes 393216 | tf_op jit(solution)/shard_map/all_to_all | solution.py:212
  26.3 0.2 shard_map.87.piece_ref
  26.5 0.0 copy-start.1
  26.5 3.9 %collective-permute-start = (bf16[6,8,256]{2,1,0:T(8,128)(2,1)S(1)}, bf16[6,8,256]{2,1,0:T(8,128)(2,1)S(1)}, u32[]{:S(2)}, u32[]{:S(2)}) collective-permute-start(bf16[6,8,256]{2,1,0:T(8,128)(2,1)S(1)} %shard_map.87.piece_ref), channel_id=1, source_target_pairs={{0,416},{1,384},{2,128},{3,352},{4,160},{5,448},{6,192},{7,480},{8... | collective-permute-start | bytes 73736 | tf_op jit(solution)/shard_map/ppermute | solution.py:220
  30.4 8.6 %collective-permute-done = bf16[6,8,256]{2,1,0:T(8,128)(2,1)S(1)} collective-permute-done((bf16[6,8,256]{2,1,0:T(8,128)(2,1)S(1)}, bf16[6,8,256]{2,1,0:T(8,128)(2,1)S(1)}, u32[]{:S(2)}, u32[]{:S(2)}) %collective-permute-start) | collective-permute-done | bytes 24608 | tf_op jit(solution)/shard_map/ppermute | solution.py:220
  39.0 0.8 broadcast_in_dim.2
  39.8 4.8 %all-to-all-start.1 = ((bf16[16,6,8,256]{3,2,1,0:T(8,128)(2,1)}), bf16[16,6,8,256]{3,2,1,0:T(8,128)(2,1)S(1)}, u32[]{:S(2)}, u32[]{:S(2)}) async-start(bf16[16,6,8,256]{3,2,1,0:T(8,128)(2,1)} %broadcast_in_dim.2), calls=%async_computation.1 | async-start | bytes 786432 | tf_op jit(solution)/shard_map/all_to_all | solution.py:177
  44.6 0.7 dynamic-slice_bitcast_fusion.chip_ref
  45.3 10.0 %all-to-all-done.1 = bf16[16,6,8,256]{3,2,1,0:T(8,128)(2,1)S(1)} async-done(((bf16[16,6,8,256]{3,2,1,0:T(8,128)(2,1)}), bf16[16,6,8,256]{3,2,1,0:T(8,128)(2,1)S(1)}, u32[]{:S(2)}, u32[]{:S(2)}) %all-to-all-start.1) | async-done | bytes 393248 | tf_op jit(solution)/shard_map/all_to_all | solution.py:177
  55.3 6.8 %all-gather = bf16[32,6,8,256]{3,2,1,0:T(8,128)(2,1)S(1)} all-gather(bf16[16,6,8,256]{3,2,1,0:T(8,128)(2,1)S(1)} %all-to-all-done.1), channel_id=2, replica_groups={{0,16},{32,48},{64,80},{96,112},{128,144},{160,176},{192,208},{224,240}..., dimensions={0}, use_global_device_ids=true | all-gather | bytes 1179648 | tf_op jit(solution)/shard_map/all_gather | solution.py:174
  62.1 1.8 %shard_map.88 = bf16[16,32,512]{2,1,0:T(8,128)(2,1)S(1)} custom-call(s32[1]{0:T(128)} %bitcast.col_ref, s32[16]{0:T(128)S(1)} %dynamic-slice_bitcast_fusion.chip_ref, f32[384,768]{1,0:T(8,128)S(1)} %copy-done, bf16[2,16,6,8,256]{4,3,2,1,0:T(8,128)(2,1)S(1)} %bitcast.9, bf16[6,8,256]{2,1,0:T(8,128)(2,1)S(1)} %shard_map.87.piece_ref, ...), custom_call_target="tpu_custom_call" | custom-call | tf_op jit(solution)/shard_map/pallas_call | solution.py:223
  63.8 23.1 %all_to_all.26.arrived_ref = bf16[16,32,512]{2,1,0:T(8,128)(2,1)S(1)} all-to-all(bf16[16,32,512]{2,1,0:T(8,128)(2,1)S(1)} %shard_map.88), channel_id=1, replica_groups=mesh['row'=32,'col'=16] {'col'}, dimensions={0} | all-to-all | bytes 1048576 | tf_op jit(solution)/shard_map/all_to_all | solution.py:180
  86.9 0.1 shard_map.89
  87.0 4.2 %all-gather.1 = f32[48,512]{1,0:T(8,128)S(1)} all-gather(f32[24,512]{1,0:T(8,128)S(1)} %get-tuple-element.4), channel_id=3, replica_groups={{0,16},{32,48},{64,80},{96,112},{128,144},{160,176},{192,208},{224,240}..., dimensions={0}, use_global_device_ids=true | all-gather | bytes 147456 | tf_op jit(solution)/shard_map/all_gather | solution.py:174
  91.2 0.4 convolution_convert_fusion
  91.7 13.9 %all_to_all.27.arrived_ref = bf16[16,16,512]{2,1,0:T(8,128)(2,1)S(1)} all-to-all(bf16[16,16,512]{2,1,0:T(8,128)(2,1)S(1)} %bitcast.10), channel_id=1, replica_groups=mesh['row'=32,'col'=16] {'col'}, dimensions={0} | all-to-all | bytes 524288 | tf_op jit(solution)/shard_map/all_to_all | solution.py:180
  105.6 0.8 shard_map.90
  106.4 4.6 %all-to-all-start.4 = ((bf16[16,16,512]{2,1,0:T(8,128)(2,1)}), bf16[16,16,512]{2,1,0:T(8,128)(2,1)S(1)}, u32[]{:S(2)}, u32[]{:S(2)}) async-start(bf16[16,16,512]{2,1,0:T(8,128)(2,1)} %shard_map.90), calls=%async_computation.4 | async-start | bytes 524288 | tf_op jit(solution)/shard_map/all_to_all | solution.py:177
  111.0 0.7 fusion
  111.8 0.6 neg.3
  112.4 7.9 %all-to-all-done.4 = bf16[16,16,512]{2,1,0:T(8,128)(2,1)S(1)} async-done(((bf16[16,16,512]{2,1,0:T(8,128)(2,1)}), bf16[16,16,512]{2,1,0:T(8,128)(2,1)S(1)}, u32[]{:S(2)}, u32[]{:S(2)}) %all-to-all-start.4) | async-done | bytes 262176 | tf_op jit(solution)/shard_map/all_to_all | solution.py:177
  120.3 5.1 %all-gather.2 = f32[32,512]{1,0:T(8,128)S(1)} all-gather(f32[16,512]{1,0:T(8,128)S(1)} %convert_reduce_fusion), channel_id=4, replica_groups={{0,16},{32,48},{64,80},{96,112},{128,144},{160,176},{192,208},{224,240}..., dimensions={0}, use_global_device_ids=true | all-gather | bytes 98304 | tf_op jit(solution)/shard_map/all_gather | solution.py:174
  125.4 0.6 add.12
  (6 shorter events, 0.1 us)
Async XLA Ops:
  26.5 35.6 %copy-start = (f32[384,768]{1,0:T(8,128)S(1)}, f32[384,768]{1,0:T(8,128)}, u32[]{:S(2)}) copy-start(f32[384,768]{1,0:T(8,128)} %tile_ref.1) | copy-start | bytes 3538948
  26.5 35.6 %copy-start.1 = (bf16[512,512]{1,0:T(8,128)(2,1)S(1)}, bf16[512,512]{1,0:T(8,128)(2,1)}, u32[]{:S(2)}) copy-start(bf16[512,512]{1,0:T(8,128)(2,1)} %constant.25.clone.back_ref) | copy-start | bytes 1572868
  26.5 12.5 %collective-permute-start = (bf16[6,8,256]{2,1,0:T(8,128)(2,1)S(1)}, bf16[6,8,256]{2,1,0:T(8,128)(2,1)S(1)}, u32[]{:S(2)}, u32[]{:S(2)}) collective-permute-start(bf16[6,8,256]{2,1,0:T(8,128)(2,1)S(1)} %shard_map.87.piece_ref), channel_id=1, source_target_pairs={{0,416},{1,384},{2,128},{3,352},{4,160},{5,448},{6,192},{7,480},{8... | collective-permute-start | bytes 73736 | tf_op jit(solution)/shard_map/ppermute | solution.py:220
  39.8 15.5 %all-to-all-start.1 = ((bf16[16,6,8,256]{3,2,1,0:T(8,128)(2,1)}), bf16[16,6,8,256]{3,2,1,0:T(8,128)(2,1)S(1)}, u32[]{:S(2)}, u32[]{:S(2)}) async-start(bf16[16,6,8,256]{3,2,1,0:T(8,128)(2,1)} %broadcast_in_dim.2), calls=%async_computation.1 | async-start | bytes 786432 | tf_op jit(solution)/shard_map/all_to_all | solution.py:177
  87.0 24.0 %copy-start.2 = (f32[512,512]{1,0:T(8,128)S(1)}, f32[512,512]{1,0:T(8,128)}, u32[]{:S(2)}) copy-start(f32[512,512]{1,0:T(8,128)} %refs_2_.1) | copy-start | bytes 3145732
  106.4 13.9 %all-to-all-start.4 = ((bf16[16,16,512]{2,1,0:T(8,128)(2,1)}), bf16[16,16,512]{2,1,0:T(8,128)(2,1)S(1)}, u32[]{:S(2)}, u32[]{:S(2)}) async-start(bf16[16,16,512]{2,1,0:T(8,128)(2,1)} %shard_map.90), calls=%async_computation.4 | async-start | bytes 524288 | tf_op jit(solution)/shard_map/all_to_all | solution.py:177

commit v5 on v4

--- a/solution.py
+++ b/solution.py
@@ -105,9 +105,8 @@
             out_ref[n, :, lanes : lanes + TAG] = total.astype(BF16)
 
 
-def product_kernel(col_ref, chip_ref, tile_ref, parts_ref, piece_ref, back_ref, out_ref, panel_ref, sent_ref):
+def product_kernel(chip_ref, tile_ref, parts_ref, back_ref, out_ref, panel_ref):
     chunks, blocks, height, half = parts_ref.shape[1:]
-    share = sent_ref.shape[1] - height
     for c in range(chunks):
         for b in range(blocks):
             first = (b * chunks + c) * height
@@ -116,39 +115,18 @@
                 panel_ref[first : first + height, k * half : (k + 1) * half] = rows
     panel = dot(panel_ref[...].astype(BF16), back_ref[...]).astype(BF16)
     high, low = split(tile_ref[...])
-    sums = dot(high, panel) + dot(low, panel)
-    sent_ref[:, :share, :] = sums.reshape(chunks, share, 2 * half)
-    sent_ref[:, share:, :] = jnp.zeros((chunks, height, 2 * half), F32)
-    for b in range(blocks // 2):
-        target = (b * chunks + col_ref[0]) // (share // height)
-        for h in range(2):
-            rows = piece_ref[h * (blocks // 2) + b].astype(F32)
-            sent_ref[target, share:, h * half : (h + 1) * half] = rows
-    out_ref[...] = sent_ref[...].astype(BF16)
-
-
-def total_kernel(col_ref, arrived_ref, total_ref, factor_ref):
-    sources = arrived_ref.shape[0]
-    share, width = total_ref.shape
-    height = arrived_ref.shape[1] - share
-    total = arrived_ref[0].astype(F32)
-    for s in range(1, sources):
-        total = total + arrived_ref[s].astype(F32)
-    total_ref[...] = total[:share]
-    turns = share // height
-    for t in range(turns):
-        rows = arrived_ref[(turns * col_ref[0] + t) % sources].astype(F32)[share:]
-        for h in range(2):
-            first = h * share + t * height
-            factor_ref[first : first + height, :] = rows[:, h * width // 2 : (h + 1) * width // 2]
-
-
-def copies_kernel(arrived_ref, out_ref):
+    out_ref[...] = (dot(high, panel) + dot(low, panel)).astype(BF16)
+
+
+def total_kernel(arrived_ref, total_ref, copies_ref):
     total = arrived_ref[0].astype(F32)
     for s in range(1, arrived_ref.shape[0]):
         total = total + arrived_ref[s].astype(F32)
-    for copy in range(out_ref.shape[0]):
-        out_ref[copy] = total.astype(BF16)
+    first = copies_ref.shape[1]
+    rows = total[:first].astype(BF16)
+    for copy in range(copies_ref.shape[0]):
+        copies_ref[copy] = rows
+    total_ref[...] = total[first:]
 
 
 def body(front_rows, slot_blocks, inv_factor, ancestor_inv):
@@ -167,7 +145,6 @@
     core_pairs = [[2 * j, 2 * j + 1] for j in range(chip_count)]
     order = by_core(width, diag_width)
     table = short_routes(chip_count, col_count)
-    col_arg = jnp.reshape(col_index, (1,)).astype(jnp.int32)
     chip_arg = lax.dynamic_index_in_dim(jnp.asarray(table), col_index, 0, keepdims=False)
 
     def pair_gather(x):
@@ -218,44 +195,37 @@
         for c in range(col_count)
     ]
     turned = lax.ppermute(piece, ("row", "col"), route)
+    pair_factor = over_col(jnp.broadcast_to(piece[None], (col_count, *piece.shape)))
+    pair_factor = pair_factor.transpose(1, 0, 2, 3).reshape(2 * tile_rows, half)
     parts = pair_gather(over_row(jnp.broadcast_to(turned[None], (chip_count, *turned.shape))))
 
-    sent = pl.pallas_call(
+    partial_sums = pl.pallas_call(
         product_kernel,
-        out_shape=jax.ShapeDtypeStruct((col_count, share + chunk_rows, width), BF16),
-        in_specs=[SMEM, SMEM, VMEM, VMEM, VMEM, VMEM],
+        out_shape=jax.ShapeDtypeStruct((tile_rows, width), BF16),
+        in_specs=[SMEM, VMEM, VMEM, VMEM],
         out_specs=VMEM,
-        scratch_shapes=[
-            pltpu.VMEM((panel_rows, width), F32),
-            pltpu.VMEM((col_count, share + chunk_rows, width), F32),
+        scratch_shapes=[pltpu.VMEM((panel_rows, width), F32)],
+        compiler_params=PARAMS,
+    )(chip_arg, ancestor_inv, parts, jnp.asarray(order.T, BF16))
+    pair_sums = pair_gather(partial_sums).reshape(2 * tile_rows, width)
+    gram_half = dot(pair_factor, pair_sums, ((0,), (0,))).astype(BF16)
+    sent = jnp.concatenate(
+        [
+            gram_half.reshape(col_count, diag_width // 2, width),
+            partial_sums.reshape(col_count, share, width),
         ],
-        compiler_params=PARAMS,
-    )(col_arg, chip_arg, ancestor_inv, parts, piece, jnp.asarray(order.T, BF16))
-    column_total, pair_factor = pl.pallas_call(
+        1,
+    )
+    column_total, copies = pl.pallas_call(
         total_kernel,
         out_shape=(
             jax.ShapeDtypeStruct((share, width), F32),
-            jax.ShapeDtypeStruct((2 * share, half), F32),
+            jax.ShapeDtypeStruct((chip_count, diag_width // 2, width), BF16),
         ),
-        in_specs=[SMEM, VMEM],
+        in_specs=[VMEM],
         out_specs=(VMEM, VMEM),
         compiler_params=PARAMS,
-    )(col_arg, over_col(sent))
-
-    gram_half = lax.dot_general(
-        pair_factor,
-        pair_gather(column_total).reshape(2 * share, width),
-        (((0,), (0,)), ((), ())),
-        precision=lax.Precision.HIGH,
-        preferred_element_type=F32,
-    ).astype(BF16)
-    copies = pl.pallas_call(
-        copies_kernel,
-        out_shape=jax.ShapeDtypeStruct((chip_count, diag_width // 2, width), BF16),
-        in_specs=[VMEM],
-        out_specs=VMEM,
-        compiler_params=PARAMS,
-    )(over_col(gram_half.reshape(col_count, diag_width // 2, width)))
+    )(over_col(sent))
     gram_rows = jnp.sum(over_row(copies).astype(F32), axis=0)
     gram_block = pair_gather(gram_rows).reshape(diag_width, width)
     return (-column_total, factor_gram + gram_block)

time: 127 us -> 124 us (0.976)
  blocking collectives: 76 us -> 61.5 us
  starting transfers between devices: 13.3 us -> 25.7 us
    all_to_all x2 -> x1, blocking collectives: 37 us -> 24 us  [over_col(): return lax.all_to_all(x, 'col', 0, 0, tiled=True)]
    all_to_all x0 -> x1, starting transfers between devices: none -> 10.2 us  [over_col(): return lax.all_to_all(x, 'col', 0, 0, tiled=True)]
    all_to_all x2, starting transfers between devices: 9.44 us -> 11.1 us  [over_row(): lax.all_to_all(x, 'row', 0, 0, tiled=True, axis_index_groups=same_core)]
    all_gather x3, blocking collectives: 16.1 us -> 14.6 us  [pair_gather(): return lax.all_gather(x, 'row', axis=0, axis_index_groups=core_pairs)]
  transfers between devices with their start and end apart: 3 -> 4, of which waited for: 3 -> 3; matrix products, arithmetic and copies ran while one was open for 2% -> 2% of each run, Pallas kernels for 0% -> 0%
where the time goes in v5:
time: 124 us
  blocking collectives  61.5 us (50%)
  starting transfers between devices  25.7 us (21%)
  waiting for transfers between devices  25.4 us (20%)
  Pallas kernels  5.37 us (4%)
  local copies, waits for them, and re-layouts  2.4 us (2%)
  other arithmetic  1.35 us (1%)
    all_to_all x1, blocking collectives, over_col(): return lax.all_to_all(x, 'col', 0, 0, tiled=True)  24 us
    all_to_all x1, blocking collectives, body(): lax.all_to_all(by_panel, 'row', 0, 0, tiled=True)  22.9 us
    all_to_all x2, waiting for transfers between devices, over_row(): lax.all_to_all(x, 'row', 0, 0, tiled=True, axis_index_groups=same_core)  17.7 us
    all_gather x3, blocking collectives, pair_gather(): return lax.all_gather(x, 'row', axis=0, axis_index_groups=core_pairs)  14.6 us
    all_to_all x2, starting transfers between devices, over_row(): lax.all_to_all(x, 'row', 0, 0, tiled=True, axis_index_groups=same_core)  11.1 us
    all_to_all x1, starting transfers between devices, over_col(): return lax.all_to_all(x, 'col', 0, 0, tiled=True)  10.2 us
    ppermute x1, waiting for transfers between devices, body(): turned = lax.ppermute(piece, ('row', 'col'), route)  7.68 us
    ppermute x1, starting transfers between devices, body(): turned = lax.ppermute(piece, ('row', 'col'), route)  4.35 us
  transfers between devices with their start and end apart: 4, of which 3 were waited for; matrix products, arithmetic and copies ran while one was open for 2% of the time, Pallas kernels for 0%

profile of v5, /device:TPU:1, one launch (start us, length us, event | category | flops | bytes accessed | tf_op | source)
XLA Modules:
  0.0 123.6 jit_solution(6262530051150133267)
XLA Ops:
  0.6 2.7 %shard_map.86 = bf16[32,8,384]{2,1,0:T(8,128)(2,1)} custom-call(s32[16]{0:T(128)} %refs_0_.1, bf16[128,512]{1,0:T(8,128)(2,1)} %bitcast.16, f32[512,512]{1,0:T(8,128)} %refs_2_.1, bf16[512,512]{1,0:T(8,128)(2,1)} %constant.24.clone.refs_3_), custom_call_target="tpu_custom_call" | custom-call | tf_op jit(solution)/shard_map/pallas_call | solution.py:170
  3.4 22.9 %all_to_all.25.taken_ref = bf16[32,8,384]{2,1,0:T(8,128)(2,1)S(1)} all-to-all(bf16[32,8,384]{2,1,0:T(8,128)(2,1)} %shard_map.86), channel_id=1, replica_groups=mesh['row'=32,'col'=16] {'row'}, dimensions={0} | all-to-all | bytes 393216 | tf_op jit(solution)/shard_map/all_to_all | solution.py:189
  26.3 0.2 shard_map.87
  26.5 0.8 broadcast_in_dim.4
  27.2 10.2 %all-to-all-start.1 = ((bf16[16,6,8,256]{3,2,1,0:T(8,128)(2,1)}), bf16[16,6,8,256]{3,2,1,0:T(8,128)(2,1)S(1)}, u32[]{:S(2)}, u32[]{:S(2)}) async-start(bf16[16,6,8,256]{3,2,1,0:T(8,128)(2,1)} %broadcast_in_dim.4), calls=%async_computation.1 | async-start | bytes 786432 | tf_op jit(solution)/shard_map/all_to_all | solution.py:157
  37.4 4.3 %collective-permute-start = (bf16[6,8,256]{2,1,0:T(8,128)(2,1)S(1)}, bf16[6,8,256]{2,1,0:T(8,128)(2,1)S(1)}, u32[]{:S(2)}, u32[]{:S(2)}) collective-permute-start(bf16[6,8,256]{2,1,0:T(8,128)(2,1)S(1)} %shard_map.87), channel_id=1, source_target_pairs={{0,416},{1,384},{2,128},{3,352},{4,160},{5,448},{6,192},{7,480},{8... | collective-permute-start | bytes 73736 | tf_op jit(solution)/shard_map/ppermute | solution.py:197
  41.8 7.7 %collective-permute-done = bf16[6,8,256]{2,1,0:T(8,128)(2,1)S(1)} collective-permute-done((bf16[6,8,256]{2,1,0:T(8,128)(2,1)S(1)}, bf16[6,8,256]{2,1,0:T(8,128)(2,1)S(1)}, u32[]{:S(2)}, u32[]{:S(2)}) %collective-permute-start) | collective-permute-done | bytes 24608 | tf_op jit(solution)/shard_map/ppermute | solution.py:197
  49.5 0.8 broadcast_in_dim.5
  50.2 5.9 %all-to-all-start.2 = ((bf16[16,6,8,256]{3,2,1,0:T(8,128)(2,1)}), bf16[16,6,8,256]{3,2,1,0:T(8,128)(2,1)S(1)}, u32[]{:S(2)}, u32[]{:S(2)}) async-start(bf16[16,6,8,256]{3,2,1,0:T(8,128)(2,1)} %broadcast_in_dim.5), calls=%async_computation.2 | async-start | bytes 786432 | tf_op jit(solution)/shard_map/all_to_all | solution.py:154
  56.1 0.0 copy-start.1
  56.2 0.8 dynamic-slice_bitcast_fusion.chip_ref
  57.0 9.8 %all-to-all-done.2 = bf16[16,6,8,256]{3,2,1,0:T(8,128)(2,1)S(1)} async-done(((bf16[16,6,8,256]{3,2,1,0:T(8,128)(2,1)}), bf16[16,6,8,256]{3,2,1,0:T(8,128)(2,1)S(1)}, u32[]{:S(2)}, u32[]{:S(2)}) %all-to-all-start.2) | async-done | bytes 393248 | tf_op jit(solution)/shard_map/all_to_all | solution.py:154
  66.8 7.2 %all-gather = bf16[32,6,8,256]{3,2,1,0:T(8,128)(2,1)S(1)} all-gather(bf16[16,6,8,256]{3,2,1,0:T(8,128)(2,1)S(1)} %all-to-all-done.2), channel_id=2, replica_groups={{0,16},{32,48},{64,80},{96,112},{128,144},{160,176},{192,208},{224,240}..., dimensions={0}, use_global_device_ids=true | all-gather | bytes 1179648 | tf_op jit(solution)/shard_map/all_gather | solution.py:151
  74.0 1.7 %shard_map.88 = bf16[384,512]{1,0:T(8,128)(2,1)S(1)} custom-call(s32[16]{0:T(128)S(1)} %dynamic-slice_bitcast_fusion.chip_ref, f32[384,768]{1,0:T(8,128)S(1)} %copy-done, bf16[2,16,6,8,256]{4,3,2,1,0:T(8,128)(2,1)S(1)} %bitcast.13, bf16[512,512]{1,0:T(8,128)(2,1)S(1)} %copy-done.1), custom_call_target="tpu_custom_call" | custom-call | tf_op jit(solution)/shard_map/pallas_call | solution.py:202
  75.7 2.4 %all-gather.1 = bf16[768,512]{1,0:T(8,128)(2,1)S(1)} all-gather(bf16[384,512]{1,0:T(8,128)(2,1)S(1)} %shard_map.88), channel_id=3, replica_groups={{0,16},{32,48},{64,80},{96,112},{128,144},{160,176},{192,208},{224,240}..., dimensions={0}, use_global_device_ids=true | all-gather | bytes 1179648 | tf_op jit(solution)/shard_map/all_gather | solution.py:151
  78.1 0.4 convolution_convert_fusion
  78.6 24.0 %all_to_all.26.arrived_ref = bf16[16,40,512]{2,1,0:T(8,128)(2,1)S(1)} all-to-all(bf16[16,40,512]{2,1,0:T(8,128)(2,1)S(1)} %pad_maximum_fusion), channel_id=1, replica_groups=mesh['row'=32,'col'=16] {'col'}, dimensions={0} | all-to-all | bytes 1310720 | tf_op jit(solution)/shard_map/all_to_all | solution.py:157
  102.6 0.7 shard_map.89
  103.3 5.2 %all-to-all-start.4 = ((bf16[16,16,512]{2,1,0:T(8,128)(2,1)}), bf16[16,16,512]{2,1,0:T(8,128)(2,1)S(1)}, u32[]{:S(2)}, u32[]{:S(2)}) async-start(bf16[16,16,512]{2,1,0:T(8,128)(2,1)} %get-tuple-element.5), calls=%async_computation.4 | async-start | bytes 524288 | tf_op jit(solution)/shard_map/all_to_all | solution.py:154
  108.6 0.7 fusion
  109.4 0.6 neg.3
  110.0 7.9 %all-to-all-done.4 = bf16[16,16,512]{2,1,0:T(8,128)(2,1)S(1)} async-done(((bf16[16,16,512]{2,1,0:T(8,128)(2,1)}), bf16[16,16,512]{2,1,0:T(8,128)(2,1)S(1)}, u32[]{:S(2)}, u32[]{:S(2)}) %all-to-all-start.4) | async-done | bytes 262176 | tf_op jit(solution)/shard_map/all_to_all | solution.py:154
  117.9 5.0 %all-gather.2 = f32[32,512]{1,0:T(8,128)S(1)} all-gather(f32[16,512]{1,0:T(8,128)S(1)} %convert_reduce_fusion), channel_id=4, replica_groups={{0,16},{32,48},{64,80},{96,112},{128,144},{160,176},{192,208},{224,240}..., dimensions={0}, use_global_device_ids=true | all-gather | bytes 98304 | tf_op jit(solution)/shard_map/all_gather | solution.py:151
  122.9 0.6 add.12
  (9 shorter events, 0.1 us)
Async XLA Ops:
  27.2 22.2 %all-to-all-start.1 = ((bf16[16,6,8,256]{3,2,1,0:T(8,128)(2,1)}), bf16[16,6,8,256]{3,2,1,0:T(8,128)(2,1)S(1)}, u32[]{:S(2)}, u32[]{:S(2)}) async-start(bf16[16,6,8,256]{3,2,1,0:T(8,128)(2,1)} %broadcast_in_dim.4), calls=%async_computation.1 | async-start | bytes 786432 | tf_op jit(solution)/shard_map/all_to_all | solution.py:157
  37.4 12.0 %collective-permute-start = (bf16[6,8,256]{2,1,0:T(8,128)(2,1)S(1)}, bf16[6,8,256]{2,1,0:T(8,128)(2,1)S(1)}, u32[]{:S(2)}, u32[]{:S(2)}) collective-permute-start(bf16[6,8,256]{2,1,0:T(8,128)(2,1)S(1)} %shard_map.87), channel_id=1, source_target_pairs={{0,416},{1,384},{2,128},{3,352},{4,160},{5,448},{6,192},{7,480},{8... | collective-permute-start | bytes 73736 | tf_op jit(solution)/shard_map/ppermute | solution.py:197
  50.2 16.6 %all-to-all-start.2 = ((bf16[16,6,8,256]{3,2,1,0:T(8,128)(2,1)}), bf16[16,6,8,256]{3,2,1,0:T(8,128)(2,1)S(1)}, u32[]{:S(2)}, u32[]{:S(2)}) async-start(bf16[16,6,8,256]{3,2,1,0:T(8,128)(2,1)} %broadcast_in_dim.5), calls=%async_computation.2 | async-start | bytes 786432 | tf_op jit(solution)/shard_map/all_to_all | solution.py:154
  56.1 17.9 %copy-start = (f32[384,768]{1,0:T(8,128)S(1)}, f32[384,768]{1,0:T(8,128)}, u32[]{:S(2)}) copy-start(f32[384,768]{1,0:T(8,128)} %tile_ref.1) | copy-start | bytes 3538948
  56.1 17.9 %copy-start.1 = (bf16[512,512]{1,0:T(8,128)(2,1)S(1)}, bf16[512,512]{1,0:T(8,128)(2,1)}, u32[]{:S(2)}) copy-start(bf16[512,512]{1,0:T(8,128)(2,1)} %constant.25.clone.back_ref) | copy-start | bytes 1572868
  78.5 30.0 %copy-start.2 = (f32[512,512]{1,0:T(8,128)S(1)}, f32[512,512]{1,0:T(8,128)}, u32[]{:S(2)}) copy-start(f32[512,512]{1,0:T(8,128)} %refs_2_.1) | copy-start | bytes 3145732
  103.3 14.5 %all-to-all-start.4 = ((bf16[16,16,512]{2,1,0:T(8,128)(2,1)}), bf16[16,16,512]{2,1,0:T(8,128)(2,1)S(1)}, u32[]{:S(2)}, u32[]{:S(2)}) async-start(bf16[16,16,512]{2,1,0:T(8,128)(2,1)} %get-tuple-element.5), calls=%async_computation.4 | async-start | bytes 524288 | tf_op jit(solution)/shard_map/all_to_all | solution.py:154

commit v6 on v5

--- a/solution.py
+++ b/solution.py
@@ -24,15 +24,6 @@
 def split(x):
     high = x.astype(BF16)
     return high, (x - high.astype(F32)).astype(BF16)
-
-
-def by_core(width, group):
-    part = group // 2
-    column = np.arange(width)
-    target = (column % group) // part * (width // 2) + column // group * part + column % part
-    matrix = np.zeros((width, width), np.float32)
-    matrix[column, target] = 1.0
-    return matrix
 
 
 def chip_position(chip, col, chip_count):
@@ -70,12 +61,11 @@
     return table
 
 
-def scale_kernel(panel_blocks, slots_ref, rows_ref, factor_ref, order_ref, out_ref, scaled_ref):
+def scale_kernel(panel_blocks, slots_ref, rows_ref, factor_ref, out_ref, scaled_ref):
     half = factor_ref.shape[1] // 2
     high, low = split(factor_ref[...])
     rows = rows_ref[...]
-    scaled = (dot(rows, high) + dot(rows, low)).astype(BF16)
-    scaled_ref[...] = dot(scaled, order_ref[...])
+    scaled_ref[...] = dot(rows, high) + dot(rows, low)
     out_ref[...] = jnp.zeros_like(out_ref)
     slot_count = slots_ref.shape[0]
     height = rows_ref.shape[0] // slot_count
@@ -105,17 +95,27 @@
             out_ref[n, :, lanes : lanes + TAG] = total.astype(BF16)
 
 
-def product_kernel(chip_ref, tile_ref, parts_ref, back_ref, out_ref, panel_ref):
-    chunks, blocks, height, half = parts_ref.shape[1:]
+def product_kernel(core_ref, chip_ref, own_ref, other_ref, parts_ref, factor_ref, out_ref, panel_ref, sums_ref, sent_ref):
+    chunks, blocks, height, half = parts_ref.shape
     for c in range(chunks):
         for b in range(blocks):
             first = (b * chunks + c) * height
-            for k in range(2):
-                rows = parts_ref[k, chip_ref[c], b].astype(F32)
-                panel_ref[first : first + height, k * half : (k + 1) * half] = rows
-    panel = dot(panel_ref[...].astype(BF16), back_ref[...]).astype(BF16)
-    high, low = split(tile_ref[...])
-    out_ref[...] = (dot(high, panel) + dot(low, panel)).astype(BF16)
+            panel_ref[first : first + height, :] = parts_ref[chip_ref[c], b].astype(F32)
+    panel = panel_ref[...].astype(BF16)
+    tile_rows = own_ref.shape[0]
+    for k, ref in ((core_ref[0], own_ref), (1 - core_ref[0], other_ref)):
+        high, low = split(ref[...])
+        at = pl.ds(pl.multiple_of(k * tile_rows, tile_rows), tile_rows)
+        sums_ref[at, :] = dot(high, panel) + dot(low, panel)
+    sums = sums_ref[...]
+    gram = dot(factor_ref[...], sums.astype(BF16))
+    rows = gram.shape[0] // chunks
+    share = sums.shape[0] // 2 // chunks
+    sent_ref[:, :rows, :] = gram.reshape(chunks, rows, half)
+    sums = sums.reshape(2, chunks, share, half)
+    for k in range(2):
+        sent_ref[:, rows + k * share : rows + (k + 1) * share, :] = sums[k]
+    out_ref[...] = sent_ref[...].astype(BF16)
 
 
 def total_kernel(arrived_ref, total_ref, copies_ref):
@@ -134,6 +134,8 @@
     row_count = lax.axis_size("row")
     chip_count = row_count // 2
     col_index = lax.axis_index("col")
+    core = lax.axis_index("row") % 2
+    core_arg = jnp.reshape(core, (1,)).astype(jnp.int32)
     slot_count, chunk_rows, width = front_rows.shape
     half = width // 2
     tile_rows, panel_rows = ancestor_inv.shape
@@ -142,8 +144,8 @@
     share = tile_rows // col_count
     diag_width = width // col_count
     same_core = [[2 * j + k for j in range(chip_count)] for k in range(2)]
+    core_swap = [(i, i ^ 1) for i in range(row_count)]
     core_pairs = [[2 * j, 2 * j + 1] for j in range(chip_count)]
-    order = by_core(width, diag_width)
     table = short_routes(chip_count, col_count)
     chip_arg = lax.dynamic_index_in_dim(jnp.asarray(table), col_index, 0, keepdims=False)
 
@@ -170,7 +172,7 @@
     by_panel = pl.pallas_call(
         lambda *refs: scale_kernel(panel_blocks, *refs),
         out_shape=jax.ShapeDtypeStruct((row_count, chunk_rows, half + TAG), BF16),
-        in_specs=[SMEM, VMEM, VMEM, VMEM],
+        in_specs=[SMEM, VMEM, VMEM],
         out_specs=VMEM,
         scratch_shapes=[pltpu.VMEM((slot_count * chunk_rows, width), F32)],
         compiler_params=FETCHING,
@@ -178,15 +180,15 @@
         slot_blocks,
         front_rows.reshape(slot_count * chunk_rows, width),
         inv_factor,
-        jnp.asarray(order, BF16),
     )
+    taken = lax.all_to_all(by_panel, "row", 0, 0, tiled=True)
     piece = pl.pallas_call(
         place_kernel,
         out_shape=jax.ShapeDtypeStruct((panel_blocks, chunk_rows, half), BF16),
         in_specs=[VMEM],
         out_specs=VMEM,
         compiler_params=PARAMS,
-    )(lax.all_to_all(by_panel, "row", 0, 0, tiled=True))
+    )(taken)
 
     route = [
         ((2 * p + k) * col_count + c, (2 * int(table[p, c]) + k) * col_count + p)
@@ -195,40 +197,42 @@
         for c in range(col_count)
     ]
     turned = lax.ppermute(piece, ("row", "col"), route)
-    pair_factor = over_col(jnp.broadcast_to(piece[None], (col_count, *piece.shape)))
-    pair_factor = pair_factor.transpose(1, 0, 2, 3).reshape(2 * tile_rows, half)
-    parts = pair_gather(over_row(jnp.broadcast_to(turned[None], (chip_count, *turned.shape))))
-
-    partial_sums = pl.pallas_call(
+    turned, own_tile = lax.optimization_barrier((turned, ancestor_inv))
+    other_tile = lax.ppermute(own_tile, "row", core_swap)
+    factor = over_col(jnp.broadcast_to(piece[None], (col_count, *piece.shape)))
+    tile_factor = pair_gather(factor)
+    tile_factor = tile_factor.transpose(0, 4, 2, 1, 3).reshape(width, 2 * tile_rows)
+    parts = over_row(jnp.broadcast_to(turned[None], (chip_count, *turned.shape)))
+
+    sent = (col_count, diag_width + 2 * share, half)
+    sent = pl.pallas_call(
         product_kernel,
-        out_shape=jax.ShapeDtypeStruct((tile_rows, width), BF16),
-        in_specs=[SMEM, VMEM, VMEM, VMEM],
+        out_shape=jax.ShapeDtypeStruct(sent, BF16),
+        in_specs=[SMEM, SMEM, VMEM, VMEM, VMEM, VMEM],
         out_specs=VMEM,
-        scratch_shapes=[pltpu.VMEM((panel_rows, width), F32)],
+        scratch_shapes=[
+            pltpu.VMEM((panel_rows, half), F32),
+            pltpu.VMEM((2 * tile_rows, half), F32),
+            pltpu.VMEM(sent, F32),
+        ],
         compiler_params=PARAMS,
-    )(chip_arg, ancestor_inv, parts, jnp.asarray(order.T, BF16))
-    pair_sums = pair_gather(partial_sums).reshape(2 * tile_rows, width)
-    gram_half = dot(pair_factor, pair_sums, ((0,), (0,))).astype(BF16)
-    sent = jnp.concatenate(
-        [
-            gram_half.reshape(col_count, diag_width // 2, width),
-            partial_sums.reshape(col_count, share, width),
-        ],
-        1,
-    )
-    column_total, copies = pl.pallas_call(
+    )(core_arg, chip_arg, ancestor_inv, other_tile, parts, tile_factor)
+    totals, copies = pl.pallas_call(
         total_kernel,
         out_shape=(
-            jax.ShapeDtypeStruct((share, width), F32),
-            jax.ShapeDtypeStruct((chip_count, diag_width // 2, width), BF16),
+            jax.ShapeDtypeStruct((2 * share, half), F32),
+            jax.ShapeDtypeStruct((chip_count, diag_width, half), BF16),
         ),
         in_specs=[VMEM],
         out_specs=(VMEM, VMEM),
         compiler_params=PARAMS,
     )(over_col(sent))
-    gram_rows = jnp.sum(over_row(copies).astype(F32), axis=0)
-    gram_block = pair_gather(gram_rows).reshape(diag_width, width)
-    return (-column_total, factor_gram + gram_block)
+    halves = pair_gather(totals).reshape(2, 2, share, half)
+    product = lax.dynamic_index_in_dim(halves, core, 1, keepdims=False)
+    product = jnp.concatenate([product[0], product[1]], 1)
+    gram_rows = pair_gather(jnp.sum(over_row(copies).astype(F32), axis=0))
+    gram_rows = jnp.concatenate([gram_rows[0], gram_rows[1]], 1)
+    return (-product, factor_gram + gram_rows)
 
 
 def solution(mesh):

time: 124 us -> 122 us (0.984)
  blocking collectives: 61.5 us -> 36.1 us
  starting transfers between devices: 25.7 us -> 36 us
  waiting for transfers between devices: 25.4 us -> 34.6 us
  local copies, waits for them, and re-layouts: 2.4 us -> 5.8 us
    all_to_all x2 -> x1, blocking collectives: 47 us -> 23.1 us  [body(): taken = lax.all_to_all(by_panel, 'row', 0, 0, tiled=True)]
    all_to_all x1 -> x2, waiting for transfers between devices: 0.01 us -> 17.1 us  [over_col(): return lax.all_to_all(x, 'col', 0, 0, tiled=True)]
    all_to_all x2, waiting for transfers between devices: 17.7 us -> 9.82 us  [over_row(): lax.all_to_all(x, 'row', 0, 0, tiled=True, axis_index_groups=same_core)]
    ppermute x0 -> x1, starting transfers between devices: none -> 5.98 us  [body(): other_tile = lax.ppermute(own_tile, 'row', core_swap)]
    all_to_all x1 -> x2, starting transfers between devices: 10.2 us -> 14 us  [over_col(): return lax.all_to_all(x, 'col', 0, 0, tiled=True)]
    all_gather x3, blocking collectives: 14.6 us -> 12.9 us  [pair_gather(): return lax.all_gather(x, 'row', axis=0, axis_index_groups=core_pairs)]
    reshape x0 -> x1, local copies, waits for them, and re-layouts: none -> 1.4 us  [body(): tile_factor.transpose(0, 4, 2, 1, 3).reshape(width, 2 * tile_rows)]
  transfers between devices with their start and end apart: 4 -> 6, of which waited for: 3 -> 4; matrix products, arithmetic and copies ran while one was open for 2% -> 5% of each run, Pallas kernels for 0% -> 0%
where the time goes in v6:
time: 122 us; the launch traced here: 121 us
  blocking collectives  36.1 us (30%)
  starting transfers between devices  36 us (30%)
  waiting for transfers between devices  34.6 us (28%)
  Pallas kernels  6.11 us (5%)
  local copies, waits for them, and re-layouts  5.8 us (5%)
  other arithmetic  1.31 us (1%)
    all_to_all x1, blocking collectives, body(): taken = lax.all_to_all(by_panel, 'row', 0, 0, tiled=True)  23.1 us
    all_to_all x2, waiting for transfers between devices, over_col(): return lax.all_to_all(x, 'col', 0, 0, tiled=True)  17.1 us
    all_to_all x2, starting transfers between devices, over_col(): return lax.all_to_all(x, 'col', 0, 0, tiled=True)  14 us
    all_gather x3, blocking collectives, pair_gather(): return lax.all_gather(x, 'row', axis=0, axis_index_groups=core_pairs)  12.9 us
    all_to_all x2, starting transfers between devices, over_row(): lax.all_to_all(x, 'row', 0, 0, tiled=True, axis_index_groups=same_core)  11.7 us
    all_to_all x2, waiting for transfers between devices, over_row(): lax.all_to_all(x, 'row', 0, 0, tiled=True, axis_index_groups=same_core)  9.82 us
    ppermute x1, waiting for transfers between devices, body(): turned = lax.ppermute(piece, ('row', 'col'), route)  7.68 us
    ppermute x1, starting transfers between devices, body(): other_tile = lax.ppermute(own_tile, 'row', core_swap)  5.98 us
  transfers between devices with their start and end apart: 6, of which 4 were waited for; matrix products, arithmetic and copies ran while one was open for 5% of the time, Pallas kernels for 0%

profile of v6, /device:TPU:1, one launch (start us, length us, event | category | flops | bytes accessed | tf_op | source)
XLA Modules:
  0.0 121.3 jit_solution(610079987728497739)
XLA Ops:
  0.6 2.5 %shard_map.68 = bf16[32,8,384]{2,1,0:T(8,128)(2,1)} custom-call(s32[16]{0:T(128)} %refs_0_.1, bf16[128,512]{1,0:T(8,128)(2,1)} %bitcast.22, f32[512,512]{1,0:T(8,128)} %refs_2_.1), custom_call_target="tpu_custom_call" | custom-call | tf_op jit(solution)/shard_map/pallas_call | solution.py:172
  3.1 23.1 %all_to_all.25.taken_ref = bf16[32,8,384]{2,1,0:T(8,128)(2,1)S(1)} all-to-all(bf16[32,8,384]{2,1,0:T(8,128)(2,1)} %shard_map.68), channel_id=1, replica_groups=mesh['row'=32,'col'=16] {'row'}, dimensions={0} | all-to-all | bytes 393216 | tf_op jit(solution)/shard_map/all_to_all | solution.py:184
  26.4 0.8 broadcast_in_dim.5
  27.2 10.2 %all-to-all-start.2 = ((bf16[16,6,8,256]{3,2,1,0:T(8,128)(2,1)}), bf16[16,6,8,256]{3,2,1,0:T(8,128)(2,1)S(1)}, u32[]{:S(2)}, u32[]{:S(2)}) async-start(bf16[16,6,8,256]{3,2,1,0:T(8,128)(2,1)} %broadcast_in_dim.5), calls=%async_computation.2 | async-start | bytes 786432 | tf_op jit(solution)/shard_map/all_to_all | solution.py:159
  37.4 4.3 %collective-permute-start = (bf16[6,8,256]{2,1,0:T(8,128)(2,1)S(1)}, bf16[6,8,256]{2,1,0:T(8,128)(2,1)S(1)}, u32[]{:S(2)}, u32[]{:S(2)}) collective-permute-start(bf16[6,8,256]{2,1,0:T(8,128)(2,1)S(1)} %shard_map.69), channel_id=1, source_target_pairs={{0,416},{1,384},{2,128},{3,352},{4,160},{5,448},{6,192},{7,480},{8... | collective-permute-start | bytes 73736 | tf_op jit(solution)/shard_map/ppermute | solution.py:199
  41.7 7.7 %collective-permute-done = bf16[6,8,256]{2,1,0:T(8,128)(2,1)S(1)} collective-permute-done((bf16[6,8,256]{2,1,0:T(8,128)(2,1)S(1)}, bf16[6,8,256]{2,1,0:T(8,128)(2,1)S(1)}, u32[]{:S(2)}, u32[]{:S(2)}) %collective-permute-start) | collective-permute-done | bytes 24608 | tf_op jit(solution)/shard_map/ppermute | solution.py:199
  49.4 6.0 %collective-permute-start.1 = (f32[384,768]{1,0:T(8,128)S(1)}, f32[384,768]{1,0:T(8,128)S(1)}, u32[]{:S(2)}, u32[]{:S(2)}) collective-permute-start(f32[384,768]{1,0:T(8,128)S(1)} %copy-done), channel_id=1, source_target_pairs={{0,16},{16,0},{32,48},{48,32},{64,80},{80,64},{96,112},{112,96},{1... | collective-permute-start | bytes 3538952 | tf_op jit(solution)/shard_map/ppermute | solution.py:201
  55.4 0.8 broadcast_in_dim.4
  56.2 4.0 %all-to-all-start.1 = ((bf16[16,6,8,256]{3,2,1,0:T(8,128)(2,1)}), bf16[16,6,8,256]{3,2,1,0:T(8,128)(2,1)S(1)}, u32[]{:S(2)}, u32[]{:S(2)}) async-start(bf16[16,6,8,256]{3,2,1,0:T(8,128)(2,1)} %broadcast_in_dim.4), calls=%async_computation.1 | async-start | bytes 786432 | tf_op jit(solution)/shard_map/all_to_all | solution.py:156
  60.2 0.7 fusion.3.chip_ref
  60.9 2.4 %all-gather = bf16[32,6,8,256]{3,2,1,0:T(8,128)(2,1)S(1)} all-gather(bf16[16,6,8,256]{3,2,1,0:T(8,128)(2,1)S(1)} %all-to-all-done.2), channel_id=2, replica_groups={{0,16},{32,48},{64,80},{96,112},{128,144},{160,176},{192,208},{224,240}..., dimensions={0}, use_global_device_ids=true | all-gather | bytes 1179648 | tf_op jit(solution)/shard_map/all_gather | solution.py:153
  63.3 1.1 copy.9
  64.3 1.1 copy.11
  65.4 1.4 %copy.10.factor_ref = bf16[512,768]{1,0:T(8,128)(2,1)S(1)} copy(bf16[512,768]{0,1:T(8,128)(2,1)} %bitcast.20) | data formatting | bytes 1572864 | tf_op jit(solution)/shard_map/reshape | solution.py:204
  66.8 6.6 %all-to-all-done.1.parts_ref = bf16[16,6,8,256]{3,2,1,0:T(8,128)(2,1)S(1)} async-done(((bf16[16,6,8,256]{3,2,1,0:T(8,128)(2,1)}), bf16[16,6,8,256]{3,2,1,0:T(8,128)(2,1)S(1)}, u32[]{:S(2)}, u32[]{:S(2)}) %all-to-all-start.1) | async-done | bytes 393248 | tf_op jit(solution)/shard_map/all_to_all | solution.py:156
  73.4 2.7 %shard_map.70 = bf16[16,80,256]{2,1,0:T(8,128)(2,1)} custom-call(s32[1]{0:T(128)} %bitcast.core_ref, s32[16]{0:T(128)S(1)} %fusion.3.chip_ref, f32[384,768]{1,0:T(8,128)S(1)} %copy-done, f32[384,768]{1,0:T(8,128)S(1)} %collective-permute-done.1.other_ref, bf16[16,6,8,256]{3,2,1,0:T(8,128)(2,1)S(1)} %all-to-all-done.1.parts_ref, ...), custom_call_target="tpu_custom_call" | custom-call | tf_op jit(solution)/shard_map/pallas_call | solution.py:208
  76.1 3.8 %all-to-all-start.3 = ((bf16[16,80,256]{2,1,0:T(8,128)(2,1)}), bf16[16,80,256]{2,1,0:T(8,128)(2,1)S(1)}, u32[]{:S(2)}, u32[]{:S(2)}) async-start(bf16[16,80,256]{2,1,0:T(8,128)(2,1)} %shard_map.70), calls=%async_computation.3 | async-start | bytes 1310720 | tf_op jit(solution)/shard_map/all_to_all | solution.py:159
  79.9 17.1 %all-to-all-done.3.arrived_ref = bf16[16,80,256]{2,1,0:T(8,128)(2,1)S(1)} async-done(((bf16[16,80,256]{2,1,0:T(8,128)(2,1)}), bf16[16,80,256]{2,1,0:T(8,128)(2,1)S(1)}, u32[]{:S(2)}, u32[]{:S(2)}) %all-to-all-start.3) | async-done | bytes 655392 | tf_op jit(solution)/shard_map/all_to_all | solution.py:159
  97.0 0.8 shard_map.71
  97.8 7.7 %all-to-all-start.4 = ((bf16[16,32,256]{2,1,0:T(8,128)(2,1)}), bf16[16,32,256]{2,1,0:T(8,128)(2,1)S(1)}, u32[]{:S(2)}, u32[]{:S(2)}) async-start(bf16[16,32,256]{2,1,0:T(8,128)(2,1)} %get-tuple-element.9), calls=%async_computation.4 | async-start | bytes 524288 | tf_op jit(solution)/shard_map/all_to_all | solution.py:156
  105.5 0.7 fusion
  106.2 4.7 %all-gather.1 = f32[96,256]{1,0:T(8,128)S(1)} all-gather(f32[48,256]{1,0:T(8,128)S(1)} %get-tuple-element.8), channel_id=3, replica_groups={{0,16},{32,48},{64,80},{96,112},{128,144},{160,176},{192,208},{224,240}..., dimensions={0}, use_global_device_ids=true | all-gather | bytes 147456 | tf_op jit(solution)/shard_map/all_gather | solution.py:153
  111.5 3.2 %all-to-all-done.4 = bf16[16,32,256]{2,1,0:T(8,128)(2,1)S(1)} async-done(((bf16[16,32,256]{2,1,0:T(8,128)(2,1)}), bf16[16,32,256]{2,1,0:T(8,128)(2,1)S(1)}, u32[]{:S(2)}, u32[]{:S(2)}) %all-to-all-start.4) | async-done | bytes 262176 | tf_op jit(solution)/shard_map/all_to_all | solution.py:156
  114.8 5.9 %all-gather.2 = f32[64,256]{1,0:T(8,128)S(1)} all-gather(f32[32,256]{1,0:T(8,128)S(1)} %convert_reduce_fusion), channel_id=4, replica_groups={{0,16},{32,48},{64,80},{96,112},{128,144},{160,176},{192,208},{224,240}..., dimensions={0}, use_global_device_ids=true | all-gather | bytes 98304 | tf_op jit(solution)/shard_map/all_gather | solution.py:153
  (12 shorter events, 1.5 us)
Async XLA Ops:
  3.1 46.3 %copy-start = (f32[384,768]{1,0:T(8,128)S(1)}, f32[384,768]{1,0:T(8,128)}, u32[]{:S(2)}) copy-start(f32[384,768]{1,0:T(8,128)} %own_ref.1) | copy-start | bytes 3538948
  27.2 28.2 %all-to-all-start.2 = ((bf16[16,6,8,256]{3,2,1,0:T(8,128)(2,1)}), bf16[16,6,8,256]{3,2,1,0:T(8,128)(2,1)S(1)}, u32[]{:S(2)}, u32[]{:S(2)}) async-start(bf16[16,6,8,256]{3,2,1,0:T(8,128)(2,1)} %broadcast_in_dim.5), calls=%async_computation.2 | async-start | bytes 786432 | tf_op jit(solution)/shard_map/all_to_all | solution.py:159
  37.4 12.0 %collective-permute-start = (bf16[6,8,256]{2,1,0:T(8,128)(2,1)S(1)}, bf16[6,8,256]{2,1,0:T(8,128)(2,1)S(1)}, u32[]{:S(2)}, u32[]{:S(2)}) collective-permute-start(bf16[6,8,256]{2,1,0:T(8,128)(2,1)S(1)} %shard_map.69), channel_id=1, source_target_pairs={{0,416},{1,384},{2,128},{3,352},{4,160},{5,448},{6,192},{7,480},{8... | collective-permute-start | bytes 73736 | tf_op jit(solution)/shard_map/ppermute | solution.py:199
  49.4 24.0 %collective-permute-start.1 = (f32[384,768]{1,0:T(8,128)S(1)}, f32[384,768]{1,0:T(8,128)S(1)}, u32[]{:S(2)}, u32[]{:S(2)}) collective-permute-start(f32[384,768]{1,0:T(8,128)S(1)} %copy-done), channel_id=1, source_target_pairs={{0,16},{16,0},{32,48},{48,32},{64,80},{80,64},{96,112},{112,96},{1... | collective-permute-start | bytes 3538952 | tf_op jit(solution)/shard_map/ppermute | solution.py:201
  56.2 17.3 %all-to-all-start.1 = ((bf16[16,6,8,256]{3,2,1,0:T(8,128)(2,1)}), bf16[16,6,8,256]{3,2,1,0:T(8,128)(2,1)S(1)}, u32[]{:S(2)}, u32[]{:S(2)}) async-start(bf16[16,6,8,256]{3,2,1,0:T(8,128)(2,1)} %broadcast_in_dim.4), calls=%async_computation.1 | async-start | bytes 786432 | tf_op jit(solution)/shard_map/all_to_all | solution.py:156
  76.1 29.3 %copy-start.1 = (f32[512,512]{1,0:T(8,128)S(1)}, f32[512,512]{1,0:T(8,128)}, u32[]{:S(2)}) copy-start(f32[512,512]{1,0:T(8,128)} %refs_2_.1) | copy-start | bytes 3145732
  76.1 20.9 %all-to-all-start.3 = ((bf16[16,80,256]{2,1,0:T(8,128)(2,1)}), bf16[16,80,256]{2,1,0:T(8,128)(2,1)S(1)}, u32[]{:S(2)}, u32[]{:S(2)}) async-start(bf16[16,80,256]{2,1,0:T(8,128)(2,1)} %shard_map.70), calls=%async_computation.3 | async-start | bytes 1310720 | tf_op jit(solution)/shard_map/all_to_all | solution.py:159
  97.8 16.9 %all-to-all-start.4 = ((bf16[16,32,256]{2,1,0:T(8,128)(2,1)}), bf16[16,32,256]{2,1,0:T(8,128)(2,1)S(1)}, u32[]{:S(2)}, u32[]{:S(2)}) async-start(bf16[16,32,256]{2,1,0:T(8,128)(2,1)} %get-tuple-element.9), calls=%async_computation.4 | async-start | bytes 524288 | tf_op jit(solution)/shard_map/all_to_all | solution.py:156

commit v7 on v6

--- a/solution.py
+++ b/solution.py
@@ -95,19 +95,15 @@
             out_ref[n, :, lanes : lanes + TAG] = total.astype(BF16)
 
 
-def product_kernel(core_ref, chip_ref, own_ref, other_ref, parts_ref, factor_ref, out_ref, panel_ref, sums_ref, sent_ref):
+def product_kernel(chip_ref, tiles_ref, parts_ref, factor_ref, out_ref, panel_ref, sent_ref):
     chunks, blocks, height, half = parts_ref.shape
     for c in range(chunks):
         for b in range(blocks):
             first = (b * chunks + c) * height
             panel_ref[first : first + height, :] = parts_ref[chip_ref[c], b].astype(F32)
     panel = panel_ref[...].astype(BF16)
-    tile_rows = own_ref.shape[0]
-    for k, ref in ((core_ref[0], own_ref), (1 - core_ref[0], other_ref)):
-        high, low = split(ref[...])
-        at = pl.ds(pl.multiple_of(k * tile_rows, tile_rows), tile_rows)
-        sums_ref[at, :] = dot(high, panel) + dot(low, panel)
-    sums = sums_ref[...]
+    high, low = split(tiles_ref[...])
+    sums = dot(high, panel) + dot(low, panel)
     gram = dot(factor_ref[...], sums.astype(BF16))
     rows = gram.shape[0] // chunks
     share = sums.shape[0] // 2 // chunks
@@ -135,7 +131,6 @@
     chip_count = row_count // 2
     col_index = lax.axis_index("col")
     core = lax.axis_index("row") % 2
-    core_arg = jnp.reshape(core, (1,)).astype(jnp.int32)
     slot_count, chunk_rows, width = front_rows.shape
     half = width // 2
     tile_rows, panel_rows = ancestor_inv.shape
@@ -144,7 +139,6 @@
     share = tile_rows // col_count
     diag_width = width // col_count
     same_core = [[2 * j + k for j in range(chip_count)] for k in range(2)]
-    core_swap = [(i, i ^ 1) for i in range(row_count)]
     core_pairs = [[2 * j, 2 * j + 1] for j in range(chip_count)]
     table = short_routes(chip_count, col_count)
     chip_arg = lax.dynamic_index_in_dim(jnp.asarray(table), col_index, 0, keepdims=False)
@@ -168,6 +162,8 @@
             preferred_element_type=F32,
         )
     )
+
+    tiles = pair_gather(ancestor_inv).reshape(2 * tile_rows, panel_rows)
 
     by_panel = pl.pallas_call(
         lambda *refs: scale_kernel(panel_blocks, *refs),
@@ -197,10 +193,8 @@
         for c in range(col_count)
     ]
     turned = lax.ppermute(piece, ("row", "col"), route)
-    turned, own_tile = lax.optimization_barrier((turned, ancestor_inv))
-    other_tile = lax.ppermute(own_tile, "row", core_swap)
     factor = over_col(jnp.broadcast_to(piece[None], (col_count, *piece.shape)))
-    tile_factor = pair_gather(factor)
+    tile_factor, tiles = lax.optimization_barrier((pair_gather(factor), tiles))
     tile_factor = tile_factor.transpose(0, 4, 2, 1, 3).reshape(width, 2 * tile_rows)
     parts = over_row(jnp.broadcast_to(turned[None], (chip_count, *turned.shape)))
 
@@ -208,15 +202,14 @@
     sent = pl.pallas_call(
         product_kernel,
         out_shape=jax.ShapeDtypeStruct(sent, BF16),
-        in_specs=[SMEM, SMEM, VMEM, VMEM, VMEM, VMEM],
+        in_specs=[SMEM, VMEM, VMEM, VMEM],
         out_specs=VMEM,
         scratch_shapes=[
             pltpu.VMEM((panel_rows, half), F32),
-            pltpu.VMEM((2 * tile_rows, half), F32),
             pltpu.VMEM(sent, F32),
         ],
         compiler_params=PARAMS,
-    )(core_arg, chip_arg, ancestor_inv, other_tile, parts, tile_factor)
+    )(chip_arg, tiles, parts, tile_factor)
     totals, copies = pl.pallas_call(
         total_kernel,
         out_shape=(

time: 122 us -> 133 us (1.090)
  between operations: 0.75 us -> 14.1 us
  waiting for transfers between devices: 34.6 us -> 29.3 us
  blocking collectives: 36.1 us -> 39.5 us
    all_to_all x2, waiting for transfers between devices: 9.82 us -> 3.74 us  [over_row(): lax.all_to_all(x, 'row', 0, 0, tiled=True, axis_index_groups=same_core)]
    ppermute x1 -> x0, starting transfers between devices: 5.98 us -> none  [body(): other_tile = lax.ppermute(own_tile, 'row', core_swap)]
    all_gather x3, blocking collectives: 12.9 us -> 16.5 us  [pair_gather(): return lax.all_gather(x, 'row', axis=0, axis_index_groups=core_pairs)]
    all_to_all x2, starting transfers between devices: 14 us -> 17.3 us  [over_col(): return lax.all_to_all(x, 'col', 0, 0, tiled=True)]
    all_to_all x2, starting transfers between devices: 11.7 us -> 13.3 us  [over_row(): lax.all_to_all(x, 'row', 0, 0, tiled=True, axis_index_groups=same_core)]
  transfers between devices with their start and end apart: 6 -> 6, of which waited for: 4 -> 4; matrix products, arithmetic and copies ran while one was open for 5% -> 5% of each run, Pallas kernels for 0% -> 2%
where the time goes in v7:
time: 133 us; the launch traced here: 132 us
  blocking collectives  39.5 us (30%)
  starting transfers between devices  35 us (26%)
  waiting for transfers between devices  29.3 us (22%)
  between operations  14.1 us (11%)
  Pallas kernels  6.17 us (5%)
  local copies, waits for them, and re-layouts  5.81 us (4%)
    all_to_all x1, blocking collectives, body(): taken = lax.all_to_all(by_panel, 'row', 0, 0, tiled=True)  23 us
    all_to_all x2, starting transfers between devices, over_col(): return lax.all_to_all(x, 'col', 0, 0, tiled=True)  17.3 us
    all_to_all x2, waiting for transfers between devices, over_col(): return lax.all_to_all(x, 'col', 0, 0, tiled=True)  17.2 us
    all_gather x3, blocking collectives, pair_gather(): return lax.all_gather(x, 'row', axis=0, axis_index_groups=core_pairs)  16.5 us
    all_to_all x2, starting transfers between devices, over_row(): lax.all_to_all(x, 'row', 0, 0, tiled=True, axis_index_groups=same_core)  13.3 us
    ppermute x1, waiting for transfers between devices, body(): turned = lax.ppermute(piece, ('row', 'col'), route)  7.68 us
    ppermute x1, starting transfers between devices, body(): turned = lax.ppermute(piece, ('row', 'col'), route)  4.35 us
    all_to_all x2, waiting for transfers between devices, over_row(): lax.all_to_all(x, 'row', 0, 0, tiled=True, axis_index_groups=same_core)  3.74 us
  transfers between devices with their start and end apart: 6, of which 4 were waited for; matrix products, arithmetic and copies ran while one was open for 5% of the time, Pallas kernels for 2%

profile of v7, /device:TPU:1, one launch (start us, length us, event | category | flops | bytes accessed | tf_op | source)
XLA Modules:
  0.0 131.9 jit_solution(3973363150387510209)
XLA Ops:
  7.2 0.7 all-gather.6.cloned.1.call-update
  7.9 2.5 %shard_map.68 = bf16[32,8,384]{2,1,0:T(8,128)(2,1)} custom-call(s32[16]{0:T(128)} %refs_0_.1, bf16[128,512]{1,0:T(8,128)(2,1)} %bitcast.20, f32[512,512]{1,0:T(8,128)} %refs_2_.1), custom_call_target="tpu_custom_call" | custom-call | tf_op jit(solution)/shard_map/pallas_call | solution.py:168
  10.4 23.0 %all_to_all.25.taken_ref = bf16[32,8,384]{2,1,0:T(8,128)(2,1)S(1)} all-to-all(bf16[32,8,384]{2,1,0:T(8,128)(2,1)} %shard_map.68), channel_id=1, replica_groups=mesh['row'=32,'col'=16] {'row'}, dimensions={0} | all-to-all | bytes 393216 | tf_op jit(solution)/shard_map/all_to_all | solution.py:180
  33.5 0.8 broadcast_in_dim.4
  34.3 10.2 %all-to-all-start.1 = ((bf16[16,6,8,256]{3,2,1,0:T(8,128)(2,1)}), bf16[16,6,8,256]{3,2,1,0:T(8,128)(2,1)S(1)}, u32[]{:S(2)}, u32[]{:S(2)}) async-start(bf16[16,6,8,256]{3,2,1,0:T(8,128)(2,1)} %broadcast_in_dim.4), calls=%async_computation.1 | async-start | bytes 786432 | tf_op jit(solution)/shard_map/all_to_all | solution.py:153
  44.5 4.3 %collective-permute-start = (bf16[6,8,256]{2,1,0:T(8,128)(2,1)S(1)}, bf16[6,8,256]{2,1,0:T(8,128)(2,1)S(1)}, u32[]{:S(2)}, u32[]{:S(2)}) collective-permute-start(bf16[6,8,256]{2,1,0:T(8,128)(2,1)S(1)} %shard_map.69), channel_id=1, source_target_pairs={{0,416},{1,384},{2,128},{3,352},{4,160},{5,448},{6,192},{7,480},{8... | collective-permute-start | bytes 73736 | tf_op jit(solution)/shard_map/ppermute | solution.py:195
  48.8 7.7 %collective-permute-done = bf16[6,8,256]{2,1,0:T(8,128)(2,1)S(1)} collective-permute-done((bf16[6,8,256]{2,1,0:T(8,128)(2,1)S(1)}, bf16[6,8,256]{2,1,0:T(8,128)(2,1)S(1)}, u32[]{:S(2)}, u32[]{:S(2)}) %collective-permute-start) | collective-permute-done | bytes 24608 | tf_op jit(solution)/shard_map/ppermute | solution.py:195
  56.5 0.8 broadcast_in_dim.5
  57.3 5.9 %all-to-all-start.2 = ((bf16[16,6,8,256]{3,2,1,0:T(8,128)(2,1)}), bf16[16,6,8,256]{3,2,1,0:T(8,128)(2,1)S(1)}, u32[]{:S(2)}, u32[]{:S(2)}) async-start(bf16[16,6,8,256]{3,2,1,0:T(8,128)(2,1)} %broadcast_in_dim.5), calls=%async_computation.2 | async-start | bytes 786432 | tf_op jit(solution)/shard_map/all_to_all | solution.py:150
  63.2 0.7 fusion.3.chip_ref
  63.9 5.9 %all-gather = bf16[32,6,8,256]{3,2,1,0:T(8,128)(2,1)S(1)} all-gather(bf16[16,6,8,256]{3,2,1,0:T(8,128)(2,1)S(1)} %all-to-all-done.1), channel_id=2, replica_groups={{0,16},{32,48},{64,80},{96,112},{128,144},{160,176},{192,208},{224,240}..., dimensions={0}, use_global_device_ids=true | all-gather | bytes 1179648 | tf_op jit(solution)/shard_map/all_gather | solution.py:147
  69.8 1.1 copy.9
  70.9 1.1 copy.11
  72.0 1.4 %copy.10.factor_ref = bf16[512,768]{1,0:T(8,128)(2,1)S(1)} copy(bf16[512,768]{0,1:T(8,128)(2,1)} %bitcast.18) | data formatting | bytes 1572864 | tf_op jit(solution)/shard_map/reshape | solution.py:198
  73.9 2.7 %shard_map.70 = bf16[16,80,256]{2,1,0:T(8,128)(2,1)} custom-call(s32[16]{0:T(128)S(1)} %fusion.3.chip_ref, f32[768,768]{1,0:T(8,128)S(1)} %copy-done, bf16[16,6,8,256]{3,2,1,0:T(8,128)(2,1)S(1)} %all-to-all-done.2.parts_ref, bf16[512,768]{1,0:T(8,128)(2,1)S(1)} %copy.10.factor_ref), custom_call_target="tpu_custom_call" | custom-call | tf_op jit(solution)/shard_map/pallas_call | solution.py:202
  76.7 7.1 %all-to-all-start.3 = ((bf16[16,80,256]{2,1,0:T(8,128)(2,1)}), bf16[16,80,256]{2,1,0:T(8,128)(2,1)S(1)}, u32[]{:S(2)}, u32[]{:S(2)}) async-start(bf16[16,80,256]{2,1,0:T(8,128)(2,1)} %shard_map.70), calls=%async_computation.3 | async-start | bytes 1310720 | tf_op jit(solution)/shard_map/all_to_all | solution.py:153
  83.8 17.2 %all-to-all-done.3.arrived_ref = bf16[16,80,256]{2,1,0:T(8,128)(2,1)S(1)} async-done(((bf16[16,80,256]{2,1,0:T(8,128)(2,1)}), bf16[16,80,256]{2,1,0:T(8,128)(2,1)S(1)}, u32[]{:S(2)}, u32[]{:S(2)}) %all-to-all-start.3) | async-done | bytes 655392 | tf_op jit(solution)/shard_map/all_to_all | solution.py:153
  101.0 0.8 shard_map.71
  101.7 7.4 %all-to-all-start.4 = ((bf16[16,32,256]{2,1,0:T(8,128)(2,1)}), bf16[16,32,256]{2,1,0:T(8,128)(2,1)S(1)}, u32[]{:S(2)}, u32[]{:S(2)}) async-start(bf16[16,32,256]{2,1,0:T(8,128)(2,1)} %get-tuple-element.9), calls=%async_computation.4 | async-start | bytes 524288 | tf_op jit(solution)/shard_map/all_to_all | solution.py:150
  109.2 0.7 fusion
  109.9 4.7 %all-gather.2 = f32[96,256]{1,0:T(8,128)S(1)} all-gather(f32[48,256]{1,0:T(8,128)S(1)} %get-tuple-element.8), channel_id=4, replica_groups={{0,16},{32,48},{64,80},{96,112},{128,144},{160,176},{192,208},{224,240}..., dimensions={0}, use_global_device_ids=true | all-gather | bytes 147456 | tf_op jit(solution)/shard_map/all_gather | solution.py:147
  115.3 3.2 %all-to-all-done.4 = bf16[16,32,256]{2,1,0:T(8,128)(2,1)S(1)} async-done(((bf16[16,32,256]{2,1,0:T(8,128)(2,1)}), bf16[16,32,256]{2,1,0:T(8,128)(2,1)S(1)}, u32[]{:S(2)}, u32[]{:S(2)}) %all-to-all-start.4) | async-done | bytes 262176 | tf_op jit(solution)/shard_map/all_to_all | solution.py:150
  118.5 5.9 %all-gather.3 = f32[64,256]{1,0:T(8,128)S(1)} all-gather(f32[32,256]{1,0:T(8,128)S(1)} %convert_reduce_fusion), channel_id=5, replica_groups={{0,16},{32,48},{64,80},{96,112},{128,144},{160,176},{192,208},{224,240}..., dimensions={0}, use_global_device_ids=true | all-gather | bytes 98304 | tf_op jit(solution)/shard_map/all_gather | solution.py:147
  124.4 0.6 maximum_add_fusion
  (13 shorter events, 1.5 us)
Async XLA Ops:
  7.2 62.7 %all-gather.6.cloned.1.call-start = ((), (), s32[]{:S(2)}) async-start(), calls=%async_computation.5 | async-start | bytes 3538944 | tf_op jit(solution)/shard_map/all_gather | solution.py:147
  34.3 22.2 %all-to-all-start.1 = ((bf16[16,6,8,256]{3,2,1,0:T(8,128)(2,1)}), bf16[16,6,8,256]{3,2,1,0:T(8,128)(2,1)S(1)}, u32[]{:S(2)}, u32[]{:S(2)}) async-start(bf16[16,6,8,256]{3,2,1,0:T(8,128)(2,1)} %broadcast_in_dim.4), calls=%async_computation.1 | async-start | bytes 786432 | tf_op jit(solution)/shard_map/all_to_all | solution.py:153
  44.5 12.0 %collective-permute-start = (bf16[6,8,256]{2,1,0:T(8,128)(2,1)S(1)}, bf16[6,8,256]{2,1,0:T(8,128)(2,1)S(1)}, u32[]{:S(2)}, u32[]{:S(2)}) collective-permute-start(bf16[6,8,256]{2,1,0:T(8,128)(2,1)S(1)} %shard_map.69), channel_id=1, source_target_pairs={{0,416},{1,384},{2,128},{3,352},{4,160},{5,448},{6,192},{7,480},{8... | collective-permute-start | bytes 73736 | tf_op jit(solution)/shard_map/ppermute | solution.py:195
  57.3 16.6 %all-to-all-start.2 = ((bf16[16,6,8,256]{3,2,1,0:T(8,128)(2,1)}), bf16[16,6,8,256]{3,2,1,0:T(8,128)(2,1)S(1)}, u32[]{:S(2)}, u32[]{:S(2)}) async-start(bf16[16,6,8,256]{3,2,1,0:T(8,128)(2,1)} %broadcast_in_dim.5), calls=%async_computation.2 | async-start | bytes 786432 | tf_op jit(solution)/shard_map/all_to_all | solution.py:150
  69.8 4.1 %copy-start = (f32[768,768]{1,0:T(8,128)S(1)}, f32[768,768]{1,0:T(8,128)}, u32[]{:S(2)}) copy-start(f32[768,768]{1,0:T(8,128)} %all-gather.6.cloned.1.call-done.tiles_ref) | copy-start | bytes 7077892
  76.7 32.5 %copy-start.1 = (f32[512,512]{1,0:T(8,128)S(1)}, f32[512,512]{1,0:T(8,128)}, u32[]{:S(2)}) copy-start(f32[512,512]{1,0:T(8,128)} %refs_2_.1) | copy-start | bytes 3145732
  76.7 24.3 %all-to-all-start.3 = ((bf16[16,80,256]{2,1,0:T(8,128)(2,1)}), bf16[16,80,256]{2,1,0:T(8,128)(2,1)S(1)}, u32[]{:S(2)}, u32[]{:S(2)}) async-start(bf16[16,80,256]{2,1,0:T(8,128)(2,1)} %shard_map.70), calls=%async_computation.3 | async-start | bytes 1310720 | tf_op jit(solution)/shard_map/all_to_all | solution.py:153
  101.7 16.7 %all-to-all-start.4 = ((bf16[16,32,256]{2,1,0:T(8,128)(2,1)}), bf16[16,32,256]{2,1,0:T(8,128)(2,1)S(1)}, u32[]{:S(2)}, u32[]{:S(2)}) async-start(bf16[16,32,256]{2,1,0:T(8,128)(2,1)} %get-tuple-element.9), calls=%async_computation.4 | async-start | bytes 524288 | tf_op jit(solution)/shard_map/all_to_all | solution.py:150
Sparse Core Ops, SparseCore 0:
  10.1 26.0 all-gather.5

commit v8 on v7

--- a/solution.py
+++ b/solution.py
@@ -95,15 +95,20 @@
             out_ref[n, :, lanes : lanes + TAG] = total.astype(BF16)
 
 
-def product_kernel(chip_ref, tiles_ref, parts_ref, factor_ref, out_ref, panel_ref, sent_ref):
+def product_kernel(chip_ref, *refs):
+    *tile_refs, parts_ref, factor_ref, out_ref, panel_ref, high_ref, low_ref, sent_ref = refs
     chunks, blocks, height, half = parts_ref.shape
+    for b, ref in enumerate(tile_refs):
+        rows = ref.shape[1]
+        for k in range(2):
+            first = (k * len(tile_refs) + b) * rows
+            high_ref[first : first + rows, :], low_ref[first : first + rows, :] = split(ref[k])
     for c in range(chunks):
         for b in range(blocks):
             first = (b * chunks + c) * height
             panel_ref[first : first + height, :] = parts_ref[chip_ref[c], b].astype(F32)
     panel = panel_ref[...].astype(BF16)
-    high, low = split(tiles_ref[...])
-    sums = dot(high, panel) + dot(low, panel)
+    sums = dot(high_ref[...], panel) + dot(low_ref[...], panel)
     gram = dot(factor_ref[...], sums.astype(BF16))
     rows = gram.shape[0] // chunks
     share = sums.shape[0] // 2 // chunks
@@ -153,17 +158,13 @@
         return lax.all_to_all(x, "col", 0, 0, tiled=True)
 
     factor_cols = lax.dynamic_slice_in_dim(inv_factor, col_index * diag_width, diag_width, 1)
-    factor_gram = lax.optimization_barrier(
-        lax.dot_general(
-            factor_cols,
-            inv_factor,
-            (((0,), (0,)), ((), ())),
-            precision=lax.Precision.HIGHEST,
-            preferred_element_type=F32,
-        )
+    factor_gram = lax.dot_general(
+        factor_cols,
+        inv_factor,
+        (((0,), (0,)), ((), ())),
+        precision=lax.Precision.HIGHEST,
+        preferred_element_type=F32,
     )
-
-    tiles = pair_gather(ancestor_inv).reshape(2 * tile_rows, panel_rows)
 
     by_panel = pl.pallas_call(
         lambda *refs: scale_kernel(panel_blocks, *refs),
@@ -177,7 +178,13 @@
         front_rows.reshape(slot_count * chunk_rows, width),
         inv_factor,
     )
-    taken = lax.all_to_all(by_panel, "row", 0, 0, tiled=True)
+    by_panel, tile = lax.optimization_barrier((by_panel, ancestor_inv))
+    tiles = [
+        pair_gather(tile[first : first + block_rows]) for first in range(0, tile_rows, block_rows)
+    ]
+    taken, factor_gram, core, *tiles = lax.optimization_barrier(
+        (lax.all_to_all(by_panel, "row", 0, 0, tiled=True), factor_gram, core, *tiles)
+    )
     piece = pl.pallas_call(
         place_kernel,
         out_shape=jax.ShapeDtypeStruct((panel_blocks, chunk_rows, half), BF16),
@@ -194,7 +201,7 @@
     ]
     turned = lax.ppermute(piece, ("row", "col"), route)
     factor = over_col(jnp.broadcast_to(piece[None], (col_count, *piece.shape)))
-    tile_factor, tiles = lax.optimization_barrier((pair_gather(factor), tiles))
+    tile_factor = pair_gather(factor)
     tile_factor = tile_factor.transpose(0, 4, 2, 1, 3).reshape(width, 2 * tile_rows)
     parts = over_row(jnp.broadcast_to(turned[None], (chip_count, *turned.shape)))
 
@@ -202,14 +209,16 @@
     sent = pl.pallas_call(
         product_kernel,
         out_shape=jax.ShapeDtypeStruct(sent, BF16),
-        in_specs=[SMEM, VMEM, VMEM, VMEM],
+        in_specs=[SMEM] + [VMEM] * (len(tiles) + 2),
         out_specs=VMEM,
         scratch_shapes=[
             pltpu.VMEM((panel_rows, half), F32),
+            pltpu.VMEM((2 * tile_rows, panel_rows), BF16),
+            pltpu.VMEM((2 * tile_rows, panel_rows), BF16),
             pltpu.VMEM(sent, F32),
         ],
-        compiler_params=PARAMS,
-    )(chip_arg, tiles, parts, tile_factor)
+        compiler_params=pltpu.CompilerParams(vmem_limit_bytes=52 * 2**20),
+    )(chip_arg, *tiles, parts, tile_factor)
     totals, copies = pl.pallas_call(
         total_kernel,
         out_shape=(
@@ -221,7 +230,7 @@
         compiler_params=PARAMS,
     )(over_col(sent))
     halves = pair_gather(totals).reshape(2, 2, share, half)
-    product = lax.dynamic_index_in_dim(halves, core, 1, keepdims=False)
+    product = jnp.where(core == 0, halves[:, 0], halves[:, 1])
     product = jnp.concatenate([product[0], product[1]], 1)
     gram_rows = pair_gather(jnp.sum(over_row(copies).astype(F32), axis=0))
     gram_rows = jnp.concatenate([gram_rows[0], gram_rows[1]], 1)

time: 133 us -> 120 us (0.902)
  blocking collectives: 39.5 us -> 24.2 us
  starting transfers between devices: 35 us -> 49.8 us
  between operations: 14.1 us -> 0.75 us
    all_to_all x1 -> x0, blocking collectives: 23 us -> none  [body(): taken = lax.all_to_all(by_panel, 'row', 0, 0, tiled=True)]
    all_to_all x0 -> x1, starting transfers between devices: none -> 11.2 us  [body(): lax.all_to_all(by_panel, 'row', 0, 0, tiled=True)]
    all_gather x3 -> x6, blocking collectives: 16.5 us -> 24.2 us  [pair_gather(): return lax.all_gather(x, 'row', axis=0, axis_index_groups=core_pairs)]
    all_to_all x0 -> x1, waiting for transfers between devices: none -> 3.35 us  [body(): lax.all_to_all(by_panel, 'row', 0, 0, tiled=True)]
    all_to_all x2, starting transfers between devices: 13.3 us -> 16.6 us  [over_row(): lax.all_to_all(x, 'row', 0, 0, tiled=True, axis_index_groups=same_core)]
    ppermute x1, starting transfers between devices: 4.35 us -> 6.03 us  [body(): turned = lax.ppermute(piece, ('row', 'col'), route)]
    ppermute x1, waiting for transfers between devices: 7.68 us -> 6 us  [body(): turned = lax.ppermute(piece, ('row', 'col'), route)]
    all_to_all x2, waiting for transfers between devices: 3.74 us -> 5.34 us  [over_row(): lax.all_to_all(x, 'row', 0, 0, tiled=True, axis_index_groups=same_core)]
  transfers between devices with their start and end apart: 6 -> 6, of which waited for: 4 -> 5; matrix products, arithmetic and copies ran while one was open for 5% -> 4% of each run, Pallas kernels for 2% -> 0%
where the time goes in v8:
time: 120 us; the launch traced here: 119 us
  starting transfers between devices  49.8 us (42%)
  waiting for transfers between devices  30.3 us (25%)
  blocking collectives  24.2 us (20%)
  Pallas kernels  7.35 us (6%)
  local copies, waits for them, and re-layouts  4.77 us (4%)
  other arithmetic  1.31 us (1%)
    all_gather x6, blocking collectives, pair_gather(): return lax.all_gather(x, 'row', axis=0, axis_index_groups=core_pairs)  24.2 us
    all_to_all x2, starting transfers between devices, over_row(): lax.all_to_all(x, 'row', 0, 0, tiled=True, axis_index_groups=same_core)  16.6 us
    all_to_all x2, starting transfers between devices, over_col(): return lax.all_to_all(x, 'col', 0, 0, tiled=True)  16.1 us
    all_to_all x2, waiting for transfers between devices, over_col(): return lax.all_to_all(x, 'col', 0, 0, tiled=True)  15.6 us
    all_to_all x1, starting transfers between devices, body(): lax.all_to_all(by_panel, 'row', 0, 0, tiled=True)  11.2 us
    ppermute x1, starting transfers between devices, body(): turned = lax.ppermute(piece, ('row', 'col'), route)  6.03 us
    ppermute x1, waiting for transfers between devices, body(): turned = lax.ppermute(piece, ('row', 'col'), route)  6 us
    all_to_all x2, waiting for transfers between devices, over_row(): lax.all_to_all(x, 'row', 0, 0, tiled=True, axis_index_groups=same_core)  5.34 us
  transfers between devices with their start and end apart: 6, of which 5 were waited for; matrix products, arithmetic and copies ran while one was open for 4% of the time, Pallas kernels for 0%

profile of v8, /device:TPU:1, one launch (start us, length us, event | category | flops | bytes accessed | tf_op | source)
XLA Modules:
  0.0 119.3 jit_solution(6725597742487780060)
XLA Ops:
  0.6 2.6 %shard_map.68 = bf16[32,8,384]{2,1,0:T(8,128)(2,1)} custom-call(s32[16]{0:T(128)} %refs_0_.1, bf16[128,512]{1,0:T(8,128)(2,1)} %bitcast.27, f32[512,512]{1,0:T(8,128)} %refs_2_.1), custom_call_target="tpu_custom_call" | custom-call | tf_op jit(solution)/shard_map/pallas_call | solution.py:169
  3.2 11.2 %all-to-all-start = ((bf16[32,8,384]{2,1,0:T(8,128)(2,1)}), bf16[32,8,384]{2,1,0:T(8,128)(2,1)S(1)}, u32[]{:S(2)}, u32[]{:S(2)}) async-start(bf16[32,8,384]{2,1,0:T(8,128)(2,1)} %shard_map.68), calls=%async_computation | async-start | bytes 393216 | tf_op jit(solution)/shard_map/all_to_all | solution.py:186
  14.6 2.4 %all-gather = f32[256,768]{1,0:T(8,128)S(1)} all-gather(f32[128,768]{1,0:T(8,128)S(1)} %get-tuple-element.24), channel_id=2, replica_groups={{0,16},{32,48},{64,80},{96,112},{128,144},{160,176},{192,208},{224,240}..., dimensions={0}, use_global_device_ids=true | all-gather | bytes 1179648 | tf_op jit(solution)/shard_map/all_gather | solution.py:152
  16.9 2.6 %all-gather.1 = f32[256,768]{1,0:T(8,128)} all-gather(f32[128,768]{1,0:T(8,128)S(1)} %get-tuple-element.23), channel_id=3, replica_groups={{0,16},{32,48},{64,80},{96,112},{128,144},{160,176},{192,208},{224,240}..., dimensions={0}, use_global_device_ids=true | all-gather | bytes 1179648 | tf_op jit(solution)/shard_map/all_gather | solution.py:152
  19.6 2.5 %all-gather.2 = f32[256,768]{1,0:T(8,128)} all-gather(f32[128,768]{1,0:T(8,128)S(1)} %get-tuple-element.22), channel_id=4, replica_groups={{0,16},{32,48},{64,80},{96,112},{128,144},{160,176},{192,208},{224,240}..., dimensions={0}, use_global_device_ids=true | all-gather | bytes 1179648 | tf_op jit(solution)/shard_map/all_gather | solution.py:152
  22.8 3.4 %all-to-all-done.taken_ref = bf16[32,8,384]{2,1,0:T(8,128)(2,1)S(1)} async-done(((bf16[32,8,384]{2,1,0:T(8,128)(2,1)}), bf16[32,8,384]{2,1,0:T(8,128)(2,1)S(1)}, u32[]{:S(2)}, u32[]{:S(2)}) %all-to-all-start) | async-done | bytes 196640 | tf_op jit(solution)/shard_map/all_to_all | solution.py:186
  26.3 0.8 broadcast_in_dim.5
  27.1 10.2 %all-to-all-start.2 = ((bf16[16,6,8,256]{3,2,1,0:T(8,128)(2,1)}), bf16[16,6,8,256]{3,2,1,0:T(8,128)(2,1)S(1)}, u32[]{:S(2)}, u32[]{:S(2)}) async-start(bf16[16,6,8,256]{3,2,1,0:T(8,128)(2,1)} %broadcast_in_dim.5), calls=%async_computation.2 | async-start | bytes 786432 | tf_op jit(solution)/shard_map/all_to_all | solution.py:158
  37.3 6.0 %collective-permute-start = (bf16[6,8,256]{2,1,0:T(8,128)(2,1)S(1)}, bf16[6,8,256]{2,1,0:T(8,128)(2,1)S(1)}, u32[]{:S(2)}, u32[]{:S(2)}) collective-permute-start(bf16[6,8,256]{2,1,0:T(8,128)(2,1)S(1)} %shard_map.69), channel_id=1, source_target_pairs={{0,416},{1,384},{2,128},{3,352},{4,160},{5,448},{6,192},{7,480},{8... | collective-permute-start | bytes 73736 | tf_op jit(solution)/shard_map/ppermute | solution.py:202
  43.3 6.0 %collective-permute-done = bf16[6,8,256]{2,1,0:T(8,128)(2,1)S(1)} collective-permute-done((bf16[6,8,256]{2,1,0:T(8,128)(2,1)S(1)}, bf16[6,8,256]{2,1,0:T(8,128)(2,1)S(1)}, u32[]{:S(2)}, u32[]{:S(2)}) %collective-permute-start) | collective-permute-done | bytes 24608 | tf_op jit(solution)/shard_map/ppermute | solution.py:202
  49.3 0.8 broadcast_in_dim.4
  50.1 7.8 %all-to-all-start.1 = ((bf16[16,6,8,256]{3,2,1,0:T(8,128)(2,1)}), bf16[16,6,8,256]{3,2,1,0:T(8,128)(2,1)S(1)}, u32[]{:S(2)}, u32[]{:S(2)}) async-start(bf16[16,6,8,256]{3,2,1,0:T(8,128)(2,1)} %broadcast_in_dim.4), calls=%async_computation.1 | async-start | bytes 786432 | tf_op jit(solution)/shard_map/all_to_all | solution.py:155
  58.6 6.3 %all-gather.3 = bf16[32,6,8,256]{3,2,1,0:T(8,128)(2,1)S(1)} all-gather(bf16[16,6,8,256]{3,2,1,0:T(8,128)(2,1)S(1)} %all-to-all-done.2), channel_id=5, replica_groups={{0,16},{32,48},{64,80},{96,112},{128,144},{160,176},{192,208},{224,240}..., dimensions={0}, use_global_device_ids=true | all-gather | bytes 1179648 | tf_op jit(solution)/shard_map/all_gather | solution.py:152
  64.9 1.1 copy.9
  66.2 1.2 copy.10.refs_4_
  67.3 1.3 %all-to-all-done.1.refs_3_ = bf16[16,6,8,256]{3,2,1,0:T(8,128)(2,1)S(1)} async-done(((bf16[16,6,8,256]{3,2,1,0:T(8,128)(2,1)}), bf16[16,6,8,256]{3,2,1,0:T(8,128)(2,1)S(1)}, u32[]{:S(2)}, u32[]{:S(2)}) %all-to-all-start.1) | async-done | bytes 393248 | tf_op jit(solution)/shard_map/all_to_all | solution.py:155
  68.6 3.8 %shard_map.70 = bf16[16,80,256]{2,1,0:T(8,128)(2,1)} custom-call(s32[16]{0:T(128)S(1)} %dynamic-slice_bitcast_fusion.chip_ref, f32[2,128,768]{2,1,0:T(8,128)S(1)} %bitcast.20, f32[2,128,768]{2,1,0:T(8,128)} %bitcast.21, f32[2,128,768]{2,1,0:T(8,128)} %bitcast.22, bf16[16,6,8,256]{3,2,1,0:T(8,128)(2,1)S(1)} %all-to-all-done.1.refs_3_, ...), custom_call_target="tpu_custom_call" | custom-call | tf_op jit(solution)/shard_map/pallas_call | solution.py:209
  72.4 5.9 %all-to-all-start.3 = ((bf16[16,80,256]{2,1,0:T(8,128)(2,1)}), bf16[16,80,256]{2,1,0:T(8,128)(2,1)S(1)}, u32[]{:S(2)}, u32[]{:S(2)}) async-start(bf16[16,80,256]{2,1,0:T(8,128)(2,1)} %shard_map.70), calls=%async_computation.3 | async-start | bytes 1310720 | tf_op jit(solution)/shard_map/all_to_all | solution.py:158
  78.3 15.6 %all-to-all-done.3.arrived_ref = bf16[16,80,256]{2,1,0:T(8,128)(2,1)S(1)} async-done(((bf16[16,80,256]{2,1,0:T(8,128)(2,1)}), bf16[16,80,256]{2,1,0:T(8,128)(2,1)S(1)}, u32[]{:S(2)}, u32[]{:S(2)}) %all-to-all-start.3) | async-done | bytes 655392 | tf_op jit(solution)/shard_map/all_to_all | solution.py:158
  94.0 0.8 shard_map.71
  94.7 8.7 %all-to-all-start.4 = ((bf16[16,32,256]{2,1,0:T(8,128)(2,1)}), bf16[16,32,256]{2,1,0:T(8,128)(2,1)S(1)}, u32[]{:S(2)}, u32[]{:S(2)}) async-start(bf16[16,32,256]{2,1,0:T(8,128)(2,1)} %get-tuple-element.21), calls=%async_computation.4 | async-start | bytes 524288 | tf_op jit(solution)/shard_map/all_to_all | solution.py:155
  103.5 4.6 %all-gather.4 = f32[96,256]{1,0:T(8,128)S(1)} all-gather(f32[48,256]{1,0:T(8,128)S(1)} %get-tuple-element.19), channel_id=6, replica_groups={{0,16},{32,48},{64,80},{96,112},{128,144},{160,176},{192,208},{224,240}..., dimensions={0}, use_global_device_ids=true | all-gather | bytes 147456 | tf_op jit(solution)/shard_map/all_gather | solution.py:152
  108.7 4.1 %all-to-all-done.4 = bf16[16,32,256]{2,1,0:T(8,128)(2,1)S(1)} async-done(((bf16[16,32,256]{2,1,0:T(8,128)(2,1)}), bf16[16,32,256]{2,1,0:T(8,128)(2,1)S(1)}, u32[]{:S(2)}, u32[]{:S(2)}) %all-to-all-start.4) | async-done | bytes 262176 | tf_op jit(solution)/shard_map/all_to_all | solution.py:155
  112.8 5.9 %all-gather.5 = f32[64,256]{1,0:T(8,128)S(1)} all-gather(f32[32,256]{1,0:T(8,128)S(1)} %convert_reduce_fusion), channel_id=7, replica_groups={{0,16},{32,48},{64,80},{96,112},{128,144},{160,176},{192,208},{224,240}..., dimensions={0}, use_global_device_ids=true | all-gather | bytes 98304 | tf_op jit(solution)/shard_map/all_gather | solution.py:152
  (16 shorter events, 3.2 us)
Async XLA Ops:
  0.6 13.8 %copy-start.1 = (f32[384,768]{1,0:T(8,128)S(1)}, f32[384,768]{1,0:T(8,128)}, u32[]{:S(2)}) copy-start(f32[384,768]{1,0:T(8,128)} %param.8) | copy-start | bytes 3538948
  3.2 22.9 %all-to-all-start = ((bf16[32,8,384]{2,1,0:T(8,128)(2,1)}), bf16[32,8,384]{2,1,0:T(8,128)(2,1)S(1)}, u32[]{:S(2)}, u32[]{:S(2)}) async-start(bf16[32,8,384]{2,1,0:T(8,128)(2,1)} %shard_map.68), calls=%async_computation | async-start | bytes 393216 | tf_op jit(solution)/shard_map/all_to_all | solution.py:186
  16.9 5.1 %copy-start = (f32[512,512]{1,0:T(8,128)S(1)}, f32[512,512]{1,0:T(8,128)}, u32[]{:S(2)}) copy-start(f32[512,512]{1,0:T(8,128)} %refs_2_.1) | copy-start | bytes 3145732
  27.1 22.2 %all-to-all-start.2 = ((bf16[16,6,8,256]{3,2,1,0:T(8,128)(2,1)}), bf16[16,6,8,256]{3,2,1,0:T(8,128)(2,1)S(1)}, u32[]{:S(2)}, u32[]{:S(2)}) async-start(bf16[16,6,8,256]{3,2,1,0:T(8,128)(2,1)} %broadcast_in_dim.5), calls=%async_computation.2 | async-start | bytes 786432 | tf_op jit(solution)/shard_map/all_to_all | solution.py:158
  37.3 12.0 %collective-permute-start = (bf16[6,8,256]{2,1,0:T(8,128)(2,1)S(1)}, bf16[6,8,256]{2,1,0:T(8,128)(2,1)S(1)}, u32[]{:S(2)}, u32[]{:S(2)}) collective-permute-start(bf16[6,8,256]{2,1,0:T(8,128)(2,1)S(1)} %shard_map.69), channel_id=1, source_target_pairs={{0,416},{1,384},{2,128},{3,352},{4,160},{5,448},{6,192},{7,480},{8... | collective-permute-start | bytes 73736 | tf_op jit(solution)/shard_map/ppermute | solution.py:202
  50.1 18.5 %all-to-all-start.1 = ((bf16[16,6,8,256]{3,2,1,0:T(8,128)(2,1)}), bf16[16,6,8,256]{3,2,1,0:T(8,128)(2,1)S(1)}, u32[]{:S(2)}, u32[]{:S(2)}) async-start(bf16[16,6,8,256]{3,2,1,0:T(8,128)(2,1)} %broadcast_in_dim.4), calls=%async_computation.1 | async-start | bytes 786432 | tf_op jit(solution)/shard_map/all_to_all | solution.py:155
  72.4 21.5 %all-to-all-start.3 = ((bf16[16,80,256]{2,1,0:T(8,128)(2,1)}), bf16[16,80,256]{2,1,0:T(8,128)(2,1)S(1)}, u32[]{:S(2)}, u32[]{:S(2)}) async-start(bf16[16,80,256]{2,1,0:T(8,128)(2,1)} %shard_map.70), calls=%async_computation.3 | async-start | bytes 1310720 | tf_op jit(solution)/shard_map/all_to_all | solution.py:158
  94.7 18.0 %all-to-all-start.4 = ((bf16[16,32,256]{2,1,0:T(8,128)(2,1)}), bf16[16,32,256]{2,1,0:T(8,128)(2,1)S(1)}, u32[]{:S(2)}, u32[]{:S(2)}) async-start(bf16[16,32,256]{2,1,0:T(8,128)(2,1)} %get-tuple-element.21), calls=%async_computation.4 | async-start | bytes 524288 | tf_op jit(solution)/shard_map/all_to_all | solution.py:155

commit v9 on v8

--- a/solution.py
+++ b/solution.py
@@ -158,12 +158,14 @@
         return lax.all_to_all(x, "col", 0, 0, tiled=True)
 
     factor_cols = lax.dynamic_slice_in_dim(inv_factor, col_index * diag_width, diag_width, 1)
-    factor_gram = lax.dot_general(
-        factor_cols,
-        inv_factor,
-        (((0,), (0,)), ((), ())),
-        precision=lax.Precision.HIGHEST,
-        preferred_element_type=F32,
+    factor_gram = lax.optimization_barrier(
+        lax.dot_general(
+            factor_cols,
+            inv_factor,
+            (((0,), (0,)), ((), ())),
+            precision=lax.Precision.HIGHEST,
+            preferred_element_type=F32,
+        )
     )
 
     by_panel = pl.pallas_call(
@@ -180,10 +182,11 @@
     )
     by_panel, tile = lax.optimization_barrier((by_panel, ancestor_inv))
     tiles = [
-        pair_gather(tile[first : first + block_rows]) for first in range(0, tile_rows, block_rows)
+        pair_gather(tile[first : first + block_rows])
+        for first in range(0, tile_rows - block_rows, block_rows)
     ]
-    taken, factor_gram, core, *tiles = lax.optimization_barrier(
-        (lax.all_to_all(by_panel, "row", 0, 0, tiled=True), factor_gram, core, *tiles)
+    taken, core, *tiles = lax.optimization_barrier(
+        (lax.all_to_all(by_panel, "row", 0, 0, tiled=True), core, *tiles)
     )
     piece = pl.pallas_call(
         place_kernel,
@@ -199,8 +202,13 @@
         for k in range(2)
         for c in range(col_count)
     ]
+    piece, tile = lax.optimization_barrier((piece, tile))
     turned = lax.ppermute(piece, ("row", "col"), route)
     factor = over_col(jnp.broadcast_to(piece[None], (col_count, *piece.shape)))
+    factor, last_tile = lax.optimization_barrier(
+        (factor, pair_gather(tile[tile_rows - block_rows :]))
+    )
+    tiles.append(last_tile)
     tile_factor = pair_gather(factor)
     tile_factor = tile_factor.transpose(0, 4, 2, 1, 3).reshape(width, 2 * tile_rows)
     parts = over_row(jnp.broadcast_to(turned[None], (chip_count, *turned.shape)))
@@ -217,7 +225,7 @@
             pltpu.VMEM((2 * tile_rows, panel_rows), BF16),
             pltpu.VMEM(sent, F32),
         ],
-        compiler_params=pltpu.CompilerParams(vmem_limit_bytes=52 * 2**20),
+        compiler_params=pltpu.CompilerParams(vmem_limit_bytes=50 * 2**20),
     )(chip_arg, *tiles, parts, tile_factor)
     totals, copies = pl.pallas_call(
         total_kernel,

time: 120 us -> 119 us (level)
  waiting for transfers between devices: 30.3 us -> 34.8 us
  starting transfers between devices: 49.8 us -> 45.5 us
    all_to_all x1, waiting for transfers between devices: 3.35 us -> 6.89 us  [body(): lax.all_to_all(by_panel, 'row', 0, 0, tiled=True)]
    all_to_all x2, starting transfers between devices: 16.6 us -> 13.1 us  [over_row(): lax.all_to_all(x, 'row', 0, 0, tiled=True, axis_index_groups=same_core)]
    ppermute x1, starting transfers between devices: 6.03 us -> 4.48 us  [body(): turned = lax.ppermute(piece, ('row', 'col'), route)]
    ppermute x1, waiting for transfers between devices: 6 us -> 7.54 us  [body(): turned = lax.ppermute(piece, ('row', 'col'), route)]
    all_to_all x2, waiting for transfers between devices: 5.34 us -> 3.94 us  [over_row(): lax.all_to_all(x, 'row', 0, 0, tiled=True, axis_index_groups=same_core)]
  transfers between devices with their start and end apart: 6 -> 6, of which waited for: 5 -> 4; matrix products, arithmetic and copies ran while one was open for 4% -> 4% of each run, Pallas kernels for 0% -> 0%
where the time goes in v9:
time: 119 us; the launch traced here: 118 us
  starting transfers between devices  45.5 us (38%)
  waiting for transfers between devices  34.8 us (29%)
  blocking collectives  23.5 us (20%)
  Pallas kernels  7 us (6%)
  local copies, waits for them, and re-layouts  4.78 us (4%)
  other arithmetic  1.32 us (1%)
    all_gather x6, blocking collectives, pair_gather(): return lax.all_gather(x, 'row', axis=0, axis_index_groups=core_pairs)  23.5 us
    all_to_all x2, starting transfers between devices, over_col(): return lax.all_to_all(x, 'col', 0, 0, tiled=True)  16.8 us
    all_to_all x2, waiting for transfers between devices, over_col(): return lax.all_to_all(x, 'col', 0, 0, tiled=True)  16.4 us
    all_to_all x2, starting transfers between devices, over_row(): lax.all_to_all(x, 'row', 0, 0, tiled=True, axis_index_groups=same_core)  13.1 us
    all_to_all x1, starting transfers between devices, body(): lax.all_to_all(by_panel, 'row', 0, 0, tiled=True)  11.1 us
    ppermute x1, waiting for transfers between devices, body(): turned = lax.ppermute(piece, ('row', 'col'), route)  7.54 us
    all_to_all x1, waiting for transfers between devices, body(): lax.all_to_all(by_panel, 'row', 0, 0, tiled=True)  6.89 us
    ppermute x1, starting transfers between devices, body(): turned = lax.ppermute(piece, ('row', 'col'), route)  4.48 us
  transfers between devices with their start and end apart: 6, of which 4 were waited for; matrix products, arithmetic and copies ran while one was open for 4% of the time, Pallas kernels for 0%

profile of v9, /device:TPU:1, one launch (start us, length us, event | category | flops | bytes accessed | tf_op | source)
XLA Modules:
  0.0 118.5 jit_solution(3368171079818894675)
XLA Ops:
  0.6 2.7 %shard_map.68 = bf16[32,8,384]{2,1,0:T(8,128)(2,1)} custom-call(s32[16]{0:T(128)} %refs_0_.1, bf16[128,512]{1,0:T(8,128)(2,1)} %bitcast.27, f32[512,512]{1,0:T(8,128)} %refs_2_.1), custom_call_target="tpu_custom_call" | custom-call | tf_op jit(solution)/shard_map/pallas_call | solution.py:171
  3.4 11.1 %all-to-all-start = ((bf16[32,8,384]{2,1,0:T(8,128)(2,1)}), bf16[32,8,384]{2,1,0:T(8,128)(2,1)S(1)}, u32[]{:S(2)}, u32[]{:S(2)}) async-start(bf16[32,8,384]{2,1,0:T(8,128)(2,1)} %shard_map.68), calls=%async_computation | async-start | bytes 393216 | tf_op jit(solution)/shard_map/all_to_all | solution.py:189
  14.5 2.4 %all-gather = f32[256,768]{1,0:T(8,128)S(1)} all-gather(f32[128,768]{1,0:T(8,128)S(1)} %get-tuple-element.27), channel_id=2, replica_groups={{0,16},{32,48},{64,80},{96,112},{128,144},{160,176},{192,208},{224,240}..., dimensions={0}, use_global_device_ids=true | all-gather | bytes 1179648 | tf_op jit(solution)/shard_map/all_gather | solution.py:152
  16.9 2.4 %all-gather.1 = f32[256,768]{1,0:T(8,128)S(1)} all-gather(f32[128,768]{1,0:T(8,128)S(1)} %get-tuple-element.26), channel_id=3, replica_groups={{0,16},{32,48},{64,80},{96,112},{128,144},{160,176},{192,208},{224,240}..., dimensions={0}, use_global_device_ids=true | all-gather | bytes 1179648 | tf_op jit(solution)/shard_map/all_gather | solution.py:152
  19.2 6.9 %all-to-all-done.taken_ref = bf16[32,8,384]{2,1,0:T(8,128)(2,1)S(1)} async-done(((bf16[32,8,384]{2,1,0:T(8,128)(2,1)}), bf16[32,8,384]{2,1,0:T(8,128)(2,1)S(1)}, u32[]{:S(2)}, u32[]{:S(2)}) %all-to-all-start) | async-done | bytes 196640 | tf_op jit(solution)/shard_map/all_to_all | solution.py:189
  26.3 0.8 broadcast_in_dim.4
  27.1 10.2 %all-to-all-start.1 = ((bf16[16,6,8,256]{3,2,1,0:T(8,128)(2,1)}), bf16[16,6,8,256]{3,2,1,0:T(8,128)(2,1)S(1)}, u32[]{:S(2)}, u32[]{:S(2)}) async-start(bf16[16,6,8,256]{3,2,1,0:T(8,128)(2,1)} %broadcast_in_dim.4), calls=%async_computation.1 | async-start | bytes 786432 | tf_op jit(solution)/shard_map/all_to_all | solution.py:158
  37.3 4.5 %collective-permute-start = (bf16[6,8,256]{2,1,0:T(8,128)(2,1)S(1)}, bf16[6,8,256]{2,1,0:T(8,128)(2,1)S(1)}, u32[]{:S(2)}, u32[]{:S(2)}) collective-permute-start(bf16[6,8,256]{2,1,0:T(8,128)(2,1)S(1)} %shard_map.69), channel_id=1, source_target_pairs={{0,416},{1,384},{2,128},{3,352},{4,160},{5,448},{6,192},{7,480},{8... | collective-permute-start | bytes 73736 | tf_op jit(solution)/shard_map/ppermute | solution.py:206
  41.8 7.5 %collective-permute-done = bf16[6,8,256]{2,1,0:T(8,128)(2,1)S(1)} collective-permute-done((bf16[6,8,256]{2,1,0:T(8,128)(2,1)S(1)}, bf16[6,8,256]{2,1,0:T(8,128)(2,1)S(1)}, u32[]{:S(2)}, u32[]{:S(2)}) %collective-permute-start) | collective-permute-done | bytes 24608 | tf_op jit(solution)/shard_map/ppermute | solution.py:206
  49.3 0.8 broadcast_in_dim.5
  50.1 5.7 %all-to-all-start.2 = ((bf16[16,6,8,256]{3,2,1,0:T(8,128)(2,1)}), bf16[16,6,8,256]{3,2,1,0:T(8,128)(2,1)S(1)}, u32[]{:S(2)}, u32[]{:S(2)}) async-start(bf16[16,6,8,256]{3,2,1,0:T(8,128)(2,1)} %broadcast_in_dim.5), calls=%async_computation.2 | async-start | bytes 786432 | tf_op jit(solution)/shard_map/all_to_all | solution.py:155
  56.5 5.8 %all-gather.2 = f32[256,768]{1,0:T(8,128)S(1)} all-gather(f32[128,768]{1,0:T(8,128)S(1)} %slice-done), channel_id=4, replica_groups={{0,16},{32,48},{64,80},{96,112},{128,144},{160,176},{192,208},{224,240}..., dimensions={0}, use_global_device_ids=true | all-gather | bytes 1179648 | tf_op jit(solution)/shard_map/all_gather | solution.py:152
  62.4 2.4 %all-gather.3 = bf16[32,6,8,256]{3,2,1,0:T(8,128)(2,1)S(1)} all-gather(bf16[16,6,8,256]{3,2,1,0:T(8,128)(2,1)S(1)} %all-to-all-done.1), channel_id=5, replica_groups={{0,16},{32,48},{64,80},{96,112},{128,144},{160,176},{192,208},{224,240}..., dimensions={0}, use_global_device_ids=true | all-gather | bytes 1179648 | tf_op jit(solution)/shard_map/all_gather | solution.py:152
  64.7 1.1 copy.9
  66.0 1.2 copy.10.refs_4_
  67.2 3.4 %shard_map.70 = bf16[16,80,256]{2,1,0:T(8,128)(2,1)} custom-call(s32[16]{0:T(128)S(1)} %dynamic-slice_bitcast_fusion.chip_ref, f32[2,128,768]{2,1,0:T(8,128)S(1)} %bitcast.20, f32[2,128,768]{2,1,0:T(8,128)S(1)} %bitcast.21, f32[2,128,768]{2,1,0:T(8,128)S(1)} %bitcast.22, bf16[16,6,8,256]{3,2,1,0:T(8,128)(2,1)S(1)} %all-to-all-done.2.refs_3_, ...), custom_call_target="tpu_custom_call" | custom-call | tf_op jit(solution)/shard_map/pallas_call | solution.py:217
  70.5 6.7 %all-to-all-start.3 = ((bf16[16,80,256]{2,1,0:T(8,128)(2,1)}), bf16[16,80,256]{2,1,0:T(8,128)(2,1)S(1)}, u32[]{:S(2)}, u32[]{:S(2)}) async-start(bf16[16,80,256]{2,1,0:T(8,128)(2,1)} %shard_map.70), calls=%async_computation.3 | async-start | bytes 1310720 | tf_op jit(solution)/shard_map/all_to_all | solution.py:158
  77.2 0.7 fusion
  78.0 16.4 %all-to-all-done.3.arrived_ref = bf16[16,80,256]{2,1,0:T(8,128)(2,1)S(1)} async-done(((bf16[16,80,256]{2,1,0:T(8,128)(2,1)}), bf16[16,80,256]{2,1,0:T(8,128)(2,1)S(1)}, u32[]{:S(2)}, u32[]{:S(2)}) %all-to-all-start.3) | async-done | bytes 655392 | tf_op jit(solution)/shard_map/all_to_all | solution.py:158
  94.4 0.7 shard_map.71
  95.1 7.4 %all-to-all-start.4 = ((bf16[16,32,256]{2,1,0:T(8,128)(2,1)}), bf16[16,32,256]{2,1,0:T(8,128)(2,1)S(1)}, u32[]{:S(2)}, u32[]{:S(2)}) async-start(bf16[16,32,256]{2,1,0:T(8,128)(2,1)} %get-tuple-element.25), calls=%async_computation.4 | async-start | bytes 524288 | tf_op jit(solution)/shard_map/all_to_all | solution.py:155
  102.6 4.7 %all-gather.4 = f32[96,256]{1,0:T(8,128)S(1)} all-gather(f32[48,256]{1,0:T(8,128)S(1)} %get-tuple-element.24), channel_id=6, replica_groups={{0,16},{32,48},{64,80},{96,112},{128,144},{160,176},{192,208},{224,240}..., dimensions={0}, use_global_device_ids=true | all-gather | bytes 147456 | tf_op jit(solution)/shard_map/all_gather | solution.py:152
  107.9 3.9 %all-to-all-done.4 = bf16[16,32,256]{2,1,0:T(8,128)(2,1)S(1)} async-done(((bf16[16,32,256]{2,1,0:T(8,128)(2,1)}), bf16[16,32,256]{2,1,0:T(8,128)(2,1)S(1)}, u32[]{:S(2)}, u32[]{:S(2)}) %all-to-all-start.4) | async-done | bytes 262176 | tf_op jit(solution)/shard_map/all_to_all | solution.py:155
  111.9 5.9 %all-gather.5 = f32[64,256]{1,0:T(8,128)S(1)} all-gather(f32[32,256]{1,0:T(8,128)S(1)} %convert_reduce_fusion), channel_id=7, replica_groups={{0,16},{32,48},{64,80},{96,112},{128,144},{160,176},{192,208},{224,240}..., dimensions={0}, use_global_device_ids=true | all-gather | bytes 98304 | tf_op jit(solution)/shard_map/all_gather | solution.py:152
  (18 shorter events, 2.5 us)
Async XLA Ops:
  0.6 13.8 %copy-start.1 = (f32[384,768]{1,0:T(8,128)S(1)}, f32[384,768]{1,0:T(8,128)}, u32[]{:S(2)}) copy-start(f32[384,768]{1,0:T(8,128)} %param.8) | copy-start | bytes 3538948
  3.4 22.8 %all-to-all-start = ((bf16[32,8,384]{2,1,0:T(8,128)(2,1)}), bf16[32,8,384]{2,1,0:T(8,128)(2,1)S(1)}, u32[]{:S(2)}, u32[]{:S(2)}) async-start(bf16[32,8,384]{2,1,0:T(8,128)(2,1)} %shard_map.68), calls=%async_computation | async-start | bytes 393216 | tf_op jit(solution)/shard_map/all_to_all | solution.py:189
  27.1 22.2 %all-to-all-start.1 = ((bf16[16,6,8,256]{3,2,1,0:T(8,128)(2,1)}), bf16[16,6,8,256]{3,2,1,0:T(8,128)(2,1)S(1)}, u32[]{:S(2)}, u32[]{:S(2)}) async-start(bf16[16,6,8,256]{3,2,1,0:T(8,128)(2,1)} %broadcast_in_dim.4), calls=%async_computation.1 | async-start | bytes 786432 | tf_op jit(solution)/shard_map/all_to_all | solution.py:158
  37.3 19.2 %slice-start = ((f32[384,768]{1,0:T(8,128)}), f32[128,768]{1,0:T(8,128)S(1)}, s32[]{:S(2)}) async-start(f32[384,768]{1,0:T(8,128)} %param.8), calls=%async_computation.5 | async-start | bytes 786432 | tf_op jit(solution)/shard_map/slice | solution.py:209
  37.3 12.0 %collective-permute-start = (bf16[6,8,256]{2,1,0:T(8,128)(2,1)S(1)}, bf16[6,8,256]{2,1,0:T(8,128)(2,1)S(1)}, u32[]{:S(2)}, u32[]{:S(2)}) collective-permute-start(bf16[6,8,256]{2,1,0:T(8,128)(2,1)S(1)} %shard_map.69), channel_id=1, source_target_pairs={{0,416},{1,384},{2,128},{3,352},{4,160},{5,448},{6,192},{7,480},{8... | collective-permute-start | bytes 73736 | tf_op jit(solution)/shard_map/ppermute | solution.py:206
  50.1 17.0 %all-to-all-start.2 = ((bf16[16,6,8,256]{3,2,1,0:T(8,128)(2,1)}), bf16[16,6,8,256]{3,2,1,0:T(8,128)(2,1)S(1)}, u32[]{:S(2)}, u32[]{:S(2)}) async-start(bf16[16,6,8,256]{3,2,1,0:T(8,128)(2,1)} %broadcast_in_dim.5), calls=%async_computation.2 | async-start | bytes 786432 | tf_op jit(solution)/shard_map/all_to_all | solution.py:155
  70.5 6.7 %copy-start = (f32[512,512]{1,0:T(8,128)S(1)}, f32[512,512]{1,0:T(8,128)}, u32[]{:S(2)}) copy-start(f32[512,512]{1,0:T(8,128)} %refs_2_.1) | copy-start | bytes 3145732
  70.5 23.9 %all-to-all-start.3 = ((bf16[16,80,256]{2,1,0:T(8,128)(2,1)}), bf16[16,80,256]{2,1,0:T(8,128)(2,1)S(1)}, u32[]{:S(2)}, u32[]{:S(2)}) async-start(bf16[16,80,256]{2,1,0:T(8,128)(2,1)} %shard_map.70), calls=%async_computation.3 | async-start | bytes 1310720 | tf_op jit(solution)/shard_map/all_to_all | solution.py:158
  95.1 16.7 %all-to-all-start.4 = ((bf16[16,32,256]{2,1,0:T(8,128)(2,1)}), bf16[16,32,256]{2,1,0:T(8,128)(2,1)S(1)}, u32[]{:S(2)}, u32[]{:S(2)}) async-start(bf16[16,32,256]{2,1,0:T(8,128)(2,1)} %get-tuple-element.25), calls=%async_computation.4 | async-start | bytes 524288 | tf_op jit(solution)/shard_map/all_to_all | solution.py:155

commit v10 on v9

--- a/solution.py
+++ b/solution.py
@@ -13,6 +13,7 @@
 TAG = 128
 SMEM = pl.BlockSpec(memory_space=pltpu.SMEM)
 VMEM = pl.BlockSpec(memory_space=pltpu.VMEM)
+ANY = pl.BlockSpec(memory_space=pl.ANY)
 PARAMS = pltpu.CompilerParams(vmem_limit_bytes=16 * 2**20)
 FETCHING = pltpu.CompilerParams(vmem_limit_bytes=60 * 2**20)
 
@@ -61,12 +62,24 @@
     return table
 
 
-def scale_kernel(panel_blocks, slots_ref, rows_ref, factor_ref, out_ref, scaled_ref):
+def scale_kernel(panel_blocks, slots_ref, rows_hbm, factor_hbm, out_ref, rows_ref, factor_ref, scaled_ref, sems):
     half = factor_ref.shape[1] // 2
-    high, low = split(factor_ref[...])
-    rows = rows_ref[...]
-    scaled_ref[...] = dot(rows, high) + dot(rows, low)
+    parts = [pl.ds(k * half, half) for k in range(2)]
+    copies = [pltpu.make_async_copy(rows_hbm, rows_ref, sems.at[0])]
+    for k, part in enumerate(parts):
+        copies.append(
+            pltpu.make_async_copy(factor_hbm.at[part], factor_ref.at[part], sems.at[k + 1])
+        )
+    for copy in copies:
+        copy.start()
     out_ref[...] = jnp.zeros_like(out_ref)
+    copies[0].wait()
+    for k, part in enumerate(parts):
+        copies[k + 1].wait()
+        high, low = split(factor_ref[part, :])
+        rows = rows_ref[:, part]
+        scaled = dot(rows, high) + dot(rows, low)
+        scaled_ref[...] = scaled if k == 0 else scaled_ref[...] + scaled
     slot_count = slots_ref.shape[0]
     height = rows_ref.shape[0] // slot_count
     for s in range(slot_count):
@@ -95,7 +108,17 @@
             out_ref[n, :, lanes : lanes + TAG] = total.astype(BF16)
 
 
-def product_kernel(chip_ref, *refs):
+def turn_kernel(halves_ref, out_ref, rows_ref):
+    _, chunks, blocks, height, half = halves_ref.shape
+    for k in range(2):
+        for c in range(chunks):
+            for b in range(blocks):
+                first = (b * chunks + c) * height
+                rows_ref[first : first + height, :] = halves_ref[k, c, b].astype(F32)
+        out_ref[k * half : (k + 1) * half, :] = rows_ref[...].T.astype(BF16)
+
+
+def product_kernel(col_ref, chip_ref, *refs):
     *tile_refs, parts_ref, factor_ref, out_ref, panel_ref, high_ref, low_ref, sent_ref = refs
     chunks, blocks, height, half = parts_ref.shape
     for b, ref in enumerate(tile_refs):
@@ -106,7 +129,7 @@
     for c in range(chunks):
         for b in range(blocks):
             first = (b * chunks + c) * height
-            panel_ref[first : first + height, :] = parts_ref[chip_ref[c], b].astype(F32)
+            panel_ref[first : first + height, :] = parts_ref[chip_ref[col_ref[0] * chunks + c], b].astype(F32)
     panel = panel_ref[...].astype(BF16)
     sums = dot(high_ref[...], panel) + dot(low_ref[...], panel)
     gram = dot(factor_ref[...], sums.astype(BF16))
@@ -146,7 +169,8 @@
     same_core = [[2 * j + k for j in range(chip_count)] for k in range(2)]
     core_pairs = [[2 * j, 2 * j + 1] for j in range(chip_count)]
     table = short_routes(chip_count, col_count)
-    chip_arg = lax.dynamic_index_in_dim(jnp.asarray(table), col_index, 0, keepdims=False)
+    chip_arg = jnp.asarray(table.reshape(-1))
+    col_arg = jnp.reshape(col_index, (1,)).astype(jnp.int32)
 
     def pair_gather(x):
         return lax.all_gather(x, "row", axis=0, axis_index_groups=core_pairs)
@@ -171,9 +195,14 @@
     by_panel = pl.pallas_call(
         lambda *refs: scale_kernel(panel_blocks, *refs),
         out_shape=jax.ShapeDtypeStruct((row_count, chunk_rows, half + TAG), BF16),
-        in_specs=[SMEM, VMEM, VMEM],
-        out_specs=VMEM,
-        scratch_shapes=[pltpu.VMEM((slot_count * chunk_rows, width), F32)],
+        in_specs=[SMEM, ANY, ANY],
+        out_specs=VMEM,
+        scratch_shapes=[
+            pltpu.VMEM((slot_count * chunk_rows, width), BF16),
+            pltpu.VMEM((width, width), F32),
+            pltpu.VMEM((slot_count * chunk_rows, width), F32),
+            pltpu.SemaphoreType.DMA((3,)),
+        ],
         compiler_params=FETCHING,
     )(
         slot_blocks,
@@ -209,15 +238,21 @@
         (factor, pair_gather(tile[tile_rows - block_rows :]))
     )
     tiles.append(last_tile)
-    tile_factor = pair_gather(factor)
-    tile_factor = tile_factor.transpose(0, 4, 2, 1, 3).reshape(width, 2 * tile_rows)
+    tile_factor = pl.pallas_call(
+        turn_kernel,
+        out_shape=jax.ShapeDtypeStruct((width, 2 * tile_rows), BF16),
+        in_specs=[VMEM],
+        out_specs=VMEM,
+        scratch_shapes=[pltpu.VMEM((2 * tile_rows, half), F32)],
+        compiler_params=PARAMS,
+    )(pair_gather(factor))
     parts = over_row(jnp.broadcast_to(turned[None], (chip_count, *turned.shape)))
 
     sent = (col_count, diag_width + 2 * share, half)
     sent = pl.pallas_call(
         product_kernel,
         out_shape=jax.ShapeDtypeStruct(sent, BF16),
-        in_specs=[SMEM] + [VMEM] * (len(tiles) + 2),
+        in_specs=[SMEM, SMEM] + [VMEM] * (len(tiles) + 2),
         out_specs=VMEM,
         scratch_shapes=[
             pltpu.VMEM((panel_rows, half), F32),
@@ -226,7 +261,7 @@
             pltpu.VMEM(sent, F32),
         ],
         compiler_params=pltpu.CompilerParams(vmem_limit_bytes=50 * 2**20),
-    )(chip_arg, *tiles, parts, tile_factor)
+    )(col_arg, chip_arg, *tiles, parts, tile_factor)
     totals, copies = pl.pallas_call(
         total_kernel,
         out_shape=(

time: 119 us -> 120 us (level)
  local copies, waits for them, and re-layouts: 4.78 us -> 2.57 us
  waiting for transfers between devices: 34.8 us -> 36 us
  transfers between devices with their start and end apart: 6 -> 6, of which waited for: 4 -> 5; matrix products, arithmetic and copies ran while one was open for 4% -> 1% of each run, Pallas kernels for 0% -> 0%
where the time goes in v10:
time: 120 us; the launch traced here: 119 us
  starting transfers between devices  46.1 us (38%)
  waiting for transfers between devices  36 us (30%)
  blocking collectives  23.7 us (20%)
  Pallas kernels  7.75 us (6%)
  local copies, waits for them, and re-layouts  2.57 us (2%)
  other arithmetic  1.32 us (1%)
    all_gather x6, blocking collectives, pair_gather(): return lax.all_gather(x, 'row', axis=0, axis_index_groups=core_pairs)  23.7 us
    all_to_all x2, starting transfers between devices, over_col(): return lax.all_to_all(x, 'col', 0, 0, tiled=True)  17.2 us
    all_to_all x2, waiting for transfers between devices, over_col(): return lax.all_to_all(x, 'col', 0, 0, tiled=True)  16.4 us
    all_to_all x2, starting transfers between devices, over_row(): lax.all_to_all(x, 'row', 0, 0, tiled=True, axis_index_groups=same_core)  13.3 us
    all_to_all x1, starting transfers between devices, body(): lax.all_to_all(by_panel, 'row', 0, 0, tiled=True)  11.2 us
    ppermute x1, waiting for transfers between devices, body(): turned = lax.ppermute(piece, ('row', 'col'), route)  7.68 us
    all_to_all x1, waiting for transfers between devices, body(): lax.all_to_all(by_panel, 'row', 0, 0, tiled=True)  6.89 us
    all_to_all x2, waiting for transfers between devices, over_row(): lax.all_to_all(x, 'row', 0, 0, tiled=True, axis_index_groups=same_core)  5.03 us
  transfers between devices with their start and end apart: 6, of which 5 were waited for; matrix products, arithmetic and copies ran while one was open for 1% of the time, Pallas kernels for 0%

profile of v10, /device:TPU:1, one launch (start us, length us, event | category | flops | bytes accessed | tf_op | source)
XLA Modules:
  0.0 119.1 jit_solution(6279992444396320874)
XLA Ops:
  0.6 3.2 %shard_map.68 = bf16[32,8,384]{2,1,0:T(8,128)(2,1)} custom-call(s32[16]{0:T(128)} %refs_0_.1, bf16[128,512]{1,0:T(8,128)(2,1)} %bitcast.17, f32[512,512]{1,0:T(8,128)} %refs_2_.1), custom_call_target="tpu_custom_call" | custom-call | tf_op jit(solution)/shard_map/pallas_call | solution.py:195
  3.8 11.2 %all-to-all-start = ((bf16[32,8,384]{2,1,0:T(8,128)(2,1)}), bf16[32,8,384]{2,1,0:T(8,128)(2,1)S(1)}, u32[]{:S(2)}, u32[]{:S(2)}) async-start(bf16[32,8,384]{2,1,0:T(8,128)(2,1)} %shard_map.68), calls=%async_computation | async-start | bytes 393216 | tf_op jit(solution)/shard_map/all_to_all | solution.py:218
  15.1 2.4 %all-gather = f32[256,768]{1,0:T(8,128)S(1)} all-gather(f32[128,768]{1,0:T(8,128)S(1)} %get-tuple-element.27), channel_id=2, replica_groups={{0,16},{32,48},{64,80},{96,112},{128,144},{160,176},{192,208},{224,240}..., dimensions={0}, use_global_device_ids=true | all-gather | bytes 1179648 | tf_op jit(solution)/shard_map/all_gather | solution.py:176
  17.5 2.4 %all-gather.1 = f32[256,768]{1,0:T(8,128)S(1)} all-gather(f32[128,768]{1,0:T(8,128)S(1)} %get-tuple-element.26), channel_id=3, replica_groups={{0,16},{32,48},{64,80},{96,112},{128,144},{160,176},{192,208},{224,240}..., dimensions={0}, use_global_device_ids=true | all-gather | bytes 1179648 | tf_op jit(solution)/shard_map/all_gather | solution.py:176
  19.8 6.9 %all-to-all-done.taken_ref = bf16[32,8,384]{2,1,0:T(8,128)(2,1)S(1)} async-done(((bf16[32,8,384]{2,1,0:T(8,128)(2,1)}), bf16[32,8,384]{2,1,0:T(8,128)(2,1)S(1)}, u32[]{:S(2)}, u32[]{:S(2)}) %all-to-all-start) | async-done | bytes 196640 | tf_op jit(solution)/shard_map/all_to_all | solution.py:218
  26.9 0.8 broadcast_in_dim.4
  27.7 10.2 %all-to-all-start.1 = ((bf16[16,6,8,256]{3,2,1,0:T(8,128)(2,1)}), bf16[16,6,8,256]{3,2,1,0:T(8,128)(2,1)S(1)}, u32[]{:S(2)}, u32[]{:S(2)}) async-start(bf16[16,6,8,256]{3,2,1,0:T(8,128)(2,1)} %broadcast_in_dim.4), calls=%async_computation.1 | async-start | bytes 786432 | tf_op jit(solution)/shard_map/all_to_all | solution.py:182
  37.9 4.3 %collective-permute-start = (bf16[6,8,256]{2,1,0:T(8,128)(2,1)S(1)}, bf16[6,8,256]{2,1,0:T(8,128)(2,1)S(1)}, u32[]{:S(2)}, u32[]{:S(2)}) collective-permute-start(bf16[6,8,256]{2,1,0:T(8,128)(2,1)S(1)} %shard_map.69), channel_id=1, source_target_pairs={{0,416},{1,384},{2,128},{3,352},{4,160},{5,448},{6,192},{7,480},{8... | collective-permute-start | bytes 73736 | tf_op jit(solution)/shard_map/ppermute | solution.py:235
  42.2 7.7 %collective-permute-done = bf16[6,8,256]{2,1,0:T(8,128)(2,1)S(1)} collective-permute-done((bf16[6,8,256]{2,1,0:T(8,128)(2,1)S(1)}, bf16[6,8,256]{2,1,0:T(8,128)(2,1)S(1)}, u32[]{:S(2)}, u32[]{:S(2)}) %collective-permute-start) | collective-permute-done | bytes 24608 | tf_op jit(solution)/shard_map/ppermute | solution.py:235
  49.9 0.8 broadcast_in_dim.5
  50.7 5.9 %all-to-all-start.2 = ((bf16[16,6,8,256]{3,2,1,0:T(8,128)(2,1)}), bf16[16,6,8,256]{3,2,1,0:T(8,128)(2,1)S(1)}, u32[]{:S(2)}, u32[]{:S(2)}) async-start(bf16[16,6,8,256]{3,2,1,0:T(8,128)(2,1)} %broadcast_in_dim.5), calls=%async_computation.2 | async-start | bytes 786432 | tf_op jit(solution)/shard_map/all_to_all | solution.py:179
  56.7 5.9 %all-gather.2 = f32[256,768]{1,0:T(8,128)S(1)} all-gather(f32[128,768]{1,0:T(8,128)S(1)} %slice.31), channel_id=4, replica_groups={{0,16},{32,48},{64,80},{96,112},{128,144},{160,176},{192,208},{224,240}..., dimensions={0}, use_global_device_ids=true | all-gather | bytes 1179648 | tf_op jit(solution)/shard_map/all_gather | solution.py:176
  62.6 2.5 %all-gather.3 = bf16[32,6,8,256]{3,2,1,0:T(8,128)(2,1)S(1)} all-gather(bf16[16,6,8,256]{3,2,1,0:T(8,128)(2,1)S(1)} %all-to-all-done.1), channel_id=5, replica_groups={{0,16},{32,48},{64,80},{96,112},{128,144},{160,176},{192,208},{224,240}..., dimensions={0}, use_global_device_ids=true | all-gather | bytes 1179648 | tf_op jit(solution)/shard_map/all_gather | solution.py:176
  65.3 0.9 copy-done
  66.2 1.1 all-to-all-done.2.refs_3_
  67.3 3.4 %shard_map.71 = bf16[16,80,256]{2,1,0:T(8,128)(2,1)} custom-call(s32[1]{0:T(128)} %bitcast.3.col_ref, s32[256]{0:T(256)S(1)} %copy-done.1, f32[2,128,768]{2,1,0:T(8,128)S(1)} %bitcast.12, f32[2,128,768]{2,1,0:T(8,128)S(1)} %bitcast.13, f32[2,128,768]{2,1,0:T(8,128)S(1)} %bitcast.14, bf16[16,6,8,256]{3,2,1,0:T(8,128)(2,1)S(1)} %all-to-all-done.2.refs_3_, ...), custom_call_target="tpu_custom_call" | custom-call | tf_op jit(solution)/shard_map/pallas_call | solution.py:252
  70.7 7.1 %all-to-all-start.3 = ((bf16[16,80,256]{2,1,0:T(8,128)(2,1)}), bf16[16,80,256]{2,1,0:T(8,128)(2,1)S(1)}, u32[]{:S(2)}, u32[]{:S(2)}) async-start(bf16[16,80,256]{2,1,0:T(8,128)(2,1)} %shard_map.71), calls=%async_computation.3 | async-start | bytes 1310720 | tf_op jit(solution)/shard_map/all_to_all | solution.py:182
  77.8 0.7 fusion
  78.6 16.4 %all-to-all-done.3.arrived_ref = bf16[16,80,256]{2,1,0:T(8,128)(2,1)S(1)} async-done(((bf16[16,80,256]{2,1,0:T(8,128)(2,1)}), bf16[16,80,256]{2,1,0:T(8,128)(2,1)S(1)}, u32[]{:S(2)}, u32[]{:S(2)}) %all-to-all-start.3) | async-done | bytes 655392 | tf_op jit(solution)/shard_map/all_to_all | solution.py:182
  95.0 0.7 shard_map.72
  95.7 7.4 %all-to-all-start.4 = ((bf16[16,32,256]{2,1,0:T(8,128)(2,1)}), bf16[16,32,256]{2,1,0:T(8,128)(2,1)S(1)}, u32[]{:S(2)}, u32[]{:S(2)}) async-start(bf16[16,32,256]{2,1,0:T(8,128)(2,1)} %get-tuple-element.25), calls=%async_computation.4 | async-start | bytes 524288 | tf_op jit(solution)/shard_map/all_to_all | solution.py:179
  103.2 4.7 %all-gather.4 = f32[96,256]{1,0:T(8,128)S(1)} all-gather(f32[48,256]{1,0:T(8,128)S(1)} %get-tuple-element.24), channel_id=6, replica_groups={{0,16},{32,48},{64,80},{96,112},{128,144},{160,176},{192,208},{224,240}..., dimensions={0}, use_global_device_ids=true | all-gather | bytes 147456 | tf_op jit(solution)/shard_map/all_gather | solution.py:176
  108.5 3.9 %all-to-all-done.4 = bf16[16,32,256]{2,1,0:T(8,128)(2,1)S(1)} async-done(((bf16[16,32,256]{2,1,0:T(8,128)(2,1)}), bf16[16,32,256]{2,1,0:T(8,128)(2,1)S(1)}, u32[]{:S(2)}, u32[]{:S(2)}) %all-to-all-start.4) | async-done | bytes 262176 | tf_op jit(solution)/shard_map/all_to_all | solution.py:179
  112.5 5.9 %all-gather.5 = f32[64,256]{1,0:T(8,128)S(1)} all-gather(f32[32,256]{1,0:T(8,128)S(1)} %convert_reduce_fusion), channel_id=7, replica_groups={{0,16},{32,48},{64,80},{96,112},{128,144},{160,176},{192,208},{224,240}..., dimensions={0}, use_global_device_ids=true | all-gather | bytes 98304 | tf_op jit(solution)/shard_map/all_gather | solution.py:176
  (18 shorter events, 1.9 us)
Async XLA Ops:
  0.6 14.4 %copy-start.3 = (f32[384,768]{1,0:T(8,128)S(1)}, f32[384,768]{1,0:T(8,128)}, u32[]{:S(2)}) copy-start(f32[384,768]{1,0:T(8,128)} %param.8) | copy-start | bytes 3538948
  3.8 22.9 %all-to-all-start = ((bf16[32,8,384]{2,1,0:T(8,128)(2,1)}), bf16[32,8,384]{2,1,0:T(8,128)(2,1)S(1)}, u32[]{:S(2)}, u32[]{:S(2)}) async-start(bf16[32,8,384]{2,1,0:T(8,128)(2,1)} %shard_map.68), calls=%async_computation | async-start | bytes 393216 | tf_op jit(solution)/shard_map/all_to_all | solution.py:218
  27.7 22.2 %all-to-all-start.1 = ((bf16[16,6,8,256]{3,2,1,0:T(8,128)(2,1)}), bf16[16,6,8,256]{3,2,1,0:T(8,128)(2,1)S(1)}, u32[]{:S(2)}, u32[]{:S(2)}) async-start(bf16[16,6,8,256]{3,2,1,0:T(8,128)(2,1)} %broadcast_in_dim.4), calls=%async_computation.1 | async-start | bytes 786432 | tf_op jit(solution)/shard_map/all_to_all | solution.py:182
  37.9 12.0 %collective-permute-start = (bf16[6,8,256]{2,1,0:T(8,128)(2,1)S(1)}, bf16[6,8,256]{2,1,0:T(8,128)(2,1)S(1)}, u32[]{:S(2)}, u32[]{:S(2)}) collective-permute-start(bf16[6,8,256]{2,1,0:T(8,128)(2,1)S(1)} %shard_map.69), channel_id=1, source_target_pairs={{0,416},{1,384},{2,128},{3,352},{4,160},{5,448},{6,192},{7,480},{8... | collective-permute-start | bytes 73736 | tf_op jit(solution)/shard_map/ppermute | solution.py:235
  50.7 16.6 %all-to-all-start.2 = ((bf16[16,6,8,256]{3,2,1,0:T(8,128)(2,1)}), bf16[16,6,8,256]{3,2,1,0:T(8,128)(2,1)S(1)}, u32[]{:S(2)}, u32[]{:S(2)}) async-start(bf16[16,6,8,256]{3,2,1,0:T(8,128)(2,1)} %broadcast_in_dim.5), calls=%async_computation.2 | async-start | bytes 786432 | tf_op jit(solution)/shard_map/all_to_all | solution.py:179
  62.6 4.8 %copy-start.1 = (s32[256]{0:T(256)S(1)}, s32[256]{0:T(256)}, u32[]{:S(2)}) copy-start(s32[256]{0:T(256)} %constant.31.clone.chip_ref) | copy-start | bytes 3076
  65.3 0.9 copy-start
  70.7 7.1 %copy-start.2 = (f32[512,512]{1,0:T(8,128)S(1)}, f32[512,512]{1,0:T(8,128)}, u32[]{:S(2)}) copy-start(f32[512,512]{1,0:T(8,128)} %refs_2_.1) | copy-start | bytes 3145732
  70.7 24.3 %all-to-all-start.3 = ((bf16[16,80,256]{2,1,0:T(8,128)(2,1)}), bf16[16,80,256]{2,1,0:T(8,128)(2,1)S(1)}, u32[]{:S(2)}, u32[]{:S(2)}) async-start(bf16[16,80,256]{2,1,0:T(8,128)(2,1)} %shard_map.71), calls=%async_computation.3 | async-start | bytes 1310720 | tf_op jit(solution)/shard_map/all_to_all | solution.py:182
  95.7 16.7 %all-to-all-start.4 = ((bf16[16,32,256]{2,1,0:T(8,128)(2,1)}), bf16[16,32,256]{2,1,0:T(8,128)(2,1)S(1)}, u32[]{:S(2)}, u32[]{:S(2)}) async-start(bf16[16,32,256]{2,1,0:T(8,128)(2,1)} %get-tuple-element.25), calls=%async_computation.4 | async-start | bytes 524288 | tf_op jit(solution)/shard_map/all_to_all | solution.py:179

commit v11 on v7

--- a/solution.py
+++ b/solution.py
@@ -62,7 +62,7 @@
 
 
 def scale_kernel(panel_blocks, slots_ref, rows_ref, factor_ref, out_ref, scaled_ref):
-    half = factor_ref.shape[1] // 2
+    width = factor_ref.shape[1]
     high, low = split(factor_ref[...])
     rows = rows_ref[...]
     scaled_ref[...] = dot(rows, high) + dot(rows, low)
@@ -76,10 +76,8 @@
         def _():
             panel = block // panel_blocks
             number = (block - panel * panel_blocks + 1).astype(F32)
-            for k in range(2):
-                part = scaled_ref[s * height : (s + 1) * height, k * half : (k + 1) * half]
-                out_ref[2 * panel + k, :, :half] = part.astype(BF16)
-                out_ref[2 * panel + k, :, half:] = jnp.full((height, TAG), number, F32).astype(BF16)
+            out_ref[panel, :, :width] = scaled_ref[s * height : (s + 1) * height, :].astype(BF16)
+            out_ref[panel, :, width:] = jnp.full((height, TAG), number, F32).astype(BF16)
 
 
 def place_kernel(taken_ref, out_ref):
@@ -95,15 +93,55 @@
             out_ref[n, :, lanes : lanes + TAG] = total.astype(BF16)
 
 
-def product_kernel(chip_ref, tiles_ref, parts_ref, factor_ref, out_ref, panel_ref, sent_ref):
+def merge_kernel(core_ref, pair_ref, piece_ref, copies_ref):
+    half = piece_ref.shape[2]
+
+    def merge(first):
+        for b in range(piece_ref.shape[0]):
+            rows = [pair_ref[k, b, :, first : first + half].astype(F32) for k in range(2)]
+            rows = (rows[0] + rows[1]).astype(BF16)
+            piece_ref[b] = rows
+            for copy in range(copies_ref.shape[0]):
+                copies_ref[copy, b] = rows
+
+    @pl.when(core_ref[0] == 0)
+    def _():
+        merge(0)
+
+    @pl.when(core_ref[0] == 1)
+    def _():
+        merge(half)
+
+
+def turn_kernel(halves_ref, out_ref, rows_ref):
+    _, chunks, blocks, height, half = halves_ref.shape
+    for k in range(2):
+        for c in range(chunks):
+            for b in range(blocks):
+                first = (b * chunks + c) * height
+                rows_ref[first : first + height, :] = halves_ref[k, c, b].astype(F32)
+        out_ref[k * half : (k + 1) * half, :] = rows_ref[...].T.astype(BF16)
+
+
+def product_kernel(core_ref, col_ref, chip_ref, own_ref, *refs):
+    *tile_refs, parts_ref, factor_ref, out_ref, panel_ref, high_ref, sums_ref, sent_ref = refs
     chunks, blocks, height, half = parts_ref.shape
+    tile_rows = own_ref.shape[0]
+    for b, ref in enumerate(tile_refs):
+        rows = ref.shape[1]
+        for k in range(2):
+            first = k * tile_rows + b * rows
+            high_ref[first : first + rows, :] = ref[k]
+    low = split(own_ref[...])[1]
     for c in range(chunks):
         for b in range(blocks):
             first = (b * chunks + c) * height
-            panel_ref[first : first + height, :] = parts_ref[chip_ref[c], b].astype(F32)
+            panel_ref[first : first + height, :] = parts_ref[chip_ref[col_ref[0] * chunks + c], b].astype(F32)
     panel = panel_ref[...].astype(BF16)
-    high, low = split(tiles_ref[...])
-    sums = dot(high, panel) + dot(low, panel)
+    sums_ref[...] = dot(high_ref[...], panel)
+    own = pl.ds(pl.multiple_of(core_ref[0] * tile_rows, tile_rows), tile_rows)
+    sums_ref[own, :] = sums_ref[own, :] + dot(low, panel)
+    sums = sums_ref[...]
     gram = dot(factor_ref[...], sums.astype(BF16))
     rows = gram.shape[0] // chunks
     share = sums.shape[0] // 2 // chunks
@@ -141,7 +179,8 @@
     same_core = [[2 * j + k for j in range(chip_count)] for k in range(2)]
     core_pairs = [[2 * j, 2 * j + 1] for j in range(chip_count)]
     table = short_routes(chip_count, col_count)
-    chip_arg = lax.dynamic_index_in_dim(jnp.asarray(table), col_index, 0, keepdims=False)
+    chip_arg = jnp.asarray(table.reshape(-1))
+    col_arg = jnp.reshape(col_index, (1,)).astype(jnp.int32)
 
     def pair_gather(x):
         return lax.all_gather(x, "row", axis=0, axis_index_groups=core_pairs)
@@ -163,11 +202,9 @@
         )
     )
 
-    tiles = pair_gather(ancestor_inv).reshape(2 * tile_rows, panel_rows)
-
     by_panel = pl.pallas_call(
         lambda *refs: scale_kernel(panel_blocks, *refs),
-        out_shape=jax.ShapeDtypeStruct((row_count, chunk_rows, half + TAG), BF16),
+        out_shape=jax.ShapeDtypeStruct((chip_count, chunk_rows, width + TAG), BF16),
         in_specs=[SMEM, VMEM, VMEM],
         out_specs=VMEM,
         scratch_shapes=[pltpu.VMEM((slot_count * chunk_rows, width), F32)],
@@ -177,14 +214,30 @@
         front_rows.reshape(slot_count * chunk_rows, width),
         inv_factor,
     )
-    taken = lax.all_to_all(by_panel, "row", 0, 0, tiled=True)
-    piece = pl.pallas_call(
+    by_panel, tile = lax.optimization_barrier((by_panel, ancestor_inv))
+    high = tile.astype(BF16)
+    middle = tile_rows // 2
+    taken, core, *tiles = lax.optimization_barrier(
+        (over_row(by_panel), core, pair_gather(high[:middle]), pair_gather(high[middle:]))
+    )
+    core_arg = jnp.reshape(core, (1,)).astype(jnp.int32)
+    placed = pl.pallas_call(
         place_kernel,
-        out_shape=jax.ShapeDtypeStruct((panel_blocks, chunk_rows, half), BF16),
+        out_shape=jax.ShapeDtypeStruct((panel_blocks, chunk_rows, width), BF16),
         in_specs=[VMEM],
         out_specs=VMEM,
         compiler_params=PARAMS,
     )(taken)
+    piece, copies = pl.pallas_call(
+        merge_kernel,
+        out_shape=(
+            jax.ShapeDtypeStruct((panel_blocks, chunk_rows, half), BF16),
+            jax.ShapeDtypeStruct((col_count, panel_blocks, chunk_rows, half), BF16),
+        ),
+        in_specs=[SMEM, VMEM],
+        out_specs=(VMEM, VMEM),
+        compiler_params=PARAMS,
+    )(core_arg, pair_gather(placed))
 
     route = [
         ((2 * p + k) * col_count + c, (2 * int(table[p, c]) + k) * col_count + p)
@@ -193,23 +246,31 @@
         for c in range(col_count)
     ]
     turned = lax.ppermute(piece, ("row", "col"), route)
-    factor = over_col(jnp.broadcast_to(piece[None], (col_count, *piece.shape)))
-    tile_factor, tiles = lax.optimization_barrier((pair_gather(factor), tiles))
-    tile_factor = tile_factor.transpose(0, 4, 2, 1, 3).reshape(width, 2 * tile_rows)
+    factor = over_col(copies)
+    tile_factor = pl.pallas_call(
+        turn_kernel,
+        out_shape=jax.ShapeDtypeStruct((width, 2 * tile_rows), BF16),
+        in_specs=[VMEM],
+        out_specs=VMEM,
+        scratch_shapes=[pltpu.VMEM((2 * tile_rows, half), F32)],
+        compiler_params=PARAMS,
+    )(pair_gather(factor))
     parts = over_row(jnp.broadcast_to(turned[None], (chip_count, *turned.shape)))
 
     sent = (col_count, diag_width + 2 * share, half)
     sent = pl.pallas_call(
         product_kernel,
         out_shape=jax.ShapeDtypeStruct(sent, BF16),
-        in_specs=[SMEM, VMEM, VMEM, VMEM],
+        in_specs=[SMEM, SMEM, SMEM] + [VMEM] * (len(tiles) + 3),
         out_specs=VMEM,
         scratch_shapes=[
             pltpu.VMEM((panel_rows, half), F32),
+            pltpu.VMEM((2 * tile_rows, panel_rows), BF16),
+            pltpu.VMEM((2 * tile_rows, half), F32),
             pltpu.VMEM(sent, F32),
         ],
-        compiler_params=PARAMS,
-    )(chip_arg, tiles, parts, tile_factor)
+        compiler_params=pltpu.CompilerParams(vmem_limit_bytes=24 * 2**20),
+    )(core_arg, col_arg, chip_arg, tile, *tiles, parts, tile_factor)
     totals, copies = pl.pallas_call(
         total_kernel,
         out_shape=(
@@ -221,7 +282,7 @@
         compiler_params=PARAMS,
     )(over_col(sent))
     halves = pair_gather(totals).reshape(2, 2, share, half)
-    product = lax.dynamic_index_in_dim(halves, core, 1, keepdims=False)
+    product = jnp.where(core == 0, halves[:, 0], halves[:, 1])
     product = jnp.concatenate([product[0], product[1]], 1)
     gram_rows = pair_gather(jnp.sum(over_row(copies).astype(F32), axis=0))
     gram_rows = jnp.concatenate([gram_rows[0], gram_rows[1]], 1)

time: 133 us -> 119 us (0.89)
  blocking collectives: 39.5 us -> 24.3 us
  between operations: 14.1 us -> 0.77 us
  waiting for transfers between devices: 29.3 us -> 39.4 us
  starting transfers between devices: 35 us -> 43.3 us
  local copies, waits for them, and re-layouts: 5.81 us -> 0.85 us
    all_to_all x1 -> x0, blocking collectives: 23 us -> none  [body(): taken = lax.all_to_all(by_panel, 'row', 0, 0, tiled=True)]
    all_to_all x2 -> x3, waiting for transfers between devices: 3.74 us -> 13.3 us  [over_row(): lax.all_to_all(x, 'row', 0, 0, tiled=True, axis_index_groups=same_core)]
    all_to_all x2 -> x3, starting transfers between devices: 13.3 us -> 22.5 us  [over_row(): lax.all_to_all(x, 'row', 0, 0, tiled=True, axis_index_groups=same_core)]
    all_gather x3 -> x6, blocking collectives: 16.5 us -> 24.3 us  [pair_gather(): return lax.all_gather(x, 'row', axis=0, axis_index_groups=core_pairs)]
    ppermute x1, waiting for transfers between devices: 7.68 us -> 9.75 us  [body(): turned = lax.ppermute(piece, ('row', 'col'), route)]
    reshape x1 -> x0, local copies, waits for them, and re-layouts: 1.4 us -> none  [body(): tile_factor.transpose(0, 4, 2, 1, 3).reshape(width, 2 * tile_rows)]
  transfers between devices with their start and end apart: 6 -> 6, of which waited for: 4 -> 5; matrix products, arithmetic and copies ran while one was open for 5% -> 1% of each run, Pallas kernels for 2% -> 0%
where the time goes in v11:
time: 119 us; the launch traced here: 118 us
  starting transfers between devices  43.3 us (36%)
  waiting for transfers between devices  39.4 us (33%)
  blocking collectives  24.3 us (20%)
  Pallas kernels  7.35 us (6%)
  other arithmetic  1.38 us (1%)
    all_gather x6, blocking collectives, pair_gather(): return lax.all_gather(x, 'row', axis=0, axis_index_groups=core_pairs)  24.3 us
    all_to_all x3, starting transfers between devices, over_row(): lax.all_to_all(x, 'row', 0, 0, tiled=True, axis_index_groups=same_core)  22.5 us
    all_to_all x2, waiting for transfers between devices, over_col(): return lax.all_to_all(x, 'col', 0, 0, tiled=True)  16.4 us
    all_to_all x2, starting transfers between devices, over_col(): return lax.all_to_all(x, 'col', 0, 0, tiled=True)  16.4 us
    all_to_all x3, waiting for transfers between devices, over_row(): lax.all_to_all(x, 'row', 0, 0, tiled=True, axis_index_groups=same_core)  13.3 us
    ppermute x1, waiting for transfers between devices, body(): turned = lax.ppermute(piece, ('row', 'col'), route)  9.75 us
    ppermute x1, starting transfers between devices, body(): turned = lax.ppermute(piece, ('row', 'col'), route)  4.34 us
    pallas_call x1, Pallas kernels, body(): pl.pallas_call(product_kernel, out_shape=jax.ShapeDtypeStruct(sent, BF16)...  2.78 us
  transfers between devices with their start and end apart: 6, of which 5 were waited for; matrix products, arithmetic and copies ran while one was open for 1% of the time, Pallas kernels for 0%

profile of v11, /device:TPU:1, one launch (start us, length us, event | category | flops | bytes accessed | tf_op | source)
XLA Modules:
  0.0 118.1 jit_solution(16527035250243412624)
XLA Ops:
  0.6 2.6 %shard_map.68 = bf16[16,8,640]{2,1,0:T(8,128)(2,1)} custom-call(s32[16]{0:T(128)} %refs_0_.1, bf16[128,512]{1,0:T(8,128)(2,1)} %bitcast.18, f32[512,512]{1,0:T(8,128)} %refs_2_.1), custom_call_target="tpu_custom_call" | custom-call | tf_op jit(solution)/shard_map/pallas_call | solution.py:205
  3.2 10.2 %all-to-all-start = ((bf16[16,8,640]{2,1,0:T(8,128)(2,1)}), bf16[16,8,640]{2,1,0:T(8,128)(2,1)S(1)}, u32[]{:S(2)}, u32[]{:S(2)}) async-start(bf16[16,8,640]{2,1,0:T(8,128)(2,1)} %shard_map.68), calls=%async_computation | async-start | bytes 327680 | tf_op jit(solution)/shard_map/all_to_all | solution.py:189
  13.6 2.8 %all-gather = bf16[384,768]{1,0:T(8,128)(2,1)S(1)} all-gather(bf16[192,768]{1,0:T(8,128)(2,1)S(1)} %get-tuple-element.23), channel_id=2, replica_groups={{0,16},{32,48},{64,80},{96,112},{128,144},{160,176},{192,208},{224,240}..., dimensions={0}, use_global_device_ids=true | all-gather | bytes 884736 | tf_op jit(solution)/shard_map/all_gather | solution.py:186
  16.4 2.2 %all-gather.1 = bf16[384,768]{1,0:T(8,128)(2,1)S(1)} all-gather(bf16[192,768]{1,0:T(8,128)(2,1)S(1)} %get-tuple-element.22), channel_id=3, replica_groups={{0,16},{32,48},{64,80},{96,112},{128,144},{160,176},{192,208},{224,240}..., dimensions={0}, use_global_device_ids=true | all-gather | bytes 884736 | tf_op jit(solution)/shard_map/all_gather | solution.py:186
  18.6 3.8 %all-to-all-done.taken_ref = bf16[16,8,640]{2,1,0:T(8,128)(2,1)S(1)} async-done(((bf16[16,8,640]{2,1,0:T(8,128)(2,1)}), bf16[16,8,640]{2,1,0:T(8,128)(2,1)S(1)}, u32[]{:S(2)}, u32[]{:S(2)}) %all-to-all-start) | async-done | bytes 163872 | tf_op jit(solution)/shard_map/all_to_all | solution.py:189
  22.6 3.8 %all-gather.2 = bf16[12,8,512]{2,1,0:T(8,128)(2,1)S(1)} all-gather(bf16[6,8,512]{2,1,0:T(8,128)(2,1)S(1)} %shard_map.69), channel_id=4, replica_groups={{0,16},{32,48},{64,80},{96,112},{128,144},{160,176},{192,208},{224,240}..., dimensions={0}, use_global_device_ids=true | all-gather | bytes 147456 | tf_op jit(solution)/shard_map/all_gather | solution.py:186
  26.4 0.8 shard_map.70
  27.2 10.2 %all-to-all-start.2 = ((bf16[16,6,8,256]{3,2,1,0:T(8,128)(2,1)}), bf16[16,6,8,256]{3,2,1,0:T(8,128)(2,1)S(1)}, u32[]{:S(2)}, u32[]{:S(2)}) async-start(bf16[16,6,8,256]{3,2,1,0:T(8,128)(2,1)} %get-tuple-element.19), calls=%async_computation.2 | async-start | bytes 786432 | tf_op jit(solution)/shard_map/all_to_all | solution.py:192
  37.4 4.3 %collective-permute-start = (bf16[6,8,256]{2,1,0:T(8,128)(2,1)S(1)}, bf16[6,8,256]{2,1,0:T(8,128)(2,1)S(1)}, u32[]{:S(2)}, u32[]{:S(2)}) collective-permute-start(bf16[6,8,256]{2,1,0:T(8,128)(2,1)S(1)} %get-tuple-element.18), channel_id=1, source_target_pairs={{0,416},{1,384},{2,128},{3,352},{4,160},{5,448},{6,192},{7,480},{8... | collective-permute-start | bytes 73736 | tf_op jit(solution)/shard_map/ppermute | solution.py:248
  41.7 9.7 %collective-permute-done = bf16[6,8,256]{2,1,0:T(8,128)(2,1)S(1)} collective-permute-done((bf16[6,8,256]{2,1,0:T(8,128)(2,1)S(1)}, bf16[6,8,256]{2,1,0:T(8,128)(2,1)S(1)}, u32[]{:S(2)}, u32[]{:S(2)}) %collective-permute-start) | collective-permute-done | bytes 24608 | tf_op jit(solution)/shard_map/ppermute | solution.py:248
  51.5 0.8 broadcast_in_dim.2
  52.3 4.9 %all-to-all-start.1 = ((bf16[16,6,8,256]{3,2,1,0:T(8,128)(2,1)}), bf16[16,6,8,256]{3,2,1,0:T(8,128)(2,1)S(1)}, u32[]{:S(2)}, u32[]{:S(2)}) async-start(bf16[16,6,8,256]{3,2,1,0:T(8,128)(2,1)} %broadcast_in_dim.2), calls=%async_computation.1 | async-start | bytes 786432 | tf_op jit(solution)/shard_map/all_to_all | solution.py:189
  57.1 4.9 %all-gather.3 = bf16[32,6,8,256]{3,2,1,0:T(8,128)(2,1)S(1)} all-gather(bf16[16,6,8,256]{3,2,1,0:T(8,128)(2,1)S(1)} %all-to-all-done.2), channel_id=5, replica_groups={{0,16},{32,48},{64,80},{96,112},{128,144},{160,176},{192,208},{224,240}..., dimensions={0}, use_global_device_ids=true | all-gather | bytes 1179648 | tf_op jit(solution)/shard_map/all_gather | solution.py:186
  62.3 5.5 %all-to-all-done.1.refs_2_ = bf16[16,6,8,256]{3,2,1,0:T(8,128)(2,1)S(1)} async-done(((bf16[16,6,8,256]{3,2,1,0:T(8,128)(2,1)}), bf16[16,6,8,256]{3,2,1,0:T(8,128)(2,1)S(1)}, u32[]{:S(2)}, u32[]{:S(2)}) %all-to-all-start.1) | async-done | bytes 393248 | tf_op jit(solution)/shard_map/all_to_all | solution.py:189
  67.8 2.8 %shard_map.72 = bf16[16,80,256]{2,1,0:T(8,128)(2,1)} custom-call(s32[1]{0:T(128)} %bitcast.3.core_ref, s32[1]{0:T(128)} %bitcast.4.col_ref, s32[256]{0:T(256)S(1)} %copy-done.1, f32[384,768]{1,0:T(8,128)S(1)} %copy-done, bf16[2,192,768]{2,1,0:T(8,128)(2,1)S(1)} %bitcast.14, bf16[2,192,768]{2,1,0:T(8,128)(2,1)S(1)} %bitcast.15, ...), custom_call_target="tpu_custom_call" | custom-call | tf_op jit(solution)/shard_map/pallas_call | solution.py:261
  70.6 6.2 %all-to-all-start.3 = ((bf16[16,80,256]{2,1,0:T(8,128)(2,1)}), bf16[16,80,256]{2,1,0:T(8,128)(2,1)S(1)}, u32[]{:S(2)}, u32[]{:S(2)}) async-start(bf16[16,80,256]{2,1,0:T(8,128)(2,1)} %shard_map.72), calls=%async_computation.3 | async-start | bytes 1310720 | tf_op jit(solution)/shard_map/all_to_all | solution.py:192
  76.9 0.7 fusion
  77.6 16.4 %all-to-all-done.3.arrived_ref = bf16[16,80,256]{2,1,0:T(8,128)(2,1)S(1)} async-done(((bf16[16,80,256]{2,1,0:T(8,128)(2,1)}), bf16[16,80,256]{2,1,0:T(8,128)(2,1)S(1)}, u32[]{:S(2)}, u32[]{:S(2)}) %all-to-all-start.3) | async-done | bytes 655392 | tf_op jit(solution)/shard_map/all_to_all | solution.py:192
  94.0 0.7 shard_map.73
  94.8 7.4 %all-to-all-start.4 = ((bf16[16,32,256]{2,1,0:T(8,128)(2,1)}), bf16[16,32,256]{2,1,0:T(8,128)(2,1)S(1)}, u32[]{:S(2)}, u32[]{:S(2)}) async-start(bf16[16,32,256]{2,1,0:T(8,128)(2,1)} %get-tuple-element.21), calls=%async_computation.4 | async-start | bytes 524288 | tf_op jit(solution)/shard_map/all_to_all | solution.py:189
  102.2 4.7 %all-gather.4 = f32[96,256]{1,0:T(8,128)S(1)} all-gather(f32[48,256]{1,0:T(8,128)S(1)} %get-tuple-element.20), channel_id=6, replica_groups={{0,16},{32,48},{64,80},{96,112},{128,144},{160,176},{192,208},{224,240}..., dimensions={0}, use_global_device_ids=true | all-gather | bytes 147456 | tf_op jit(solution)/shard_map/all_gather | solution.py:186
  107.6 3.9 %all-to-all-done.4 = bf16[16,32,256]{2,1,0:T(8,128)(2,1)S(1)} async-done(((bf16[16,32,256]{2,1,0:T(8,128)(2,1)}), bf16[16,32,256]{2,1,0:T(8,128)(2,1)S(1)}, u32[]{:S(2)}, u32[]{:S(2)}) %all-to-all-start.4) | async-done | bytes 262176 | tf_op jit(solution)/shard_map/all_to_all | solution.py:189
  111.6 5.9 %all-gather.5 = f32[64,256]{1,0:T(8,128)S(1)} all-gather(f32[32,256]{1,0:T(8,128)S(1)} %convert_reduce_fusion), channel_id=7, replica_groups={{0,16},{32,48},{64,80},{96,112},{128,144},{160,176},{192,208},{224,240}..., dimensions={0}, use_global_device_ids=true | all-gather | bytes 98304 | tf_op jit(solution)/shard_map/all_gather | solution.py:186
  117.5 0.6 maximum_add_fusion
  (16 shorter events, 1.2 us)
Async XLA Ops:
  0.6 12.8 %copy-start = (f32[384,768]{1,0:T(8,128)S(1)}, f32[384,768]{1,0:T(8,128)}, u32[]{:S(2)}) copy-start(f32[384,768]{1,0:T(8,128)} %own_ref) | copy-start | bytes 3538948
  3.2 19.2 %all-to-all-start = ((bf16[16,8,640]{2,1,0:T(8,128)(2,1)}), bf16[16,8,640]{2,1,0:T(8,128)(2,1)S(1)}, u32[]{:S(2)}, u32[]{:S(2)}) async-start(bf16[16,8,640]{2,1,0:T(8,128)(2,1)} %shard_map.68), calls=%async_computation | async-start | bytes 327680 | tf_op jit(solution)/shard_map/all_to_all | solution.py:189
  27.2 24.3 %all-to-all-start.2 = ((bf16[16,6,8,256]{3,2,1,0:T(8,128)(2,1)}), bf16[16,6,8,256]{3,2,1,0:T(8,128)(2,1)S(1)}, u32[]{:S(2)}, u32[]{:S(2)}) async-start(bf16[16,6,8,256]{3,2,1,0:T(8,128)(2,1)} %get-tuple-element.19), calls=%async_computation.2 | async-start | bytes 786432 | tf_op jit(solution)/shard_map/all_to_all | solution.py:192
  37.4 14.1 %collective-permute-start = (bf16[6,8,256]{2,1,0:T(8,128)(2,1)S(1)}, bf16[6,8,256]{2,1,0:T(8,128)(2,1)S(1)}, u32[]{:S(2)}, u32[]{:S(2)}) collective-permute-start(bf16[6,8,256]{2,1,0:T(8,128)(2,1)S(1)} %get-tuple-element.18), channel_id=1, source_target_pairs={{0,416},{1,384},{2,128},{3,352},{4,160},{5,448},{6,192},{7,480},{8... | collective-permute-start | bytes 73736 | tf_op jit(solution)/shard_map/ppermute | solution.py:248
  52.3 15.5 %all-to-all-start.1 = ((bf16[16,6,8,256]{3,2,1,0:T(8,128)(2,1)}), bf16[16,6,8,256]{3,2,1,0:T(8,128)(2,1)S(1)}, u32[]{:S(2)}, u32[]{:S(2)}) async-start(bf16[16,6,8,256]{3,2,1,0:T(8,128)(2,1)} %broadcast_in_dim.2), calls=%async_computation.1 | async-start | bytes 786432 | tf_op jit(solution)/shard_map/all_to_all | solution.py:189
  57.1 10.7 %copy-start.1 = (s32[256]{0:T(256)S(1)}, s32[256]{0:T(256)}, u32[]{:S(2)}) copy-start(s32[256]{0:T(256)} %constant.31.clone.chip_ref) | copy-start | bytes 3076
  70.6 6.3 %copy-start.2 = (f32[512,512]{1,0:T(8,128)S(1)}, f32[512,512]{1,0:T(8,128)}, u32[]{:S(2)}) copy-start(f32[512,512]{1,0:T(8,128)} %refs_2_.1) | copy-start | bytes 3145732
  70.6 23.5 %all-to-all-start.3 = ((bf16[16,80,256]{2,1,0:T(8,128)(2,1)}), bf16[16,80,256]{2,1,0:T(8,128)(2,1)S(1)}, u32[]{:S(2)}, u32[]{:S(2)}) async-start(bf16[16,80,256]{2,1,0:T(8,128)(2,1)} %shard_map.72), calls=%async_computation.3 | async-start | bytes 1310720 | tf_op jit(solution)/shard_map/all_to_all | solution.py:192
  94.8 16.7 %all-to-all-start.4 = ((bf16[16,32,256]{2,1,0:T(8,128)(2,1)}), bf16[16,32,256]{2,1,0:T(8,128)(2,1)S(1)}, u32[]{:S(2)}, u32[]{:S(2)}) async-start(bf16[16,32,256]{2,1,0:T(8,128)(2,1)} %get-tuple-element.21), calls=%async_computation.4 | async-start | bytes 524288 | tf_op jit(solution)/shard_map/all_to_all | solution.py:189

commit v12 on v11

--- a/solution.py
+++ b/solution.py
@@ -217,8 +217,8 @@
     by_panel, tile = lax.optimization_barrier((by_panel, ancestor_inv))
     high = tile.astype(BF16)
     middle = tile_rows // 2
-    taken, core, *tiles = lax.optimization_barrier(
-        (over_row(by_panel), core, pair_gather(high[:middle]), pair_gather(high[middle:]))
+    taken, core, first_half = lax.optimization_barrier(
+        (over_row(by_panel), core, pair_gather(high[:middle]))
     )
     core_arg = jnp.reshape(core, (1,)).astype(jnp.int32)
     placed = pl.pallas_call(
@@ -246,7 +246,8 @@
         for c in range(col_count)
     ]
     turned = lax.ppermute(piece, ("row", "col"), route)
-    factor = over_col(copies)
+    factor, second_half = lax.optimization_barrier((over_col(copies), pair_gather(high[middle:])))
+    tiles = [first_half, second_half]
     tile_factor = pl.pallas_call(
         turn_kernel,
         out_shape=jax.ShapeDtypeStruct((width, 2 * tile_rows), BF16),

time: 119 us -> 119 us (level)
  transfers between devices with their start and end apart: 6 -> 6, of which waited for: 5 -> 5; matrix products, arithmetic and copies ran while one was open for 1% -> 2% of each run, Pallas kernels for 0% -> 0%
where the time goes in v12:
time: 119 us; the launch traced here: 118 us
  starting transfers between devices  43.2 us (36%)
  waiting for transfers between devices  38.7 us (33%)
  blocking collectives  24.5 us (21%)
  Pallas kernels  7.31 us (6%)
  local copies, waits for them, and re-layouts  1.56 us (1%)
  other arithmetic  1.38 us (1%)
    all_gather x6, blocking collectives, pair_gather(): return lax.all_gather(x, 'row', axis=0, axis_index_groups=core_pairs)  24.5 us
    all_to_all x3, starting transfers between devices, over_row(): lax.all_to_all(x, 'row', 0, 0, tiled=True, axis_index_groups=same_core)  22.5 us
    all_to_all x2, waiting for transfers between devices, over_col(): return lax.all_to_all(x, 'col', 0, 0, tiled=True)  16.4 us
    all_to_all x2, starting transfers between devices, over_col(): return lax.all_to_all(x, 'col', 0, 0, tiled=True)  16.4 us
    all_to_all x3, waiting for transfers between devices, over_row(): lax.all_to_all(x, 'row', 0, 0, tiled=True, axis_index_groups=same_core)  12.4 us
    ppermute x1, waiting for transfers between devices, body(): turned = lax.ppermute(piece, ('row', 'col'), route)  9.8 us
    ppermute x1, starting transfers between devices, body(): turned = lax.ppermute(piece, ('row', 'col'), route)  4.29 us
    pallas_call x1, Pallas kernels, body(): pl.pallas_call(product_kernel, out_shape=jax.ShapeDtypeStruct(sent, BF16)...  2.77 us
  transfers between devices with their start and end apart: 6, of which 5 were waited for; matrix products, arithmetic and copies ran while one was open for 2% of the time, Pallas kernels for 0%

profile of v12, /device:TPU:1, one launch (start us, length us, event | category | flops | bytes accessed | tf_op | source)
XLA Modules:
  0.0 118.1 jit_solution(6364574476247420811)
XLA Ops:
  0.6 2.6 %shard_map.68 = bf16[16,8,640]{2,1,0:T(8,128)(2,1)} custom-call(s32[16]{0:T(128)} %refs_0_.1, bf16[128,512]{1,0:T(8,128)(2,1)} %bitcast.18, f32[512,512]{1,0:T(8,128)} %refs_2_.1), custom_call_target="tpu_custom_call" | custom-call | tf_op jit(solution)/shard_map/pallas_call | solution.py:205
  3.2 10.2 %all-to-all-start = ((bf16[16,8,640]{2,1,0:T(8,128)(2,1)}), bf16[16,8,640]{2,1,0:T(8,128)(2,1)S(1)}, u32[]{:S(2)}, u32[]{:S(2)}) async-start(bf16[16,8,640]{2,1,0:T(8,128)(2,1)} %shard_map.68), calls=%async_computation | async-start | bytes 327680 | tf_op jit(solution)/shard_map/all_to_all | solution.py:189
  13.5 0.7 fusion.3
  14.3 2.8 %all-gather = bf16[384,768]{1,0:T(8,128)(2,1)S(1)} all-gather(bf16[192,768]{1,0:T(8,128)(2,1)S(1)} %get-tuple-element.25), channel_id=2, replica_groups={{0,16},{32,48},{64,80},{96,112},{128,144},{160,176},{192,208},{224,240}..., dimensions={0}, use_global_device_ids=true | all-gather | bytes 884736 | tf_op jit(solution)/shard_map/all_gather | solution.py:186
  17.1 5.3 %all-to-all-done.taken_ref = bf16[16,8,640]{2,1,0:T(8,128)(2,1)S(1)} async-done(((bf16[16,8,640]{2,1,0:T(8,128)(2,1)}), bf16[16,8,640]{2,1,0:T(8,128)(2,1)S(1)}, u32[]{:S(2)}, u32[]{:S(2)}) %all-to-all-start) | async-done | bytes 163872 | tf_op jit(solution)/shard_map/all_to_all | solution.py:189
  22.6 3.9 %all-gather.1 = bf16[12,8,512]{2,1,0:T(8,128)(2,1)S(1)} all-gather(bf16[6,8,512]{2,1,0:T(8,128)(2,1)S(1)} %shard_map.69), channel_id=3, replica_groups={{0,16},{32,48},{64,80},{96,112},{128,144},{160,176},{192,208},{224,240}..., dimensions={0}, use_global_device_ids=true | all-gather | bytes 147456 | tf_op jit(solution)/shard_map/all_gather | solution.py:186
  26.4 0.8 shard_map.70
  27.2 10.2 %all-to-all-start.1 = ((bf16[16,6,8,256]{3,2,1,0:T(8,128)(2,1)}), bf16[16,6,8,256]{3,2,1,0:T(8,128)(2,1)S(1)}, u32[]{:S(2)}, u32[]{:S(2)}) async-start(bf16[16,6,8,256]{3,2,1,0:T(8,128)(2,1)} %get-tuple-element.18), calls=%async_computation.1 | async-start | bytes 786432 | tf_op jit(solution)/shard_map/all_to_all | solution.py:192
  37.4 4.3 %collective-permute-start = (bf16[6,8,256]{2,1,0:T(8,128)(2,1)S(1)}, bf16[6,8,256]{2,1,0:T(8,128)(2,1)S(1)}, u32[]{:S(2)}, u32[]{:S(2)}) collective-permute-start(bf16[6,8,256]{2,1,0:T(8,128)(2,1)S(1)} %get-tuple-element.20), channel_id=1, source_target_pairs={{0,416},{1,384},{2,128},{3,352},{4,160},{5,448},{6,192},{7,480},{8... | collective-permute-start | bytes 73736 | tf_op jit(solution)/shard_map/ppermute | solution.py:248
  41.7 9.8 %collective-permute-done = bf16[6,8,256]{2,1,0:T(8,128)(2,1)S(1)} collective-permute-done((bf16[6,8,256]{2,1,0:T(8,128)(2,1)S(1)}, bf16[6,8,256]{2,1,0:T(8,128)(2,1)S(1)}, u32[]{:S(2)}, u32[]{:S(2)}) %collective-permute-start) | collective-permute-done | bytes 24608 | tf_op jit(solution)/shard_map/ppermute | solution.py:248
  51.5 0.8 broadcast_in_dim.2
  52.3 4.9 %all-to-all-start.2 = ((bf16[16,6,8,256]{3,2,1,0:T(8,128)(2,1)}), bf16[16,6,8,256]{3,2,1,0:T(8,128)(2,1)S(1)}, u32[]{:S(2)}, u32[]{:S(2)}) async-start(bf16[16,6,8,256]{3,2,1,0:T(8,128)(2,1)} %broadcast_in_dim.2), calls=%async_computation.2 | async-start | bytes 786432 | tf_op jit(solution)/shard_map/all_to_all | solution.py:189
  57.2 4.7 %all-gather.2 = bf16[384,768]{1,0:T(8,128)(2,1)S(1)} all-gather(bf16[192,768]{1,0:T(8,128)(2,1)S(1)} %copy-done.3), channel_id=4, replica_groups={{0,16},{32,48},{64,80},{96,112},{128,144},{160,176},{192,208},{224,240}..., dimensions={0}, use_global_device_ids=true | all-gather | bytes 884736 | tf_op jit(solution)/shard_map/all_gather | solution.py:186
  61.9 2.5 %all-gather.3 = bf16[32,6,8,256]{3,2,1,0:T(8,128)(2,1)S(1)} all-gather(bf16[16,6,8,256]{3,2,1,0:T(8,128)(2,1)S(1)} %all-to-all-done.1), channel_id=5, replica_groups={{0,16},{32,48},{64,80},{96,112},{128,144},{160,176},{192,208},{224,240}..., dimensions={0}, use_global_device_ids=true | all-gather | bytes 1179648 | tf_op jit(solution)/shard_map/all_gather | solution.py:186
  64.6 3.2 %all-to-all-done.2.refs_2_ = bf16[16,6,8,256]{3,2,1,0:T(8,128)(2,1)S(1)} async-done(((bf16[16,6,8,256]{3,2,1,0:T(8,128)(2,1)}), bf16[16,6,8,256]{3,2,1,0:T(8,128)(2,1)S(1)}, u32[]{:S(2)}, u32[]{:S(2)}) %all-to-all-start.2) | async-done | bytes 393248 | tf_op jit(solution)/shard_map/all_to_all | solution.py:189
  67.8 2.8 %shard_map.72 = bf16[16,80,256]{2,1,0:T(8,128)(2,1)} custom-call(s32[1]{0:T(128)} %bitcast.2.core_ref, s32[1]{0:T(128)} %bitcast.3.col_ref, s32[256]{0:T(256)S(1)} %copy-done.1, f32[384,768]{1,0:T(8,128)S(1)} %copy-done, bf16[2,192,768]{2,1,0:T(8,128)(2,1)S(1)} %bitcast.14, bf16[2,192,768]{2,1,0:T(8,128)(2,1)S(1)} %bitcast.15, ...), custom_call_target="tpu_custom_call" | custom-call | tf_op jit(solution)/shard_map/pallas_call | solution.py:262
  70.6 6.2 %all-to-all-start.3 = ((bf16[16,80,256]{2,1,0:T(8,128)(2,1)}), bf16[16,80,256]{2,1,0:T(8,128)(2,1)S(1)}, u32[]{:S(2)}, u32[]{:S(2)}) async-start(bf16[16,80,256]{2,1,0:T(8,128)(2,1)} %shard_map.72), calls=%async_computation.3 | async-start | bytes 1310720 | tf_op jit(solution)/shard_map/all_to_all | solution.py:192
  76.9 0.7 fusion
  77.6 16.4 %all-to-all-done.3.arrived_ref = bf16[16,80,256]{2,1,0:T(8,128)(2,1)S(1)} async-done(((bf16[16,80,256]{2,1,0:T(8,128)(2,1)}), bf16[16,80,256]{2,1,0:T(8,128)(2,1)S(1)}, u32[]{:S(2)}, u32[]{:S(2)}) %all-to-all-start.3) | async-done | bytes 655392 | tf_op jit(solution)/shard_map/all_to_all | solution.py:192
  94.0 0.7 shard_map.73
  94.8 7.4 %all-to-all-start.4 = ((bf16[16,32,256]{2,1,0:T(8,128)(2,1)}), bf16[16,32,256]{2,1,0:T(8,128)(2,1)S(1)}, u32[]{:S(2)}, u32[]{:S(2)}) async-start(bf16[16,32,256]{2,1,0:T(8,128)(2,1)} %get-tuple-element.23), calls=%async_computation.4 | async-start | bytes 524288 | tf_op jit(solution)/shard_map/all_to_all | solution.py:189
  102.2 4.7 %all-gather.4 = f32[96,256]{1,0:T(8,128)S(1)} all-gather(f32[48,256]{1,0:T(8,128)S(1)} %get-tuple-element.22), channel_id=6, replica_groups={{0,16},{32,48},{64,80},{96,112},{128,144},{160,176},{192,208},{224,240}..., dimensions={0}, use_global_device_ids=true | all-gather | bytes 147456 | tf_op jit(solution)/shard_map/all_gather | solution.py:186
  107.6 3.9 %all-to-all-done.4 = bf16[16,32,256]{2,1,0:T(8,128)(2,1)S(1)} async-done(((bf16[16,32,256]{2,1,0:T(8,128)(2,1)}), bf16[16,32,256]{2,1,0:T(8,128)(2,1)S(1)}, u32[]{:S(2)}, u32[]{:S(2)}) %all-to-all-start.4) | async-done | bytes 262176 | tf_op jit(solution)/shard_map/all_to_all | solution.py:189
  111.5 5.9 %all-gather.5 = f32[64,256]{1,0:T(8,128)S(1)} all-gather(f32[32,256]{1,0:T(8,128)S(1)} %convert_reduce_fusion), channel_id=7, replica_groups={{0,16},{32,48},{64,80},{96,112},{128,144},{160,176},{192,208},{224,240}..., dimensions={0}, use_global_device_ids=true | all-gather | bytes 98304 | tf_op jit(solution)/shard_map/all_gather | solution.py:186
  (18 shorter events, 1.8 us)
Async XLA Ops:
  0.6 12.8 %copy-start = (f32[384,768]{1,0:T(8,128)S(1)}, f32[384,768]{1,0:T(8,128)}, u32[]{:S(2)}) copy-start(f32[384,768]{1,0:T(8,128)} %own_ref) | copy-start | bytes 3538948
  3.2 19.2 %all-to-all-start = ((bf16[16,8,640]{2,1,0:T(8,128)(2,1)}), bf16[16,8,640]{2,1,0:T(8,128)(2,1)S(1)}, u32[]{:S(2)}, u32[]{:S(2)}) async-start(bf16[16,8,640]{2,1,0:T(8,128)(2,1)} %shard_map.68), calls=%async_computation | async-start | bytes 327680 | tf_op jit(solution)/shard_map/all_to_all | solution.py:189
  22.4 34.8 %copy-start.3 = (bf16[192,768]{1,0:T(8,128)(2,1)S(1)}, bf16[192,768]{1,0:T(8,128)(2,1)}, u32[]{:S(2)}) copy-start(bf16[192,768]{1,0:T(8,128)(2,1)} %get-tuple-element.24) | copy-start | bytes 884740
  27.2 24.3 %all-to-all-start.1 = ((bf16[16,6,8,256]{3,2,1,0:T(8,128)(2,1)}), bf16[16,6,8,256]{3,2,1,0:T(8,128)(2,1)S(1)}, u32[]{:S(2)}, u32[]{:S(2)}) async-start(bf16[16,6,8,256]{3,2,1,0:T(8,128)(2,1)} %get-tuple-element.18), calls=%async_computation.1 | async-start | bytes 786432 | tf_op jit(solution)/shard_map/all_to_all | solution.py:192
  37.4 14.1 %collective-permute-start = (bf16[6,8,256]{2,1,0:T(8,128)(2,1)S(1)}, bf16[6,8,256]{2,1,0:T(8,128)(2,1)S(1)}, u32[]{:S(2)}, u32[]{:S(2)}) collective-permute-start(bf16[6,8,256]{2,1,0:T(8,128)(2,1)S(1)} %get-tuple-element.20), channel_id=1, source_target_pairs={{0,416},{1,384},{2,128},{3,352},{4,160},{5,448},{6,192},{7,480},{8... | collective-permute-start | bytes 73736 | tf_op jit(solution)/shard_map/ppermute | solution.py:248
  52.3 15.5 %all-to-all-start.2 = ((bf16[16,6,8,256]{3,2,1,0:T(8,128)(2,1)}), bf16[16,6,8,256]{3,2,1,0:T(8,128)(2,1)S(1)}, u32[]{:S(2)}, u32[]{:S(2)}) async-start(bf16[16,6,8,256]{3,2,1,0:T(8,128)(2,1)} %broadcast_in_dim.2), calls=%async_computation.2 | async-start | bytes 786432 | tf_op jit(solution)/shard_map/all_to_all | solution.py:189
  61.9 6.0 %copy-start.1 = (s32[256]{0:T(256)S(1)}, s32[256]{0:T(256)}, u32[]{:S(2)}) copy-start(s32[256]{0:T(256)} %constant.31.clone.chip_ref) | copy-start | bytes 3076
  70.6 6.3 %copy-start.2 = (f32[512,512]{1,0:T(8,128)S(1)}, f32[512,512]{1,0:T(8,128)}, u32[]{:S(2)}) copy-start(f32[512,512]{1,0:T(8,128)} %refs_2_.1) | copy-start | bytes 3145732
  70.6 23.4 %all-to-all-start.3 = ((bf16[16,80,256]{2,1,0:T(8,128)(2,1)}), bf16[16,80,256]{2,1,0:T(8,128)(2,1)S(1)}, u32[]{:S(2)}, u32[]{:S(2)}) async-start(bf16[16,80,256]{2,1,0:T(8,128)(2,1)} %shard_map.72), calls=%async_computation.3 | async-start | bytes 1310720 | tf_op jit(solution)/shard_map/all_to_all | solution.py:192
  94.8 16.7 %all-to-all-start.4 = ((bf16[16,32,256]{2,1,0:T(8,128)(2,1)}), bf16[16,32,256]{2,1,0:T(8,128)(2,1)S(1)}, u32[]{:S(2)}, u32[]{:S(2)}) async-start(bf16[16,32,256]{2,1,0:T(8,128)(2,1)} %get-tuple-element.23), calls=%async_computation.4 | async-start | bytes 524288 | tf_op jit(solution)/shard_map/all_to_all | solution.py:189

commit v13 on v12

--- a/solution.py
+++ b/solution.py
@@ -62,7 +62,7 @@
 
 
 def scale_kernel(panel_blocks, slots_ref, rows_ref, factor_ref, out_ref, scaled_ref):
-    width = factor_ref.shape[1]
+    half = factor_ref.shape[1] // 2
     high, low = split(factor_ref[...])
     rows = rows_ref[...]
     scaled_ref[...] = dot(rows, high) + dot(rows, low)
@@ -76,11 +76,13 @@
         def _():
             panel = block // panel_blocks
             number = (block - panel * panel_blocks + 1).astype(F32)
-            out_ref[panel, :, :width] = scaled_ref[s * height : (s + 1) * height, :].astype(BF16)
-            out_ref[panel, :, width:] = jnp.full((height, TAG), number, F32).astype(BF16)
-
-
-def place_kernel(taken_ref, out_ref):
+            for k in range(2):
+                part = scaled_ref[s * height : (s + 1) * height, k * half : (k + 1) * half]
+                out_ref[2 * panel + k, :, :half] = part.astype(BF16)
+                out_ref[2 * panel + k, :, half:] = jnp.full((height, TAG), number, F32).astype(BF16)
+
+
+def place_kernel(taken_ref, out_ref, copies_ref):
     width = taken_ref.shape[2] - TAG
     sources = range(taken_ref.shape[0])
     for lanes in range(0, width, TAG):
@@ -90,27 +92,10 @@
             value = taken_ref[s, :, lanes : lanes + TAG].astype(F32)
             totals = [t + jnp.where(tag == n + 1, value, 0.0) for n, t in enumerate(totals)]
         for n, total in enumerate(totals):
-            out_ref[n, :, lanes : lanes + TAG] = total.astype(BF16)
-
-
-def merge_kernel(core_ref, pair_ref, piece_ref, copies_ref):
-    half = piece_ref.shape[2]
-
-    def merge(first):
-        for b in range(piece_ref.shape[0]):
-            rows = [pair_ref[k, b, :, first : first + half].astype(F32) for k in range(2)]
-            rows = (rows[0] + rows[1]).astype(BF16)
-            piece_ref[b] = rows
+            rows = total.astype(BF16)
+            out_ref[n, :, lanes : lanes + TAG] = rows
             for copy in range(copies_ref.shape[0]):
-                copies_ref[copy, b] = rows
-
-    @pl.when(core_ref[0] == 0)
-    def _():
-        merge(0)
-
-    @pl.when(core_ref[0] == 1)
-    def _():
-        merge(half)
+                copies_ref[copy, n, :, lanes : lanes + TAG] = rows
 
 
 def turn_kernel(halves_ref, out_ref, rows_ref):
@@ -204,7 +189,7 @@
 
     by_panel = pl.pallas_call(
         lambda *refs: scale_kernel(panel_blocks, *refs),
-        out_shape=jax.ShapeDtypeStruct((chip_count, chunk_rows, width + TAG), BF16),
+        out_shape=jax.ShapeDtypeStruct((row_count, chunk_rows, half + TAG), BF16),
         in_specs=[SMEM, VMEM, VMEM],
         out_specs=VMEM,
         scratch_shapes=[pltpu.VMEM((slot_count * chunk_rows, width), F32)],
@@ -218,26 +203,23 @@
     high = tile.astype(BF16)
     middle = tile_rows // 2
     taken, core, first_half = lax.optimization_barrier(
-        (over_row(by_panel), core, pair_gather(high[:middle]))
+        (
+            lax.all_to_all(by_panel, "row", 0, 0, tiled=True),
+            core,
+            pair_gather(high[:middle]),
+        )
     )
     core_arg = jnp.reshape(core, (1,)).astype(jnp.int32)
-    placed = pl.pallas_call(
+    piece, copies = pl.pallas_call(
         place_kernel,
-        out_shape=jax.ShapeDtypeStruct((panel_blocks, chunk_rows, width), BF16),
-        in_specs=[VMEM],
-        out_specs=VMEM,
-        compiler_params=PARAMS,
-    )(taken)
-    piece, copies = pl.pallas_call(
-        merge_kernel,
         out_shape=(
             jax.ShapeDtypeStruct((panel_blocks, chunk_rows, half), BF16),
             jax.ShapeDtypeStruct((col_count, panel_blocks, chunk_rows, half), BF16),
         ),
-        in_specs=[SMEM, VMEM],
+        in_specs=[VMEM],
         out_specs=(VMEM, VMEM),
         compiler_params=PARAMS,
-    )(core_arg, pair_gather(placed))
+    )(taken)
 
     route = [
         ((2 * p + k) * col_count + c, (2 * int(table[p, c]) + k) * col_count + p)

time: 119 us -> 119 us (level)
  blocking collectives: 24.5 us -> 21.3 us
  starting transfers between devices: 43.2 us -> 46.2 us
    all_to_all x0 -> x1, starting transfers between devices: none -> 11.2 us  [body(): lax.all_to_all(by_panel, 'row', 0, 0, tiled=True)]
    all_to_all x3 -> x2, starting transfers between devices: 22.5 us -> 13.4 us  [over_row(): lax.all_to_all(x, 'row', 0, 0, tiled=True, axis_index_groups=same_core)]
    all_to_all x0 -> x1, waiting for transfers between devices: none -> 8.65 us  [body(): lax.all_to_all(by_panel, 'row', 0, 0, tiled=True)]
    all_to_all x3 -> x2, waiting for transfers between devices: 12.4 us -> 5.9 us  [over_row(): lax.all_to_all(x, 'row', 0, 0, tiled=True, axis_index_groups=same_core)]
    all_gather x6 -> x5, blocking collectives: 24.5 us -> 21.3 us  [pair_gather(): return lax.all_gather(x, 'row', axis=0, axis_index_groups=core_pairs)]
    ppermute x1, waiting for transfers between devices: 9.8 us -> 7.68 us  [body(): turned = lax.ppermute(piece, ('row', 'col'), route)]
where the time goes in v13:
time: 119 us; the launch traced here: 118 us
  starting transfers between devices  46.2 us (39%)
  waiting for transfers between devices  38.7 us (33%)
  blocking collectives  21.3 us (18%)
  Pallas kernels  7.32 us (6%)
  local copies, waits for them, and re-layouts  1.56 us (1%)
  other arithmetic  1.38 us (1%)
    all_gather x5, blocking collectives, pair_gather(): return lax.all_gather(x, 'row', axis=0, axis_index_groups=core_pairs)  21.3 us
    all_to_all x2, starting transfers between devices, over_col(): return lax.all_to_all(x, 'col', 0, 0, tiled=True)  17.2 us
    all_to_all x2, waiting for transfers between devices, over_col(): return lax.all_to_all(x, 'col', 0, 0, tiled=True)  16.4 us
    all_to_all x2, starting transfers between devices, over_row(): lax.all_to_all(x, 'row', 0, 0, tiled=True, axis_index_groups=same_core)  13.4 us
    all_to_all x1, starting transfers between devices, body(): lax.all_to_all(by_panel, 'row', 0, 0, tiled=True)  11.2 us
    all_to_all x1, waiting for transfers between devices, body(): lax.all_to_all(by_panel, 'row', 0, 0, tiled=True)  8.65 us
    ppermute x1, waiting for transfers between devices, body(): turned = lax.ppermute(piece, ('row', 'col'), route)  7.68 us
    all_to_all x2, waiting for transfers between devices, over_row(): lax.all_to_all(x, 'row', 0, 0, tiled=True, axis_index_groups=same_core)  5.9 us
  transfers between devices with their start and end apart: 6, of which 5 were waited for; matrix products, arithmetic and copies ran while one was open for 2% of the time, Pallas kernels for 0%

profile of v13, /device:TPU:1, one launch (start us, length us, event | category | flops | bytes accessed | tf_op | source)
XLA Modules:
  0.0 117.9 jit_solution(4137411351748105303)
XLA Ops:
  0.6 2.6 %shard_map.68 = bf16[32,8,384]{2,1,0:T(8,128)(2,1)} custom-call(s32[16]{0:T(128)} %refs_0_.1, bf16[128,512]{1,0:T(8,128)(2,1)} %bitcast.16, f32[512,512]{1,0:T(8,128)} %refs_2_.1), custom_call_target="tpu_custom_call" | custom-call | tf_op jit(solution)/shard_map/pallas_call | solution.py:190
  3.2 11.2 %all-to-all-start = ((bf16[32,8,384]{2,1,0:T(8,128)(2,1)}), bf16[32,8,384]{2,1,0:T(8,128)(2,1)S(1)}, u32[]{:S(2)}, u32[]{:S(2)}) async-start(bf16[32,8,384]{2,1,0:T(8,128)(2,1)} %shard_map.68), calls=%async_computation | async-start | bytes 393216 | tf_op jit(solution)/shard_map/all_to_all | solution.py:207
  14.5 0.7 fusion.3
  15.3 2.2 %all-gather = bf16[384,768]{1,0:T(8,128)(2,1)S(1)} all-gather(bf16[192,768]{1,0:T(8,128)(2,1)S(1)} %get-tuple-element.25), channel_id=2, replica_groups={{0,16},{32,48},{64,80},{96,112},{128,144},{160,176},{192,208},{224,240}..., dimensions={0}, use_global_device_ids=true | all-gather | bytes 884736 | tf_op jit(solution)/shard_map/all_gather | solution.py:171
  17.5 8.6 %all-to-all-done.taken_ref = bf16[32,8,384]{2,1,0:T(8,128)(2,1)S(1)} async-done(((bf16[32,8,384]{2,1,0:T(8,128)(2,1)}), bf16[32,8,384]{2,1,0:T(8,128)(2,1)S(1)}, u32[]{:S(2)}, u32[]{:S(2)}) %all-to-all-start) | async-done | bytes 196640 | tf_op jit(solution)/shard_map/all_to_all | solution.py:207
  26.1 1.0 shard_map.69
  27.1 10.2 %all-to-all-start.1 = ((bf16[16,6,8,256]{3,2,1,0:T(8,128)(2,1)}), bf16[16,6,8,256]{3,2,1,0:T(8,128)(2,1)S(1)}, u32[]{:S(2)}, u32[]{:S(2)}) async-start(bf16[16,6,8,256]{3,2,1,0:T(8,128)(2,1)} %get-tuple-element.18), calls=%async_computation.1 | async-start | bytes 786432 | tf_op jit(solution)/shard_map/all_to_all | solution.py:177
  37.3 4.3 %collective-permute-start = (bf16[6,8,256]{2,1,0:T(8,128)(2,1)S(1)}, bf16[6,8,256]{2,1,0:T(8,128)(2,1)S(1)}, u32[]{:S(2)}, u32[]{:S(2)}) collective-permute-start(bf16[6,8,256]{2,1,0:T(8,128)(2,1)S(1)} %get-tuple-element.20), channel_id=1, source_target_pairs={{0,416},{1,384},{2,128},{3,352},{4,160},{5,448},{6,192},{7,480},{8... | collective-permute-start | bytes 73736 | tf_op jit(solution)/shard_map/ppermute | solution.py:230
  41.6 7.7 %collective-permute-done = bf16[6,8,256]{2,1,0:T(8,128)(2,1)S(1)} collective-permute-done((bf16[6,8,256]{2,1,0:T(8,128)(2,1)S(1)}, bf16[6,8,256]{2,1,0:T(8,128)(2,1)S(1)}, u32[]{:S(2)}, u32[]{:S(2)}) %collective-permute-start) | collective-permute-done | bytes 24608 | tf_op jit(solution)/shard_map/ppermute | solution.py:230
  49.3 0.8 broadcast_in_dim.2
  50.1 5.9 %all-to-all-start.2 = ((bf16[16,6,8,256]{3,2,1,0:T(8,128)(2,1)}), bf16[16,6,8,256]{3,2,1,0:T(8,128)(2,1)S(1)}, u32[]{:S(2)}, u32[]{:S(2)}) async-start(bf16[16,6,8,256]{3,2,1,0:T(8,128)(2,1)} %broadcast_in_dim.2), calls=%async_computation.2 | async-start | bytes 786432 | tf_op jit(solution)/shard_map/all_to_all | solution.py:174
  56.0 6.0 %all-gather.1 = bf16[384,768]{1,0:T(8,128)(2,1)S(1)} all-gather(bf16[192,768]{1,0:T(8,128)(2,1)} %get-tuple-element.24), channel_id=3, replica_groups={{0,16},{32,48},{64,80},{96,112},{128,144},{160,176},{192,208},{224,240}..., dimensions={0}, use_global_device_ids=true | all-gather | bytes 884736 | tf_op jit(solution)/shard_map/all_gather | solution.py:171
  62.0 2.5 %all-gather.2 = bf16[32,6,8,256]{3,2,1,0:T(8,128)(2,1)S(1)} all-gather(bf16[16,6,8,256]{3,2,1,0:T(8,128)(2,1)S(1)} %all-to-all-done.1), channel_id=4, replica_groups={{0,16},{32,48},{64,80},{96,112},{128,144},{160,176},{192,208},{224,240}..., dimensions={0}, use_global_device_ids=true | all-gather | bytes 1179648 | tf_op jit(solution)/shard_map/all_gather | solution.py:171
  64.8 2.0 %all-to-all-done.2.refs_2_ = bf16[16,6,8,256]{3,2,1,0:T(8,128)(2,1)S(1)} async-done(((bf16[16,6,8,256]{3,2,1,0:T(8,128)(2,1)}), bf16[16,6,8,256]{3,2,1,0:T(8,128)(2,1)S(1)}, u32[]{:S(2)}, u32[]{:S(2)}) %all-to-all-start.2) | async-done | bytes 393248 | tf_op jit(solution)/shard_map/all_to_all | solution.py:174
  66.7 2.8 %shard_map.71 = bf16[16,80,256]{2,1,0:T(8,128)(2,1)} custom-call(s32[1]{0:T(128)} %bitcast.2.core_ref, s32[1]{0:T(128)} %bitcast.3.col_ref, s32[256]{0:T(256)S(1)} %copy-done.1, f32[384,768]{1,0:T(8,128)S(1)} %copy-done, bf16[2,192,768]{2,1,0:T(8,128)(2,1)S(1)} %bitcast.13, bf16[2,192,768]{2,1,0:T(8,128)(2,1)S(1)} %bitcast.14, ...), custom_call_target="tpu_custom_call" | custom-call | tf_op jit(solution)/shard_map/pallas_call | solution.py:244
  69.5 7.1 %all-to-all-start.3 = ((bf16[16,80,256]{2,1,0:T(8,128)(2,1)}), bf16[16,80,256]{2,1,0:T(8,128)(2,1)S(1)}, u32[]{:S(2)}, u32[]{:S(2)}) async-start(bf16[16,80,256]{2,1,0:T(8,128)(2,1)} %shard_map.71), calls=%async_computation.3 | async-start | bytes 1310720 | tf_op jit(solution)/shard_map/all_to_all | solution.py:177
  76.6 0.7 fusion
  77.4 16.4 %all-to-all-done.3.arrived_ref = bf16[16,80,256]{2,1,0:T(8,128)(2,1)S(1)} async-done(((bf16[16,80,256]{2,1,0:T(8,128)(2,1)}), bf16[16,80,256]{2,1,0:T(8,128)(2,1)S(1)}, u32[]{:S(2)}, u32[]{:S(2)}) %all-to-all-start.3) | async-done | bytes 655392 | tf_op jit(solution)/shard_map/all_to_all | solution.py:177
  93.8 0.7 shard_map.72
  94.5 7.5 %all-to-all-start.4 = ((bf16[16,32,256]{2,1,0:T(8,128)(2,1)}), bf16[16,32,256]{2,1,0:T(8,128)(2,1)S(1)}, u32[]{:S(2)}, u32[]{:S(2)}) async-start(bf16[16,32,256]{2,1,0:T(8,128)(2,1)} %get-tuple-element.23), calls=%async_computation.4 | async-start | bytes 524288 | tf_op jit(solution)/shard_map/all_to_all | solution.py:174
  102.0 4.7 %all-gather.3 = f32[96,256]{1,0:T(8,128)S(1)} all-gather(f32[48,256]{1,0:T(8,128)S(1)} %get-tuple-element.22), channel_id=5, replica_groups={{0,16},{32,48},{64,80},{96,112},{128,144},{160,176},{192,208},{224,240}..., dimensions={0}, use_global_device_ids=true | all-gather | bytes 147456 | tf_op jit(solution)/shard_map/all_gather | solution.py:171
  107.3 3.9 %all-to-all-done.4 = bf16[16,32,256]{2,1,0:T(8,128)(2,1)S(1)} async-done(((bf16[16,32,256]{2,1,0:T(8,128)(2,1)}), bf16[16,32,256]{2,1,0:T(8,128)(2,1)S(1)}, u32[]{:S(2)}, u32[]{:S(2)}) %all-to-all-start.4) | async-done | bytes 262176 | tf_op jit(solution)/shard_map/all_to_all | solution.py:174
  111.3 5.9 %all-gather.4 = f32[64,256]{1,0:T(8,128)S(1)} all-gather(f32[32,256]{1,0:T(8,128)S(1)} %convert_reduce_fusion), channel_id=6, replica_groups={{0,16},{32,48},{64,80},{96,112},{128,144},{160,176},{192,208},{224,240}..., dimensions={0}, use_global_device_ids=true | all-gather | bytes 98304 | tf_op jit(solution)/shard_map/all_gather | solution.py:171
  117.2 0.6 maximum_add_fusion
  (14 shorter events, 1.0 us)
Async XLA Ops:
  0.6 13.8 %copy-start = (f32[384,768]{1,0:T(8,128)S(1)}, f32[384,768]{1,0:T(8,128)}, u32[]{:S(2)}) copy-start(f32[384,768]{1,0:T(8,128)} %own_ref) | copy-start | bytes 3538948
  3.2 22.9 %all-to-all-start = ((bf16[32,8,384]{2,1,0:T(8,128)(2,1)}), bf16[32,8,384]{2,1,0:T(8,128)(2,1)S(1)}, u32[]{:S(2)}, u32[]{:S(2)}) async-start(bf16[32,8,384]{2,1,0:T(8,128)(2,1)} %shard_map.68), calls=%async_computation | async-start | bytes 393216 | tf_op jit(solution)/shard_map/all_to_all | solution.py:207
  27.1 22.2 %all-to-all-start.1 = ((bf16[16,6,8,256]{3,2,1,0:T(8,128)(2,1)}), bf16[16,6,8,256]{3,2,1,0:T(8,128)(2,1)S(1)}, u32[]{:S(2)}, u32[]{:S(2)}) async-start(bf16[16,6,8,256]{3,2,1,0:T(8,128)(2,1)} %get-tuple-element.18), calls=%async_computation.1 | async-start | bytes 786432 | tf_op jit(solution)/shard_map/all_to_all | solution.py:177
  37.3 12.0 %collective-permute-start = (bf16[6,8,256]{2,1,0:T(8,128)(2,1)S(1)}, bf16[6,8,256]{2,1,0:T(8,128)(2,1)S(1)}, u32[]{:S(2)}, u32[]{:S(2)}) collective-permute-start(bf16[6,8,256]{2,1,0:T(8,128)(2,1)S(1)} %get-tuple-element.20), channel_id=1, source_target_pairs={{0,416},{1,384},{2,128},{3,352},{4,160},{5,448},{6,192},{7,480},{8... | collective-permute-start | bytes 73736 | tf_op jit(solution)/shard_map/ppermute | solution.py:230
  50.1 16.6 %all-to-all-start.2 = ((bf16[16,6,8,256]{3,2,1,0:T(8,128)(2,1)}), bf16[16,6,8,256]{3,2,1,0:T(8,128)(2,1)S(1)}, u32[]{:S(2)}, u32[]{:S(2)}) async-start(bf16[16,6,8,256]{3,2,1,0:T(8,128)(2,1)} %broadcast_in_dim.2), calls=%async_computation.2 | async-start | bytes 786432 | tf_op jit(solution)/shard_map/all_to_all | solution.py:174
  62.0 4.7 %copy-start.1 = (s32[256]{0:T(256)S(1)}, s32[256]{0:T(256)}, u32[]{:S(2)}) copy-start(s32[256]{0:T(256)} %constant.31.clone.chip_ref) | copy-start | bytes 3076
  69.5 7.1 %copy-start.2 = (f32[512,512]{1,0:T(8,128)S(1)}, f32[512,512]{1,0:T(8,128)}, u32[]{:S(2)}) copy-start(f32[512,512]{1,0:T(8,128)} %refs_2_.1) | copy-start | bytes 3145732
  69.5 24.3 %all-to-all-start.3 = ((bf16[16,80,256]{2,1,0:T(8,128)(2,1)}), bf16[16,80,256]{2,1,0:T(8,128)(2,1)S(1)}, u32[]{:S(2)}, u32[]{:S(2)}) async-start(bf16[16,80,256]{2,1,0:T(8,128)(2,1)} %shard_map.71), calls=%async_computation.3 | async-start | bytes 1310720 | tf_op jit(solution)/shard_map/all_to_all | solution.py:177
  94.5 16.7 %all-to-all-start.4 = ((bf16[16,32,256]{2,1,0:T(8,128)(2,1)}), bf16[16,32,256]{2,1,0:T(8,128)(2,1)S(1)}, u32[]{:S(2)}, u32[]{:S(2)}) async-start(bf16[16,32,256]{2,1,0:T(8,128)(2,1)} %get-tuple-element.23), calls=%async_computation.4 | async-start | bytes 524288 | tf_op jit(solution)/shard_map/all_to_all | solution.py:174

commit v14 on v9

--- a/solution.py
+++ b/solution.py
@@ -82,7 +82,7 @@
                 out_ref[2 * panel + k, :, half:] = jnp.full((height, TAG), number, F32).astype(BF16)
 
 
-def place_kernel(taken_ref, out_ref):
+def place_kernel(taken_ref, out_ref, copies_ref):
     width = taken_ref.shape[2] - TAG
     sources = range(taken_ref.shape[0])
     for lanes in range(0, width, TAG):
@@ -92,7 +92,10 @@
             value = taken_ref[s, :, lanes : lanes + TAG].astype(F32)
             totals = [t + jnp.where(tag == n + 1, value, 0.0) for n, t in enumerate(totals)]
         for n, total in enumerate(totals):
-            out_ref[n, :, lanes : lanes + TAG] = total.astype(BF16)
+            rows = total.astype(BF16)
+            out_ref[n, :, lanes : lanes + TAG] = rows
+            for copy in range(copies_ref.shape[0]):
+                copies_ref[copy, n, :, lanes : lanes + TAG] = rows
 
 
 def product_kernel(chip_ref, *refs):
@@ -188,11 +191,14 @@
     taken, core, *tiles = lax.optimization_barrier(
         (lax.all_to_all(by_panel, "row", 0, 0, tiled=True), core, *tiles)
     )
-    piece = pl.pallas_call(
+    piece, copies = pl.pallas_call(
         place_kernel,
-        out_shape=jax.ShapeDtypeStruct((panel_blocks, chunk_rows, half), BF16),
+        out_shape=(
+            jax.ShapeDtypeStruct((panel_blocks, chunk_rows, half), BF16),
+            jax.ShapeDtypeStruct((col_count, panel_blocks, chunk_rows, half), BF16),
+        ),
         in_specs=[VMEM],
-        out_specs=VMEM,
+        out_specs=(VMEM, VMEM),
         compiler_params=PARAMS,
     )(taken)
 
@@ -202,9 +208,9 @@
         for k in range(2)
         for c in range(col_count)
     ]
-    piece, tile = lax.optimization_barrier((piece, tile))
+    piece, copies, tile = lax.optimization_barrier((piece, copies, tile))
     turned = lax.ppermute(piece, ("row", "col"), route)
-    factor = over_col(jnp.broadcast_to(piece[None], (col_count, *piece.shape)))
+    factor = over_col(copies)
     factor, last_tile = lax.optimization_barrier(
         (factor, pair_gather(tile[tile_rows - block_rows :]))
     )

time: 119 us -> 119 us (level)
  no operation moved by 1% of the time
where the time goes in v14:
time: 119 us; the launch traced here: 118 us
  starting transfers between devices  45.6 us (38%)
  waiting for transfers between devices  34.8 us (29%)
  blocking collectives  23.5 us (20%)
  Pallas kernels  7.69 us (6%)
  local copies, waits for them, and re-layouts  3.98 us (3%)
  other arithmetic  1.32 us (1%)
    all_gather x6, blocking collectives, pair_gather(): return lax.all_gather(x, 'row', axis=0, axis_index_groups=core_pairs)  23.5 us
    all_to_all x2, starting transfers between devices, over_col(): return lax.all_to_all(x, 'col', 0, 0, tiled=True)  16.8 us
    all_to_all x2, waiting for transfers between devices, over_col(): return lax.all_to_all(x, 'col', 0, 0, tiled=True)  16.4 us
    all_to_all x2, starting transfers between devices, over_row(): lax.all_to_all(x, 'row', 0, 0, tiled=True, axis_index_groups=same_core)  13.2 us
    all_to_all x1, starting transfers between devices, body(): lax.all_to_all(by_panel, 'row', 0, 0, tiled=True)  11.2 us
    ppermute x1, waiting for transfers between devices, body(): turned = lax.ppermute(piece, ('row', 'col'), route)  7.54 us
    all_to_all x1, waiting for transfers between devices, body(): lax.all_to_all(by_panel, 'row', 0, 0, tiled=True)  6.89 us
    ppermute x1, starting transfers between devices, body(): turned = lax.ppermute(piece, ('row', 'col'), route)  4.48 us
  transfers between devices with their start and end apart: 6, of which 4 were waited for; matrix products, arithmetic and copies ran while one was open for 4% of the time, Pallas kernels for 0%

profile of v14, /device:TPU:1, one launch (start us, length us, event | category | flops | bytes accessed | tf_op | source)
XLA Modules:
  0.0 118.5 jit_solution(9138454627891175001)
XLA Ops:
  0.6 2.6 %shard_map.68 = bf16[32,8,384]{2,1,0:T(8,128)(2,1)} custom-call(s32[16]{0:T(128)} %refs_0_.1, bf16[128,512]{1,0:T(8,128)(2,1)} %bitcast.26, f32[512,512]{1,0:T(8,128)} %refs_2_.1), custom_call_target="tpu_custom_call" | custom-call | tf_op jit(solution)/shard_map/pallas_call | solution.py:174
  3.3 11.2 %all-to-all-start = ((bf16[32,8,384]{2,1,0:T(8,128)(2,1)}), bf16[32,8,384]{2,1,0:T(8,128)(2,1)S(1)}, u32[]{:S(2)}, u32[]{:S(2)}) async-start(bf16[32,8,384]{2,1,0:T(8,128)(2,1)} %shard_map.68), calls=%async_computation | async-start | bytes 393216 | tf_op jit(solution)/shard_map/all_to_all | solution.py:192
  14.5 2.4 %all-gather = f32[256,768]{1,0:T(8,128)S(1)} all-gather(f32[128,768]{1,0:T(8,128)S(1)} %get-tuple-element.33), channel_id=2, replica_groups={{0,16},{32,48},{64,80},{96,112},{128,144},{160,176},{192,208},{224,240}..., dimensions={0}, use_global_device_ids=true | all-gather | bytes 1179648 | tf_op jit(solution)/shard_map/all_gather | solution.py:155
  16.9 2.4 %all-gather.1 = f32[256,768]{1,0:T(8,128)S(1)} all-gather(f32[128,768]{1,0:T(8,128)S(1)} %get-tuple-element.32), channel_id=3, replica_groups={{0,16},{32,48},{64,80},{96,112},{128,144},{160,176},{192,208},{224,240}..., dimensions={0}, use_global_device_ids=true | all-gather | bytes 1179648 | tf_op jit(solution)/shard_map/all_gather | solution.py:155
  19.2 6.9 %all-to-all-done.taken_ref = bf16[32,8,384]{2,1,0:T(8,128)(2,1)S(1)} async-done(((bf16[32,8,384]{2,1,0:T(8,128)(2,1)}), bf16[32,8,384]{2,1,0:T(8,128)(2,1)S(1)}, u32[]{:S(2)}, u32[]{:S(2)}) %all-to-all-start) | async-done | bytes 196640 | tf_op jit(solution)/shard_map/all_to_all | solution.py:192
  26.1 1.0 shard_map.69
  27.1 10.2 %all-to-all-start.1 = ((bf16[16,6,8,256]{3,2,1,0:T(8,128)(2,1)}), bf16[16,6,8,256]{3,2,1,0:T(8,128)(2,1)S(1)}, u32[]{:S(2)}, u32[]{:S(2)}) async-start(bf16[16,6,8,256]{3,2,1,0:T(8,128)(2,1)} %get-tuple-element.25), calls=%async_computation.1 | async-start | bytes 786432 | tf_op jit(solution)/shard_map/all_to_all | solution.py:161
  37.3 4.5 %collective-permute-start = (bf16[6,8,256]{2,1,0:T(8,128)(2,1)S(1)}, bf16[6,8,256]{2,1,0:T(8,128)(2,1)S(1)}, u32[]{:S(2)}, u32[]{:S(2)}) collective-permute-start(bf16[6,8,256]{2,1,0:T(8,128)(2,1)S(1)} %get-tuple-element.28), channel_id=1, source_target_pairs={{0,416},{1,384},{2,128},{3,352},{4,160},{5,448},{6,192},{7,480},{8... | collective-permute-start | bytes 73736 | tf_op jit(solution)/shard_map/ppermute | solution.py:212
  41.8 7.5 %collective-permute-done = bf16[6,8,256]{2,1,0:T(8,128)(2,1)S(1)} collective-permute-done((bf16[6,8,256]{2,1,0:T(8,128)(2,1)S(1)}, bf16[6,8,256]{2,1,0:T(8,128)(2,1)S(1)}, u32[]{:S(2)}, u32[]{:S(2)}) %collective-permute-start) | collective-permute-done | bytes 24608 | tf_op jit(solution)/shard_map/ppermute | solution.py:212
  49.3 0.8 broadcast_in_dim.2
  50.1 5.7 %all-to-all-start.2 = ((bf16[16,6,8,256]{3,2,1,0:T(8,128)(2,1)}), bf16[16,6,8,256]{3,2,1,0:T(8,128)(2,1)S(1)}, u32[]{:S(2)}, u32[]{:S(2)}) async-start(bf16[16,6,8,256]{3,2,1,0:T(8,128)(2,1)} %broadcast_in_dim.2), calls=%async_computation.2 | async-start | bytes 786432 | tf_op jit(solution)/shard_map/all_to_all | solution.py:158
  56.5 5.8 %all-gather.2 = f32[256,768]{1,0:T(8,128)S(1)} all-gather(f32[128,768]{1,0:T(8,128)S(1)} %slice-done), channel_id=4, replica_groups={{0,16},{32,48},{64,80},{96,112},{128,144},{160,176},{192,208},{224,240}..., dimensions={0}, use_global_device_ids=true | all-gather | bytes 1179648 | tf_op jit(solution)/shard_map/all_gather | solution.py:155
  62.3 2.4 %all-gather.3 = bf16[32,6,8,256]{3,2,1,0:T(8,128)(2,1)S(1)} all-gather(bf16[16,6,8,256]{3,2,1,0:T(8,128)(2,1)S(1)} %all-to-all-done.1), channel_id=5, replica_groups={{0,16},{32,48},{64,80},{96,112},{128,144},{160,176},{192,208},{224,240}..., dimensions={0}, use_global_device_ids=true | all-gather | bytes 1179648 | tf_op jit(solution)/shard_map/all_gather | solution.py:155
  64.7 1.1 copy.10
  65.9 1.2 copy.11.refs_4_
  67.1 3.4 %shard_map.70 = bf16[16,80,256]{2,1,0:T(8,128)(2,1)} custom-call(s32[16]{0:T(128)S(1)} %dynamic-slice_bitcast_fusion.chip_ref, f32[2,128,768]{2,1,0:T(8,128)S(1)} %bitcast.19, f32[2,128,768]{2,1,0:T(8,128)S(1)} %bitcast.20, f32[2,128,768]{2,1,0:T(8,128)S(1)} %bitcast.21, bf16[16,6,8,256]{3,2,1,0:T(8,128)(2,1)S(1)} %all-to-all-done.2.refs_3_, ...), custom_call_target="tpu_custom_call" | custom-call | tf_op jit(solution)/shard_map/pallas_call | solution.py:223
  70.5 6.7 %all-to-all-start.3 = ((bf16[16,80,256]{2,1,0:T(8,128)(2,1)}), bf16[16,80,256]{2,1,0:T(8,128)(2,1)S(1)}, u32[]{:S(2)}, u32[]{:S(2)}) async-start(bf16[16,80,256]{2,1,0:T(8,128)(2,1)} %shard_map.70), calls=%async_computation.3 | async-start | bytes 1310720 | tf_op jit(solution)/shard_map/all_to_all | solution.py:161
  77.2 0.7 fusion
  77.9 16.4 %all-to-all-done.3.arrived_ref = bf16[16,80,256]{2,1,0:T(8,128)(2,1)S(1)} async-done(((bf16[16,80,256]{2,1,0:T(8,128)(2,1)}), bf16[16,80,256]{2,1,0:T(8,128)(2,1)S(1)}, u32[]{:S(2)}, u32[]{:S(2)}) %all-to-all-start.3) | async-done | bytes 655392 | tf_op jit(solution)/shard_map/all_to_all | solution.py:161
  94.4 0.7 shard_map.71
  95.1 7.5 %all-to-all-start.4 = ((bf16[16,32,256]{2,1,0:T(8,128)(2,1)}), bf16[16,32,256]{2,1,0:T(8,128)(2,1)S(1)}, u32[]{:S(2)}, u32[]{:S(2)}) async-start(bf16[16,32,256]{2,1,0:T(8,128)(2,1)} %get-tuple-element.31), calls=%async_computation.4 | async-start | bytes 524288 | tf_op jit(solution)/shard_map/all_to_all | solution.py:158
  102.6 4.7 %all-gather.4 = f32[96,256]{1,0:T(8,128)S(1)} all-gather(f32[48,256]{1,0:T(8,128)S(1)} %get-tuple-element.30), channel_id=6, replica_groups={{0,16},{32,48},{64,80},{96,112},{128,144},{160,176},{192,208},{224,240}..., dimensions={0}, use_global_device_ids=true | all-gather | bytes 147456 | tf_op jit(solution)/shard_map/all_gather | solution.py:155
  107.9 3.9 %all-to-all-done.4 = bf16[16,32,256]{2,1,0:T(8,128)(2,1)S(1)} async-done(((bf16[16,32,256]{2,1,0:T(8,128)(2,1)}), bf16[16,32,256]{2,1,0:T(8,128)(2,1)S(1)}, u32[]{:S(2)}, u32[]{:S(2)}) %all-to-all-start.4) | async-done | bytes 262176 | tf_op jit(solution)/shard_map/all_to_all | solution.py:158
  111.9 5.9 %all-gather.5 = f32[64,256]{1,0:T(8,128)S(1)} all-gather(f32[32,256]{1,0:T(8,128)S(1)} %convert_reduce_fusion), channel_id=7, replica_groups={{0,16},{32,48},{64,80},{96,112},{128,144},{160,176},{192,208},{224,240}..., dimensions={0}, use_global_device_ids=true | all-gather | bytes 98304 | tf_op jit(solution)/shard_map/all_gather | solution.py:155
  (17 shorter events, 2.3 us)
Async XLA Ops:
  0.6 13.8 %copy-start.1 = (f32[384,768]{1,0:T(8,128)S(1)}, f32[384,768]{1,0:T(8,128)}, u32[]{:S(2)}) copy-start(f32[384,768]{1,0:T(8,128)} %param.8) | copy-start | bytes 3538948
  3.3 22.9 %all-to-all-start = ((bf16[32,8,384]{2,1,0:T(8,128)(2,1)}), bf16[32,8,384]{2,1,0:T(8,128)(2,1)S(1)}, u32[]{:S(2)}, u32[]{:S(2)}) async-start(bf16[32,8,384]{2,1,0:T(8,128)(2,1)} %shard_map.68), calls=%async_computation | async-start | bytes 393216 | tf_op jit(solution)/shard_map/all_to_all | solution.py:192
  27.1 22.2 %all-to-all-start.1 = ((bf16[16,6,8,256]{3,2,1,0:T(8,128)(2,1)}), bf16[16,6,8,256]{3,2,1,0:T(8,128)(2,1)S(1)}, u32[]{:S(2)}, u32[]{:S(2)}) async-start(bf16[16,6,8,256]{3,2,1,0:T(8,128)(2,1)} %get-tuple-element.25), calls=%async_computation.1 | async-start | bytes 786432 | tf_op jit(solution)/shard_map/all_to_all | solution.py:161
  37.3 19.2 %slice-start = ((f32[384,768]{1,0:T(8,128)}), f32[128,768]{1,0:T(8,128)S(1)}, s32[]{:S(2)}) async-start(f32[384,768]{1,0:T(8,128)} %param.8), calls=%async_computation.5 | async-start | bytes 786432 | tf_op jit(solution)/shard_map/slice | solution.py:215
  37.3 12.0 %collective-permute-start = (bf16[6,8,256]{2,1,0:T(8,128)(2,1)S(1)}, bf16[6,8,256]{2,1,0:T(8,128)(2,1)S(1)}, u32[]{:S(2)}, u32[]{:S(2)}) collective-permute-start(bf16[6,8,256]{2,1,0:T(8,128)(2,1)S(1)} %get-tuple-element.28), channel_id=1, source_target_pairs={{0,416},{1,384},{2,128},{3,352},{4,160},{5,448},{6,192},{7,480},{8... | collective-permute-start | bytes 73736 | tf_op jit(solution)/shard_map/ppermute | solution.py:212
  50.1 17.0 %all-to-all-start.2 = ((bf16[16,6,8,256]{3,2,1,0:T(8,128)(2,1)}), bf16[16,6,8,256]{3,2,1,0:T(8,128)(2,1)S(1)}, u32[]{:S(2)}, u32[]{:S(2)}) async-start(bf16[16,6,8,256]{3,2,1,0:T(8,128)(2,1)} %broadcast_in_dim.2), calls=%async_computation.2 | async-start | bytes 786432 | tf_op jit(solution)/shard_map/all_to_all | solution.py:158
  70.5 6.7 %copy-start = (f32[512,512]{1,0:T(8,128)S(1)}, f32[512,512]{1,0:T(8,128)}, u32[]{:S(2)}) copy-start(f32[512,512]{1,0:T(8,128)} %refs_2_.1) | copy-start | bytes 3145732
  70.5 23.9 %all-to-all-start.3 = ((bf16[16,80,256]{2,1,0:T(8,128)(2,1)}), bf16[16,80,256]{2,1,0:T(8,128)(2,1)S(1)}, u32[]{:S(2)}, u32[]{:S(2)}) async-start(bf16[16,80,256]{2,1,0:T(8,128)(2,1)} %shard_map.70), calls=%async_computation.3 | async-start | bytes 1310720 | tf_op jit(solution)/shard_map/all_to_all | solution.py:161
  95.1 16.7 %all-to-all-start.4 = ((bf16[16,32,256]{2,1,0:T(8,128)(2,1)}), bf16[16,32,256]{2,1,0:T(8,128)(2,1)S(1)}, u32[]{:S(2)}, u32[]{:S(2)}) async-start(bf16[16,32,256]{2,1,0:T(8,128)(2,1)} %get-tuple-element.31), calls=%async_computation.4 | async-start | bytes 524288 | tf_op jit(solution)/shard_map/all_to_all | solution.py:158

commit v15 on v9

--- a/solution.py
+++ b/solution.py
@@ -95,7 +95,17 @@
             out_ref[n, :, lanes : lanes + TAG] = total.astype(BF16)
 
 
-def product_kernel(chip_ref, *refs):
+def turn_kernel(halves_ref, out_ref, rows_ref):
+    _, chunks, blocks, height, half = halves_ref.shape
+    for k in range(2):
+        for c in range(chunks):
+            for b in range(blocks):
+                first = (b * chunks + c) * height
+                rows_ref[first : first + height, :] = halves_ref[k, c, b].astype(F32)
+        out_ref[k * half : (k + 1) * half, :] = rows_ref[...].T.astype(BF16)
+
+
+def product_kernel(col_ref, chip_ref, *refs):
     *tile_refs, parts_ref, factor_ref, out_ref, panel_ref, high_ref, low_ref, sent_ref = refs
     chunks, blocks, height, half = parts_ref.shape
     for b, ref in enumerate(tile_refs):
@@ -106,7 +116,7 @@
     for c in range(chunks):
         for b in range(blocks):
             first = (b * chunks + c) * height
-            panel_ref[first : first + height, :] = parts_ref[chip_ref[c], b].astype(F32)
+            panel_ref[first : first + height, :] = parts_ref[chip_ref[col_ref[0] * chunks + c], b].astype(F32)
     panel = panel_ref[...].astype(BF16)
     sums = dot(high_ref[...], panel) + dot(low_ref[...], panel)
     gram = dot(factor_ref[...], sums.astype(BF16))
@@ -146,7 +156,8 @@
     same_core = [[2 * j + k for j in range(chip_count)] for k in range(2)]
     core_pairs = [[2 * j, 2 * j + 1] for j in range(chip_count)]
     table = short_routes(chip_count, col_count)
-    chip_arg = lax.dynamic_index_in_dim(jnp.asarray(table), col_index, 0, keepdims=False)
+    chip_arg = jnp.asarray(table.reshape(-1))
+    col_arg = jnp.reshape(col_index, (1,)).astype(jnp.int32)
 
     def pair_gather(x):
         return lax.all_gather(x, "row", axis=0, axis_index_groups=core_pairs)
@@ -209,15 +220,21 @@
         (factor, pair_gather(tile[tile_rows - block_rows :]))
     )
     tiles.append(last_tile)
-    tile_factor = pair_gather(factor)
-    tile_factor = tile_factor.transpose(0, 4, 2, 1, 3).reshape(width, 2 * tile_rows)
+    tile_factor = pl.pallas_call(
+        turn_kernel,
+        out_shape=jax.ShapeDtypeStruct((width, 2 * tile_rows), BF16),
+        in_specs=[VMEM],
+        out_specs=VMEM,
+        scratch_shapes=[pltpu.VMEM((2 * tile_rows, half), F32)],
+        compiler_params=PARAMS,
+    )(pair_gather(factor))
     parts = over_row(jnp.broadcast_to(turned[None], (chip_count, *turned.shape)))
 
     sent = (col_count, diag_width + 2 * share, half)
     sent = pl.pallas_call(
         product_kernel,
         out_shape=jax.ShapeDtypeStruct(sent, BF16),
-        in_specs=[SMEM] + [VMEM] * (len(tiles) + 2),
+        in_specs=[SMEM, SMEM] + [VMEM] * (len(tiles) + 2),
         out_specs=VMEM,
         scratch_shapes=[
             pltpu.VMEM((panel_rows, half), F32),
@@ -226,7 +243,7 @@
             pltpu.VMEM(sent, F32),
         ],
         compiler_params=pltpu.CompilerParams(vmem_limit_bytes=50 * 2**20),
-    )(chip_arg, *tiles, parts, tile_factor)
+    )(col_arg, chip_arg, *tiles, parts, tile_factor)
     totals, copies = pl.pallas_call(
         total_kernel,
         out_shape=(

time: 119 us -> 119 us (level)
  local copies, waits for them, and re-layouts: 4.78 us -> 2.57 us
  waiting for transfers between devices: 34.8 us -> 36 us
  transfers between devices with their start and end apart: 6 -> 6, of which waited for: 4 -> 5; matrix products, arithmetic and copies ran while one was open for 4% -> 1% of each run, Pallas kernels for 0% -> 0%
where the time goes in v15:
time: 119 us; the launch traced here: 118 us
  starting transfers between devices  46.2 us (39%)
  waiting for transfers between devices  36 us (30%)
  blocking collectives  23.7 us (20%)
  Pallas kernels  7.14 us (6%)
  local copies, waits for them, and re-layouts  2.57 us (2%)
  other arithmetic  1.32 us (1%)
    all_gather x6, blocking collectives, pair_gather(): return lax.all_gather(x, 'row', axis=0, axis_index_groups=core_pairs)  23.7 us
    all_to_all x2, starting transfers between devices, over_col(): return lax.all_to_all(x, 'col', 0, 0, tiled=True)  17.2 us
    all_to_all x2, waiting for transfers between devices, over_col(): return lax.all_to_all(x, 'col', 0, 0, tiled=True)  16.4 us
    all_to_all x2, starting transfers between devices, over_row(): lax.all_to_all(x, 'row', 0, 0, tiled=True, axis_index_groups=same_core)  13.3 us
    all_to_all x1, starting transfers between devices, body(): lax.all_to_all(by_panel, 'row', 0, 0, tiled=True)  11.2 us
    ppermute x1, waiting for transfers between devices, body(): turned = lax.ppermute(piece, ('row', 'col'), route)  7.68 us
    all_to_all x1, waiting for transfers between devices, body(): lax.all_to_all(by_panel, 'row', 0, 0, tiled=True)  6.89 us
    all_to_all x2, waiting for transfers between devices, over_row(): lax.all_to_all(x, 'row', 0, 0, tiled=True, axis_index_groups=same_core)  5.03 us
  transfers between devices with their start and end apart: 6, of which 5 were waited for; matrix products, arithmetic and copies ran while one was open for 1% of the time, Pallas kernels for 0%

profile of v15, /device:TPU:1, one launch (start us, length us, event | category | flops | bytes accessed | tf_op | source)
XLA Modules:
  0.0 118.5 jit_solution(14613296787739405669)
XLA Ops:
  0.6 2.6 %shard_map.68 = bf16[32,8,384]{2,1,0:T(8,128)(2,1)} custom-call(s32[16]{0:T(128)} %refs_0_.1, bf16[128,512]{1,0:T(8,128)(2,1)} %bitcast.17, f32[512,512]{1,0:T(8,128)} %refs_2_.1), custom_call_target="tpu_custom_call" | custom-call | tf_op jit(solution)/shard_map/pallas_call | solution.py:182
  3.2 11.2 %all-to-all-start = ((bf16[32,8,384]{2,1,0:T(8,128)(2,1)}), bf16[32,8,384]{2,1,0:T(8,128)(2,1)S(1)}, u32[]{:S(2)}, u32[]{:S(2)}) async-start(bf16[32,8,384]{2,1,0:T(8,128)(2,1)} %shard_map.68), calls=%async_computation | async-start | bytes 393216 | tf_op jit(solution)/shard_map/all_to_all | solution.py:200
  14.5 2.4 %all-gather = f32[256,768]{1,0:T(8,128)S(1)} all-gather(f32[128,768]{1,0:T(8,128)S(1)} %get-tuple-element.27), channel_id=2, replica_groups={{0,16},{32,48},{64,80},{96,112},{128,144},{160,176},{192,208},{224,240}..., dimensions={0}, use_global_device_ids=true | all-gather | bytes 1179648 | tf_op jit(solution)/shard_map/all_gather | solution.py:163
  16.9 2.4 %all-gather.1 = f32[256,768]{1,0:T(8,128)S(1)} all-gather(f32[128,768]{1,0:T(8,128)S(1)} %get-tuple-element.26), channel_id=3, replica_groups={{0,16},{32,48},{64,80},{96,112},{128,144},{160,176},{192,208},{224,240}..., dimensions={0}, use_global_device_ids=true | all-gather | bytes 1179648 | tf_op jit(solution)/shard_map/all_gather | solution.py:163
  19.3 6.9 %all-to-all-done.taken_ref = bf16[32,8,384]{2,1,0:T(8,128)(2,1)S(1)} async-done(((bf16[32,8,384]{2,1,0:T(8,128)(2,1)}), bf16[32,8,384]{2,1,0:T(8,128)(2,1)S(1)}, u32[]{:S(2)}, u32[]{:S(2)}) %all-to-all-start) | async-done | bytes 196640 | tf_op jit(solution)/shard_map/all_to_all | solution.py:200
  26.3 0.8 broadcast_in_dim.4
  27.1 10.2 %all-to-all-start.1 = ((bf16[16,6,8,256]{3,2,1,0:T(8,128)(2,1)}), bf16[16,6,8,256]{3,2,1,0:T(8,128)(2,1)S(1)}, u32[]{:S(2)}, u32[]{:S(2)}) async-start(bf16[16,6,8,256]{3,2,1,0:T(8,128)(2,1)} %broadcast_in_dim.4), calls=%async_computation.1 | async-start | bytes 786432 | tf_op jit(solution)/shard_map/all_to_all | solution.py:169
  37.3 4.3 %collective-permute-start = (bf16[6,8,256]{2,1,0:T(8,128)(2,1)S(1)}, bf16[6,8,256]{2,1,0:T(8,128)(2,1)S(1)}, u32[]{:S(2)}, u32[]{:S(2)}) collective-permute-start(bf16[6,8,256]{2,1,0:T(8,128)(2,1)S(1)} %shard_map.69), channel_id=1, source_target_pairs={{0,416},{1,384},{2,128},{3,352},{4,160},{5,448},{6,192},{7,480},{8... | collective-permute-start | bytes 73736 | tf_op jit(solution)/shard_map/ppermute | solution.py:217
  41.7 7.7 %collective-permute-done = bf16[6,8,256]{2,1,0:T(8,128)(2,1)S(1)} collective-permute-done((bf16[6,8,256]{2,1,0:T(8,128)(2,1)S(1)}, bf16[6,8,256]{2,1,0:T(8,128)(2,1)S(1)}, u32[]{:S(2)}, u32[]{:S(2)}) %collective-permute-start) | collective-permute-done | bytes 24608 | tf_op jit(solution)/shard_map/ppermute | solution.py:217
  49.3 0.8 broadcast_in_dim.5
  50.1 5.9 %all-to-all-start.2 = ((bf16[16,6,8,256]{3,2,1,0:T(8,128)(2,1)}), bf16[16,6,8,256]{3,2,1,0:T(8,128)(2,1)S(1)}, u32[]{:S(2)}, u32[]{:S(2)}) async-start(bf16[16,6,8,256]{3,2,1,0:T(8,128)(2,1)} %broadcast_in_dim.5), calls=%async_computation.2 | async-start | bytes 786432 | tf_op jit(solution)/shard_map/all_to_all | solution.py:166
  56.1 5.9 %all-gather.2 = f32[256,768]{1,0:T(8,128)S(1)} all-gather(f32[128,768]{1,0:T(8,128)S(1)} %slice.31), channel_id=4, replica_groups={{0,16},{32,48},{64,80},{96,112},{128,144},{160,176},{192,208},{224,240}..., dimensions={0}, use_global_device_ids=true | all-gather | bytes 1179648 | tf_op jit(solution)/shard_map/all_gather | solution.py:163
  62.0 2.5 %all-gather.3 = bf16[32,6,8,256]{3,2,1,0:T(8,128)(2,1)S(1)} all-gather(bf16[16,6,8,256]{3,2,1,0:T(8,128)(2,1)S(1)} %all-to-all-done.1), channel_id=5, replica_groups={{0,16},{32,48},{64,80},{96,112},{128,144},{160,176},{192,208},{224,240}..., dimensions={0}, use_global_device_ids=true | all-gather | bytes 1179648 | tf_op jit(solution)/shard_map/all_gather | solution.py:163
  64.8 0.9 copy-done
  65.7 1.1 all-to-all-done.2.refs_3_
  66.8 3.4 %shard_map.71 = bf16[16,80,256]{2,1,0:T(8,128)(2,1)} custom-call(s32[1]{0:T(128)} %bitcast.3.col_ref, s32[256]{0:T(256)S(1)} %copy-done.1, f32[2,128,768]{2,1,0:T(8,128)S(1)} %bitcast.12, f32[2,128,768]{2,1,0:T(8,128)S(1)} %bitcast.13, f32[2,128,768]{2,1,0:T(8,128)S(1)} %bitcast.14, bf16[16,6,8,256]{3,2,1,0:T(8,128)(2,1)S(1)} %all-to-all-done.2.refs_3_, ...), custom_call_target="tpu_custom_call" | custom-call | tf_op jit(solution)/shard_map/pallas_call | solution.py:234
  70.1 7.1 %all-to-all-start.3 = ((bf16[16,80,256]{2,1,0:T(8,128)(2,1)}), bf16[16,80,256]{2,1,0:T(8,128)(2,1)S(1)}, u32[]{:S(2)}, u32[]{:S(2)}) async-start(bf16[16,80,256]{2,1,0:T(8,128)(2,1)} %shard_map.71), calls=%async_computation.3 | async-start | bytes 1310720 | tf_op jit(solution)/shard_map/all_to_all | solution.py:169
  77.2 0.7 fusion
  78.0 16.4 %all-to-all-done.3.arrived_ref = bf16[16,80,256]{2,1,0:T(8,128)(2,1)S(1)} async-done(((bf16[16,80,256]{2,1,0:T(8,128)(2,1)}), bf16[16,80,256]{2,1,0:T(8,128)(2,1)S(1)}, u32[]{:S(2)}, u32[]{:S(2)}) %all-to-all-start.3) | async-done | bytes 655392 | tf_op jit(solution)/shard_map/all_to_all | solution.py:169
  94.4 0.7 shard_map.72
  95.2 7.4 %all-to-all-start.4 = ((bf16[16,32,256]{2,1,0:T(8,128)(2,1)}), bf16[16,32,256]{2,1,0:T(8,128)(2,1)S(1)}, u32[]{:S(2)}, u32[]{:S(2)}) async-start(bf16[16,32,256]{2,1,0:T(8,128)(2,1)} %get-tuple-element.25), calls=%async_computation.4 | async-start | bytes 524288 | tf_op jit(solution)/shard_map/all_to_all | solution.py:166
  102.6 4.7 %all-gather.4 = f32[96,256]{1,0:T(8,128)S(1)} all-gather(f32[48,256]{1,0:T(8,128)S(1)} %get-tuple-element.24), channel_id=6, replica_groups={{0,16},{32,48},{64,80},{96,112},{128,144},{160,176},{192,208},{224,240}..., dimensions={0}, use_global_device_ids=true | all-gather | bytes 147456 | tf_op jit(solution)/shard_map/all_gather | solution.py:163
  107.9 3.9 %all-to-all-done.4 = bf16[16,32,256]{2,1,0:T(8,128)(2,1)S(1)} async-done(((bf16[16,32,256]{2,1,0:T(8,128)(2,1)}), bf16[16,32,256]{2,1,0:T(8,128)(2,1)S(1)}, u32[]{:S(2)}, u32[]{:S(2)}) %all-to-all-start.4) | async-done | bytes 262176 | tf_op jit(solution)/shard_map/all_to_all | solution.py:166
  111.9 5.9 %all-gather.5 = f32[64,256]{1,0:T(8,128)S(1)} all-gather(f32[32,256]{1,0:T(8,128)S(1)} %convert_reduce_fusion), channel_id=7, replica_groups={{0,16},{32,48},{64,80},{96,112},{128,144},{160,176},{192,208},{224,240}..., dimensions={0}, use_global_device_ids=true | all-gather | bytes 98304 | tf_op jit(solution)/shard_map/all_gather | solution.py:163
  (18 shorter events, 1.9 us)
Async XLA Ops:
  0.6 13.8 %copy-start.3 = (f32[384,768]{1,0:T(8,128)S(1)}, f32[384,768]{1,0:T(8,128)}, u32[]{:S(2)}) copy-start(f32[384,768]{1,0:T(8,128)} %param.8) | copy-start | bytes 3538948
  3.2 22.9 %all-to-all-start = ((bf16[32,8,384]{2,1,0:T(8,128)(2,1)}), bf16[32,8,384]{2,1,0:T(8,128)(2,1)S(1)}, u32[]{:S(2)}, u32[]{:S(2)}) async-start(bf16[32,8,384]{2,1,0:T(8,128)(2,1)} %shard_map.68), calls=%async_computation | async-start | bytes 393216 | tf_op jit(solution)/shard_map/all_to_all | solution.py:200
  27.1 22.2 %all-to-all-start.1 = ((bf16[16,6,8,256]{3,2,1,0:T(8,128)(2,1)}), bf16[16,6,8,256]{3,2,1,0:T(8,128)(2,1)S(1)}, u32[]{:S(2)}, u32[]{:S(2)}) async-start(bf16[16,6,8,256]{3,2,1,0:T(8,128)(2,1)} %broadcast_in_dim.4), calls=%async_computation.1 | async-start | bytes 786432 | tf_op jit(solution)/shard_map/all_to_all | solution.py:169
  37.3 12.0 %collective-permute-start = (bf16[6,8,256]{2,1,0:T(8,128)(2,1)S(1)}, bf16[6,8,256]{2,1,0:T(8,128)(2,1)S(1)}, u32[]{:S(2)}, u32[]{:S(2)}) collective-permute-start(bf16[6,8,256]{2,1,0:T(8,128)(2,1)S(1)} %shard_map.69), channel_id=1, source_target_pairs={{0,416},{1,384},{2,128},{3,352},{4,160},{5,448},{6,192},{7,480},{8... | collective-permute-start | bytes 73736 | tf_op jit(solution)/shard_map/ppermute | solution.py:217
  50.1 16.6 %all-to-all-start.2 = ((bf16[16,6,8,256]{3,2,1,0:T(8,128)(2,1)}), bf16[16,6,8,256]{3,2,1,0:T(8,128)(2,1)S(1)}, u32[]{:S(2)}, u32[]{:S(2)}) async-start(bf16[16,6,8,256]{3,2,1,0:T(8,128)(2,1)} %broadcast_in_dim.5), calls=%async_computation.2 | async-start | bytes 786432 | tf_op jit(solution)/shard_map/all_to_all | solution.py:166
  62.0 4.8 %copy-start.1 = (s32[256]{0:T(256)S(1)}, s32[256]{0:T(256)}, u32[]{:S(2)}) copy-start(s32[256]{0:T(256)} %constant.31.clone.chip_ref) | copy-start | bytes 3076
  64.8 0.9 copy-start
  70.1 7.1 %copy-start.2 = (f32[512,512]{1,0:T(8,128)S(1)}, f32[512,512]{1,0:T(8,128)}, u32[]{:S(2)}) copy-start(f32[512,512]{1,0:T(8,128)} %refs_2_.1) | copy-start | bytes 3145732
  70.1 24.3 %all-to-all-start.3 = ((bf16[16,80,256]{2,1,0:T(8,128)(2,1)}), bf16[16,80,256]{2,1,0:T(8,128)(2,1)S(1)}, u32[]{:S(2)}, u32[]{:S(2)}) async-start(bf16[16,80,256]{2,1,0:T(8,128)(2,1)} %shard_map.71), calls=%async_computation.3 | async-start | bytes 1310720 | tf_op jit(solution)/shard_map/all_to_all | solution.py:169
  95.2 16.7 %all-to-all-start.4 = ((bf16[16,32,256]{2,1,0:T(8,128)(2,1)}), bf16[16,32,256]{2,1,0:T(8,128)(2,1)S(1)}, u32[]{:S(2)}, u32[]{:S(2)}) async-start(bf16[16,32,256]{2,1,0:T(8,128)(2,1)} %get-tuple-element.25), calls=%async_computation.4 | async-start | bytes 524288 | tf_op jit(solution)/shard_map/all_to_all | solution.py:166
